TPU v7x, 32 devices: a whole 2x2x4 slice. The times are simulated.
32 devices in a mesh: parts: 2 (over x), dp: 2 (over core), tensor: 8 (over z, y).
Axes of the slice: x: 2, y: 2, z: 4, core: 2. Of those that a mesh axis runs over, the one named last changes fastest.
Arguments:
- queries: bfloat16 [256, 64, 128], P(('parts', 'dp'), 'tensor'), parts along dimension 0, may hold values from -600 to 600
- cached_key_rows: bfloat16 [256, 8, 768, 128], P(('parts', 'dp'), None, 'tensor'), parts along dimension 0, may hold values from -6 to 6
- cached_value_rows: bfloat16 [256, 8, 768, 128], P(('parts', 'dp'), None, 'tensor'), parts along dimension 0, may hold values from -6 to 6
- cache_live_length: int32 [256], P(('parts', 'dp')), parts along dimension 0, may hold values from 2 to 768
- adapter_index: int32 [256], P(('parts', 'dp')), parts along dimension 0, may hold values from 0 to 15
- adapter_slot_index: int32 [16], replicated, may hold values from 0 to 15, each once
- output_weight: bfloat16 [8192, 8192], P('tensor'), may hold values from -0.0625 to 0.0625
- adapter_down_weight: bfloat16 [16, 8192, 64], P('dp', 'tensor'), may hold values from -0.0625 to 0.0625
- adapter_up_weight: bfloat16 [16, 64, 8192], P('dp', None, 'tensor'), may hold values from -0.75 to 0.75
Outputs:
- mixed: bfloat16 [256, 8192], P(('parts', 'dp'), 'tensor'), parts along dimension 0
There are 2 independent parts, one for each index of `parts`. A program takes and returns all parts, laid end to end along the dimension named above; an argument that names none is the same for every part. Nothing has to cross between parts.
All inputs are finite; a program needn't handle non-finite values.
Results may differ from a plain program's by a relative error of at most 0.0061.
Values may be sent and summed in bfloat16 or wider, within the bound.
No kernel may reach another device: no remote copies, remote signals or barrier semaphores. Data moves between devices by JAX's collectives and lax.ppermute only.
A program may use at most 128 MiB of HBM per device.

v0:
```python
import math

import jax
import jax.numpy as jnp
from jax import lax
from jax.sharding import PartitionSpec as P


def on_device(
    queries,
    cached_key_rows,
    cached_value_rows,
    cache_live_length,
    adapter_index,
    adapter_slot_index,
    output_weight,
    adapter_down_weight,
    adapter_up_weight,
):
    rows = queries.shape[0]
    head_size = queries.shape[2]
    kv_heads = cached_key_rows.shape[1]
    positions = cached_key_rows.shape[2]
    all_queries = lax.all_gather(queries, "tensor", axis=1, tiled=True)
    group = all_queries.shape[1] // kv_heads
    grouped = all_queries.reshape(rows, kv_heads, group, head_size)
    scores = jnp.einsum(
        "rsgd,rsld->rsgl", grouped, cached_key_rows, preferred_element_type=jnp.float32
    ) * (1.0 / math.sqrt(head_size))
    first_pos = lax.axis_index("tensor") * positions
    live = first_pos + jnp.arange(positions, dtype=jnp.int32)[None, :] < cache_live_length[:, None]
    live = live[:, None, None, :]
    scores = jnp.where(live, scores, -1e30)
    local_top = jnp.max(scores, axis=-1)
    top = lax.pmax(local_top, "tensor")
    expo = jnp.where(live, jnp.exp(scores - top[..., None]), 0.0)
    total = lax.psum(jnp.sum(expo, axis=-1), "tensor")
    weights = (expo / total[..., None]).astype(jnp.bfloat16)
    partial_vals = jnp.einsum(
        "rsgl,rsld->rsgd", weights, cached_value_rows, preferred_element_type=jnp.float32
    )
    partial_vals = partial_vals.reshape(rows, -1)
    attention_output = lax.psum_scatter(
        partial_vals, "tensor", scatter_dimension=1, tiled=True
    ).astype(jnp.bfloat16)
    base_term = jnp.dot(attention_output, output_weight, preferred_element_type=jnp.float32)
    total_slots = adapter_slot_index.shape[0]
    id_match = adapter_index[:, None] == jnp.arange(total_slots, dtype=jnp.int32)[None, :]
    slot = jnp.sum(jnp.where(id_match, adapter_slot_index[None, :], 0), axis=1)
    down_all, gathered_up_weight = (
        lax.all_gather(adapter_down_weight, "dp", axis=0, tiled=True),
        lax.all_gather(adapter_up_weight, "dp", axis=0, tiled=True),
    )
    onehot = slot[:, None] == jnp.arange(total_slots, dtype=jnp.int32)[None, :]
    gathered_partials = jnp.einsum(
        "xl,dlo->xdo", attention_output, down_all, preferred_element_type=jnp.float32
    )
    shrink_part = jnp.sum(jnp.where(onehot[:, :, None], gathered_partials, 0.0), axis=1)
    shrink = lax.psum(shrink_part, "tensor").astype(jnp.bfloat16)
    expanded_heads = jnp.where(onehot[:, :, None], shrink[:, None, :], jnp.zeros((), jnp.bfloat16))
    adapter_contribution = jnp.einsum(
        "tbz,bzy->ty", expanded_heads, gathered_up_weight, preferred_element_type=jnp.float32
    )
    base_output = lax.psum_scatter(base_term, "tensor", scatter_dimension=1, tiled=True)
    return (base_output + adapter_contribution).astype(jnp.bfloat16)


def solution(mesh):
    placed = (
        P(("parts", "dp"), "tensor", None),
        P(("parts", "dp"), None, "tensor", None),
        P(("parts", "dp"), None, "tensor", None),
        P(("parts", "dp")),
        P(("parts", "dp")),
        P(),
        P("tensor", None),
        P("dp", "tensor", None),
        P("dp", None, "tensor"),
    )
    return jax.shard_map(
        on_device,
        mesh=mesh,
        in_specs=placed,
        out_specs=P(("parts", "dp"), "tensor"),
        check_vma=False,
    )
```

profile of v0, /device:TPU:0, one launch (start us, length us, event | category | flops | bytes accessed | tf_op | source)
XLA Modules:
  0.0 301.7 jit_solution(2795142223684239754)
XLA Ops:
  7.4 0.7 all-gather.4.cloned.1.call-update
  8.1 0.0 reduce-scatter.3.cloned.1.call-start
  8.2 0.7 broadcast_compare_fusion
  8.9 43.6 %all-gather.4.cloned.1.call-done = bf16[64,64,128]{2,1,0:T(8,128)(2,1)} async-done(((bf16[64,8,128]{2,1,0:T(8,128)(2,1)}), bf16[64,64,128]{2,1,0:T(8,128)(2,1)}) %all-gather.4.cloned.1.call-update) | async-done | bytes 1048592 | tf_op jit(solution)/shard_map/all_gather | solution.py:24
  52.5 9.9 %fusion = (f32[64,8,8]{2,1,0:T(8,128)S(1)}, f32[64,8,8,96]{3,2,1,0:T(8,128)S(1)}) fusion(pred[64,96]{1,0:T(8,128)(4,1)S(1)} %broadcast_compare_fusion, bf16[64,8,96,128]{3,2,1,0:T(8,128)(2,1)} %param.10, bf16[64,64,128]{2,1,0:T(8,128)(2,1)} %all-gather.4.cloned.1.call-done), kind=kOutput, calls=%fused_computation.4 | convolution fusion | flops 101838848 | bytes 15226880 | tf_op jit(solution)/shard_map/rsgd,rsld->rsgl/dot_general | solution.py:27
  62.4 38.4 %pmax.7 = f32[64,8,8]{2,1,0:T(8,128)S(1)} all-reduce(f32[64,8,8]{2,1,0:T(8,128)S(1)} %get-tuple-element.5), channel_id=1, replica_groups=mesh['parts'=2,'dp'=2,'tensor'=8] {'tensor'}, use_global_device_ids=true, to_apply=%region_1.2 | all-reduce | flops 4096 | bytes 32768 | tf_op jit(solution)/shard_map/pmax | solution.py:35
  100.8 1.3 fusion.1
  102.1 35.9 %psum.14 = f32[64,8,8]{2,1,0:T(8,128)S(1)} all-reduce(f32[64,8,8]{2,1,0:T(8,128)S(1)} %fusion.1), channel_id=1, replica_groups=mesh['parts'=2,'dp'=2,'tensor'=8] {'tensor'}, use_global_device_ids=true, to_apply=%region_3.4 | all-reduce | flops 4096 | bytes 32768 | tf_op jit(solution)/shard_map/psum | solution.py:37
  138.1 6.4 %fusion.5 = f32[64,8,8,128]{3,2,1,0:T(8,128)S(1)} fusion(bf16[64,8,96,128]{3,2,1,0:T(8,128)(2,1)} %param.11, f32[64,8,8,96]{3,2,1,0:T(8,128)S(1)} %get-tuple-element.6, f32[64,8,8]{2,1,0:T(8,128)S(1)} %psum.14, f32[64,8,8]{2,1,0:T(8,128)S(1)} %pmax.7, pred[64,96]{1,0:T(8,128)(4,1)S(1)} %broadcast_compare_fusion), kind=kOutput, calls=%fused_computation.11 | convolution fusion | flops 103022592 | bytes 16291840 | tf_op jit(solution)/shard_map/rsgl,rsld->rsgd/dot_general | solution.py:39
  144.5 2.5 copy.12
  147.1 0.0 all-gather.6.cloned.1.call-start
  147.1 0.5 all-gather.6.cloned.1.call-update
  147.6 0.0 all-gather.8.cloned.1.call-start
  147.7 0.5 all-gather.8.cloned.1.call-update
  148.2 0.0 reduce-scatter.5.cloned.1.call-start
  148.3 65.1 %reduce-scatter.3.cloned.1.call-done = f32[64,1024]{1,0:T(8,128)} async-done(((f32[64,8192]{1,0:T(8,128)}), f32[64,1024]{1,0:T(8,128)}) %reduce-scatter.3.cloned.1.call-update) | async-done | bytes 262160 | tf_op jit(solution)/shard_map/reduce_scatter | solution.py:43
  213.4 10.2 %fusion.20 = f32[64,8192]{1,0:T(8,128)} fusion(bf16[1024,8192]{1,0:T(8,128)(2,1)} %param.15, f32[64,1024]{1,0:T(8,128)} %reduce-scatter.3.cloned.1.call-done), kind=kOutput, calls=%fused_computation.26 | convolution fusion | flops 1073807360 | bytes 19136512 | tf_op jit(solution)/shard_map/dot_general | solution.py:46
  223.7 0.6 copy-done.1
  224.3 0.1 select_reduce_fusion
  224.4 0.2 copy-done
  224.6 2.7 fusion.2
  227.3 35.4 %psum.15 = bf16[64,64]{1,0:T(8,128)(2,1)S(1)} all-reduce(f32[64,64]{1,0:T(8,128)S(1)} %fusion.2), channel_id=1, replica_groups=mesh['parts'=2,'dp'=2,'tensor'=8] {'tensor'}, use_global_device_ids=true, to_apply=%region_8.9 | all-reduce | flops 4096 | bytes 24576 | tf_op jit(solution)/shard_map/psum | solution.py:59
  262.7 29.1 %reduce-scatter.5.cloned.1.call-done = f32[64,1024]{1,0:T(8,128)} async-done(((f32[64,8192]{1,0:T(8,128)}), f32[64,1024]{1,0:T(8,128)}) %reduce-scatter.5.cloned.1.call-update) | async-done | bytes 262160 | tf_op jit(solution)/shard_map/reduce_scatter | solution.py:64
  291.8 2.9 fusion.4
  (11 shorter events, 0.1 us)
Async XLA Ops:
  7.4 45.1 %all-gather.4.cloned.1.call-start = ((), (), s32[]{:S(2)}) async-start(), calls=%async_computation.2 | async-start | bytes 1179648 | tf_op jit(solution)/shard_map/all_gather | solution.py:24
  8.1 205.3 %reduce-scatter.3.cloned.1.call-start = ((), (), s32[]{:S(2)}) async-start(), calls=%async_computation.3 | async-start | bytes 2359296 | tf_op jit(solution)/shard_map/reduce_scatter | solution.py:43
  147.1 77.4 %all-gather.6.cloned.1.call-start = ((), (), s32[]{:S(2)}) async-start(), calls=%async_computation.5 | async-start | bytes 3145728 | tf_op jit(solution)/shard_map/all_gather | solution.py:51
  147.6 115.1 %all-gather.8.cloned.1.call-start = ((), (), s32[]{:S(2)}) async-start(), calls=%async_computation.6 | async-start | bytes 3145728 | tf_op jit(solution)/shard_map/all_gather | solution.py:52
  148.2 143.5 %reduce-scatter.5.cloned.1.call-start = ((), (), s32[]{:S(2)}) async-start(), calls=%async_computation.4 | async-start | bytes 2359296 | tf_op jit(solution)/shard_map/reduce_scatter | solution.py:64
  223.6 0.7 copy-start.1
  223.6 0.7 copy-start.2
  223.6 1.0 copy-start
Sparse Core Ops, SparseCore 0:
  10.2 42.2 all-gather.3
  147.2 66.1 reduce-scatter.2
  223.8 67.9 reduce-scatter.4
Sparse Core Ops, SparseCore 1:
  149.1 8.7 all-gather.5
  159.2 11.6 all-gather.7
where the time goes:
time: 302 us
  waiting for transfers between devices  140 us (46%)
  blocking collectives  110 us (36%)
  matrix products  32.1 us (11%)
  between operations  14.6 us (5%)
  local copies, waits for them, and re-layouts  3.37 us (1%)
    reduce_scatter x1, waiting for transfers between devices, on_device(): lax.psum_scatter(partial_vals, 'tensor', scatter_dimension=1, tiled=True)  65.1 us
    all_gather x1, waiting for transfers between devices, on_device(): all_queries = lax.all_gather(queries, 'tensor', axis=1, tiled=True)  43.6 us
    pmax x1, blocking collectives, on_device(): top = lax.pmax(local_top, 'tensor')  38.4 us
    psum x1, blocking collectives, on_device(): total = lax.psum(jnp.sum(expo, axis=-1), 'tensor')  35.9 us
    psum x1, blocking collectives, on_device(): shrink = lax.psum(shrink_part, 'tensor').astype(jnp.bfloat16)  35.4 us
    reduce_scatter x1, waiting for transfers between devices, on_device(): lax.psum_scatter(base_term, 'tensor', scatter_dimension=1, tiled=True)  29.1 us
    dot_general x1, matrix products, on_device(): jnp.dot(attention_output, output_weight, preferred_element_type=jnp.float32)  10.2 us
    dot_general x1, matrix products, on_device(): jnp.einsum('rsgd,rsld->rsgl', grouped, cached_key_rows, preferred_element...  9.85 us
  transfers between devices with their start and end apart: 5, of which 3 were waited for; matrix products, arithmetic and copies ran while one was open for 5% of the time, Pallas kernels for 0%

commit v1 on v0

v1 whole, which is shorter than its diff:
```python
import functools
import math

import jax
import jax.numpy as jnp
from jax import lax
from jax.experimental import pallas as pl
from jax.experimental.pallas import tpu as pltpu
from jax.sharding import PartitionSpec as P

F32, BF16 = jnp.float32, jnp.bfloat16
DEAD = -1e30
LANES = 128
TILE = 16
VMEM_BYTES = 40 * 1024 * 1024


def call(body, grid, in_specs, out_shape, out_specs, scratch=(), prefetch=1, cost=None):
    return pl.pallas_call(
        body,
        grid_spec=pltpu.PrefetchScalarGridSpec(
            num_scalar_prefetch=prefetch,
            grid=grid,
            in_specs=in_specs,
            out_specs=out_specs,
            scratch_shapes=list(scratch),
        ),
        out_shape=out_shape,
        compiler_params=pltpu.CompilerParams(vmem_limit_bytes=VMEM_BYTES),
        cost_estimate=cost,
    )


def whole(shape):
    return pl.BlockSpec(shape, lambda i, *_: (0,) * len(shape))


def split2(x):
    high = x.astype(BF16).astype(F32)
    return high, (x - high).astype(BF16).astype(F32)


def iota(shape, dim):
    return lax.broadcasted_iota(jnp.int32, shape, dim)


def attend_body(steps, heads, scale, sc_ref, q_ref, k_ref, v_ref, o_ref):
    step = pl.program_id(0)
    reqs, positions = k_ref.shape[0], k_ref.shape[2]
    per_tile = TILE // heads
    tiles = reqs // per_tile
    body_rows = steps * tiles * TILE
    row = iota((TILE, LANES), 0) // heads
    lane = iota((TILE, LANES), 1)
    pos = iota((TILE, positions), 1)
    prow = iota((TILE, positions), 0) // heads
    stat = jnp.zeros((TILE, LANES), F32)
    for g in range(tiles):
        q = q_ref[pl.ds(g * TILE, TILE), :]
        zero = jnp.zeros_like(q)
        left = jnp.concatenate([jnp.where(row == a, q, zero) for a in range(per_tile)], axis=1)
        right = jnp.concatenate([k_ref[g * per_tile + a, 0] for a in range(per_tile)], axis=1)
        s = lax.dot_general(left, right, (((1,), (1,)), ((), ())), preferred_element_type=F32) * scale
        first = step * reqs + g * per_tile
        live = jnp.zeros((TILE, positions), jnp.int32)
        for a in range(per_tile):
            live = jnp.where(prow == a, sc_ref[1 + first + a], live)
        alive = pos < live
        s = jnp.where(alive, s, DEAD)
        high, mid = split2(jnp.max(s, axis=1, keepdims=True))
        p = jnp.where(alive, jnp.exp(s - (high + mid)), 0.0)
        lhigh, lmid = split2(jnp.sum(p, axis=1, keepdims=True))
        values = jnp.concatenate([v_ref[g * per_tile + a, 0] for a in range(per_tile)], axis=1)
        wide = jnp.dot(p.astype(BF16), values, preferred_element_type=F32)
        acc = wide[:, :LANES]
        for a in range(1, per_tile):
            acc = jnp.where(row == a, wide[:, a * LANES : (a + 1) * LANES], acc)
        o_ref[pl.ds(pl.multiple_of((step * tiles + g) * TILE, TILE), TILE), :] = acc.astype(BF16)
        at = 4 * (step * tiles + g)
        for n, val in enumerate((high, mid, lhigh, lmid)):
            stat = jnp.where(lane == at + n, val, stat)

    @pl.when(step == 0)
    def _():
        o_ref[pl.ds(body_rows, TILE), :] = stat.astype(BF16)

    @pl.when(step > 0)
    def _():
        o_ref[pl.ds(body_rows, TILE), :] = (o_ref[pl.ds(body_rows, TILE), :].astype(F32) + stat).astype(BF16)


def attend(scalars, q, keys, values, heads, scale):
    rows, _, positions, width = keys.shape
    steps = 4
    block = rows // steps
    kv = pl.BlockSpec((block, 1, positions, width), lambda i, sc: (i, sc[0], 0, 0))
    n = rows * heads + TILE
    return call(
        functools.partial(attend_body, steps, heads, scale),
        (steps,),
        [pl.BlockSpec((block * heads, width), lambda i, sc: (i, 0)), kv, kv],
        jax.ShapeDtypeStruct((n, width), BF16),
        whole((n, width)),
        cost=pl.CostEstimate(
            flops=4 * rows * heads * positions * width * 8,
            bytes_accessed=4 * rows * positions * width,
            transcendentals=rows * heads * positions,
        ),
    )(scalars, q, keys, values)


def combine(stats):
    tops = [s + pltpu.roll(s, LANES - 1, 1) for s in stats]
    sums = [pltpu.roll(t, LANES - 2, 1) for t in tops]
    best = functools.reduce(jnp.maximum, tops)
    weights = [jnp.exp(t - best) for t in tops]
    total = sum(w * l for w, l in zip(weights, sums))
    return best, weights, total


def pair_body(a_ref, b_ref, o_ref):
    n = a_ref.shape[0] - TILE
    sa = a_ref[pl.ds(n, TILE), :].astype(F32)
    sb = b_ref[pl.ds(n, TILE), :].astype(F32)
    lane = iota((TILE, LANES), 1) % 4
    first = lane == 0
    best, (wa, wb), total = combine([sa, sb])
    wa, wb = jnp.where(first, wa, 0.0), jnp.where(first, wb, 0.0)
    high, mid = split2(best)
    lhigh, lmid = split2(total)
    stat = jnp.where(first, high, 0.0)
    stat = jnp.where(lane == 1, pltpu.roll(mid, 1, 1), stat)
    stat = jnp.where(lane == 2, pltpu.roll(lhigh, 2, 1), stat)
    stat = jnp.where(lane == 3, pltpu.roll(lmid, 3, 1), stat)
    o_ref[pl.ds(n, TILE), :] = stat.astype(BF16)
    for g in range(n // TILE):
        at = pl.ds(g * TILE, TILE)
        o_ref[at, :] = (
            wa[:, 4 * g : 4 * g + 1] * a_ref[at, :].astype(F32)
            + wb[:, 4 * g : 4 * g + 1] * b_ref[at, :].astype(F32)
        ).astype(BF16)


def pair(a, b):
    return pl.pallas_call(
        pair_body,
        out_shape=jax.ShapeDtypeStruct(a.shape, BF16),
        compiler_params=pltpu.CompilerParams(vmem_limit_bytes=VMEM_BYTES),
        cost_estimate=pl.CostEstimate(flops=3 * a.size, bytes_accessed=6 * a.size, transcendentals=0),
    )(a, b)


def finish_attention(parts, att32, att_ref, heads):
    n = parts[0].shape[0] - TILE
    stats = [p[pl.ds(n, TILE), :].astype(F32) for p in parts]
    _, weights, total = combine(stats)
    inverse = 1.0 / total
    weights = [w * inverse for w in weights]
    for g in range(n // TILE):
        at = pl.ds(g * TILE, TILE)
        att32[at, :] = sum(
            w[:, 4 * g : 4 * g + 1] * p[at, :].astype(F32) for w, p in zip(weights, parts)
        )
    for h in range(heads):
        att_ref[:, h * LANES : (h + 1) * LANES] = att32[pl.ds(h, n // heads, stride=heads), :].astype(BF16)


def chosen(rel, wide, rank):
    total = None
    lane = iota((wide.shape[0], LANES), 1)
    for b in range(wide.shape[1] // LANES):
        part = jnp.where(rel == (lane + b * LANES) // rank, wide[:, b * LANES : (b + 1) * LANES], 0.0)
        total = part if total is None else total + part
    return total


def project_body(n_parts, n_out, heads, rank, sc_ref, *refs):
    parts = refs[:n_parts]
    w_ref, slot_ref, down_a, down_b = refs[n_parts : n_parts + 4]
    outs = refs[n_parts + 4 : n_parts + 4 + n_out]
    att_ref, shrink_ref, att32 = refs[n_parts + 4 + n_out :]
    step = pl.program_id(0)

    @pl.when(step == 0)
    def _():
        finish_attention(parts, att32, att_ref, heads)
        att = att_ref[...]
        over = (((1,), (1,)), ((), ()))
        own = lax.dot_general(att, down_a[...], over, preferred_element_type=F32)
        other = lax.dot_general(att, down_b[...], over, preferred_element_type=F32)
        slots = slot_ref[...]
        per = down_a.shape[0] // rank
        mine = sc_ref[0]
        s = chosen(slots - mine * per, own, rank) + chosen(slots - (1 - mine) * per, other, rank)
        s = s + pltpu.roll(s, rank, 1)
        high, mid = split2(s)
        shrink_ref[...] = jnp.where(iota(s.shape, 1) < rank, high, mid).astype(BF16)

    for k in range(n_out):

        @pl.when(step == k)
        def _(k=k):
            out = jnp.dot(att_ref[...], w_ref[...], preferred_element_type=F32)
            outs[k][:, : out.shape[1]] = out.astype(BF16)
            outs[k][:, out.shape[1] :] = shrink_ref[...]


def project(scalars, parts, weight, slots, down_a, down_b, heads, rank, cols):
    n_out = scalars.shape[0] - 1
    rows = slots.shape[0]
    width = weight.shape[0]
    msg = jax.ShapeDtypeStruct((rows, cols + LANES), BF16)
    outs = call(
        functools.partial(project_body, len(parts), n_out, heads, rank),
        (n_out,),
        [whole(p.shape) for p in parts]
        + [pl.BlockSpec((width, cols), lambda i, sc: (0, sc[1 + i]))]
        + [whole(slots.shape), whole(down_a.shape), whole(down_b.shape)],
        [msg] * n_out
        + [jax.ShapeDtypeStruct((rows, width), BF16), jax.ShapeDtypeStruct((rows, LANES), BF16)],
        [whole(msg.shape)] * n_out + [whole((rows, width)), whole((rows, LANES))],
        scratch=[pltpu.VMEM((rows * heads, LANES), F32)],
        cost=pl.CostEstimate(
            flops=2 * rows * width * cols * n_out, bytes_accessed=2 * width * cols * n_out, transcendentals=0
        ),
    )(scalars, *parts, weight, slots, down_a, down_b)
    return outs[:n_out], outs[n_out], outs[n_out + 1]


def project_more_body(n_out, sc_ref, att_ref, shrink_ref, w_ref, *outs):
    step = pl.program_id(0)
    for k in range(n_out):

        @pl.when(step == k)
        def _(k=k):
            out = jnp.dot(att_ref[...], w_ref[...], preferred_element_type=F32)
            outs[k][:, : out.shape[1]] = out
            outs[k][:, out.shape[1] :] = shrink_ref[...].astype(F32)


def project_more(scalars, att, shrink, weight, cols):
    n_out = scalars.shape[0] - 1
    rows, width = att.shape
    msg = jax.ShapeDtypeStruct((rows, cols + LANES), F32)
    return call(
        functools.partial(project_more_body, n_out),
        (n_out,),
        [
            whole(att.shape),
            whole(shrink.shape),
            pl.BlockSpec((width, cols), lambda i, sc: (0, sc[1 + i])),
        ],
        [msg] * n_out,
        [whole(msg.shape)] * n_out,
        cost=pl.CostEstimate(
            flops=2 * rows * width * cols * n_out, bytes_accessed=2 * width * cols * n_out, transcendentals=0
        ),
    )(scalars, att, shrink, weight)


def shrink_sum(parts, rank):
    both = sum(parts)
    return both + pltpu.roll(both, rank, 1)


def add_body(rank, a_ref, b_ref, o_ref):
    cols = a_ref.shape[1] - LANES
    o_ref[:, :cols] = (a_ref[:, :cols] + b_ref[:, :cols].astype(F32)).astype(BF16)
    s = shrink_sum([a_ref[:, cols:], b_ref[:, cols:].astype(F32)], rank)
    high, mid = split2(s)
    o_ref[:, cols:] = jnp.where(iota(s.shape, 1) < rank, high, mid).astype(BF16)


def add(a, b, rank):
    return pl.pallas_call(
        functools.partial(add_body, rank),
        out_shape=jax.ShapeDtypeStruct(a.shape, BF16),
        compiler_params=pltpu.CompilerParams(vmem_limit_bytes=VMEM_BYTES),
        cost_estimate=pl.CostEstimate(flops=a.size, bytes_accessed=8 * a.size, transcendentals=0),
    )(a, b)


def expanded(rel, shrink, rank, width):
    lane = iota((rel.shape[0], LANES), 1)
    zero = jnp.zeros(rel.shape, F32)
    return jnp.concatenate(
        [
            jnp.where(rel == (lane + b * LANES) // rank, shrink, zero).astype(BF16)
            for b in range(width // LANES)
        ],
        axis=1,
    )


def last_body(rank, n_parts, mine_ref, slot_ref, up_a, up_b, *refs):
    parts, o_ref = refs[:n_parts], refs[n_parts]
    cols = o_ref.shape[1]
    base = sum(p[:, :cols].astype(F32) for p in parts)
    shrink = shrink_sum([p[:, cols:].astype(F32) for p in parts], rank).astype(BF16).astype(F32)
    slots = slot_ref[...]
    mine = mine_ref[0]
    per = up_a.shape[0] // rank
    xa = expanded(slots - mine * per, shrink, rank, up_a.shape[0])
    xb = expanded(slots - (1 - mine) * per, shrink, rank, up_b.shape[0])
    lora = jnp.dot(xa, up_a[...], preferred_element_type=F32) + jnp.dot(
        xb, up_b[...], preferred_element_type=F32
    )
    o_ref[...] = (base + lora).astype(BF16)


def last(mine, slots, up_a, up_b, parts, rank):
    rows, cols = slots.shape[0], up_a.shape[1]
    return call(
        functools.partial(last_body, rank, len(parts)),
        (1,),
        [whole(slots.shape), whole(up_a.shape), whole(up_b.shape)] + [whole(p.shape) for p in parts],
        jax.ShapeDtypeStruct((rows, cols), BF16),
        whole((rows, cols)),
        cost=pl.CostEstimate(flops=4 * rows * up_a.size // rows, bytes_accessed=4 * up_a.size, transcendentals=0),
    )(mine, slots, up_a, up_b, *parts)


def on_device(
    tensor,
    queries,
    cached_key_rows,
    cached_value_rows,
    cache_live_length,
    adapter_index,
    adapter_slot_index,
    output_weight,
    adapter_down_weight,
    adapter_up_weight,
):
    rows, heads, width = queries.shape
    kv_heads, positions = cached_key_rows.shape[1:3]
    group = heads * tensor // kv_heads
    slots_here, _, rank = adapter_down_weight.shape
    cols = adapter_up_weight.shape[2]
    me = lax.axis_index("tensor")
    mine = lax.axis_index("dp")

    def hop(x, k):
        return lax.ppermute(x, "tensor", [(i, i ^ k) for i in range(tensor)])

    def across(x):
        return lax.ppermute(x, "dp", [(0, 1), (1, 0)])

    far = sorted(range(2, tensor, 2), key=lambda k: -min(k, 4))
    outer = far + [0]

    q = queries.reshape(rows * heads, width)
    held = {0: q}
    held[1] = hop(q, 1)
    for k in far:
        held[k] = hop(q, k)
    for k in far:
        held[k ^ 1] = hop(held[k], 1)

    down_a = jnp.swapaxes(adapter_down_weight, 1, 2).reshape(slots_here * rank, -1)
    up_a = adapter_up_weight.reshape(slots_here * rank, cols)
    down_b, up_b = across(down_a), across(up_a)

    live = jnp.clip(cache_live_length - me * positions, 0, positions)
    scale = 1.0 / math.sqrt(width)

    def attended(k):
        head = ((me ^ k) * heads) // group
        scalars = jnp.concatenate([head[None], live]).astype(jnp.int32)
        return attend(scalars, held[k], cached_key_rows, cached_value_rows, heads, scale)

    sent = {k: hop(attended(k ^ 1), 1) for k in [0] + far}
    merged = {k: pair(attended(k), sent[k]) for k in [0] + far}
    parts = [merged[0]] + [hop(merged[k], k) for k in far]

    total_slots = adapter_slot_index.shape[0]
    match = adapter_index[:, None] == jnp.arange(total_slots, dtype=jnp.int32)[None, :]
    slot = jnp.sum(jnp.where(match, adapter_slot_index[None, :], 0), axis=1)
    slots = jnp.broadcast_to(slot[:, None], (rows, LANES)).astype(jnp.int32)

    order = jnp.array([k for k in outer], jnp.int32)
    to_pair = jnp.concatenate([mine[None], me ^ order ^ 1]).astype(jnp.int32)
    to_own = jnp.concatenate([mine[None], me ^ order]).astype(jnp.int32)
    first, att, shrink = project(
        to_pair, parts, output_weight, slots, down_a, down_b, heads, rank, cols
    )
    arrived = [hop(x, 1) for x in first]
    own = project_more(to_own, att, shrink, output_weight, cols)
    summed = [add(a, b, rank) for a, b in zip(own, arrived)]
    final = [hop(x, k) if k else x for x, k in zip(summed, outer)]
    return last(mine[None].astype(jnp.int32), slots, up_a, up_b, final, rank)


def solution(mesh):
    placed = (
        P(("parts", "dp"), "tensor", None),
        P(("parts", "dp"), None, "tensor", None),
        P(("parts", "dp"), None, "tensor", None),
        P(("parts", "dp")),
        P(("parts", "dp")),
        P(),
        P("tensor", None),
        P("dp", "tensor", None),
        P("dp", None, "tensor"),
    )
    return jax.shard_map(
        functools.partial(on_device, mesh.shape["tensor"]),
        mesh=mesh,
        in_specs=placed,
        out_specs=P(("parts", "dp"), "tensor"),
        check_vma=False,
    )
```

time: 302 us -> 150 us (0.50)
  waiting for transfers between devices: 140 us -> 13 us
  blocking collectives: 110 us -> 0 us
  Pallas kernels: 0 us -> 92.1 us
  matrix products: 32.1 us -> 0 us
  starting transfers between devices: 0.17 us -> 29.6 us
  between operations: 14.6 us -> 0.29 us
  local copies, waits for them, and re-layouts: 3.37 us -> 13.8 us
    reduce_scatter x2 -> x0, waiting for transfers between devices: 94.2 us -> none  [the longest x1 65.1 us: on_device(): lax.psum_scatter(partial_vals, 'tensor', scatter_dimension=1, tiled=True)]
    pallas_call x0 -> x19, Pallas kernels: none -> 92.1 us  [the longest x8 76.9 us: attend(): call(functools.partial(attend_body, steps, heads, scale), (steps,), [pl.B...]
    psum x2 -> x0, blocking collectives: 71.3 us -> none  [the longest x1 35.9 us: on_device(): total = lax.psum(jnp.sum(expo, axis=-1), 'tensor')]
    all_gather x3 -> x0, waiting for transfers between devices: 43.6 us -> none  [the longest x1 43.6 us: on_device(): all_queries = lax.all_gather(queries, 'tensor', axis=1, tiled=True)]
    pmax x1 -> x0, blocking collectives: 38.4 us -> none  [on_device(): top = lax.pmax(local_top, 'tensor')]
    dot_general x5 -> x0, matrix products: 32.1 us -> none  [the longest x1 10.2 us: on_device(): jnp.dot(attention_output, output_weight, preferred_element_type=jnp.float32)]
    ppermute x0 -> x23, starting transfers between devices: none -> 29.6 us  [the longest x21 29.6 us: hop(): return lax.ppermute(x, 'tensor', [(i, i ^ k) for i in range(tensor)])]
    ppermute x0 -> x23, waiting for transfers between devices: none -> 13 us  [the longest x21 13 us: hop(): return lax.ppermute(x, 'tensor', [(i, i ^ k) for i in range(tensor)])]
  transfers between devices with their start and end apart: 5 -> 23, of which waited for: 3 -> 4; matrix products, arithmetic and copies ran while one was open for 5% -> 1% of each run, Pallas kernels for 0% -> 61%
where the time goes in v1:
time: 150 us
  Pallas kernels  92.1 us (61%)
  starting transfers between devices  29.6 us (20%)
  local copies, waits for them, and re-layouts  13.8 us (9%)
  waiting for transfers between devices  13 us (9%)
    pallas_call x8, Pallas kernels, attend(): call(functools.partial(attend_body, steps, heads, scale), (steps,), [pl.B...  76.9 us
    ppermute x21, starting transfers between devices, hop(): return lax.ppermute(x, 'tensor', [(i, i ^ k) for i in range(tensor)])  29.6 us
    unnamed x18, local copies, waits for them, and re-layouts  13.7 us
    ppermute x21, waiting for transfers between devices, hop(): return lax.ppermute(x, 'tensor', [(i, i ^ k) for i in range(tensor)])  13 us
    pallas_call x1, Pallas kernels, project(): call(functools.partial(project_body, len(parts), n_out, heads, rank), (n_...  6.68 us
    pallas_call x1, Pallas kernels, project_more(): call(functools.partial(project_more_body, n_out), (n_out,), [whole(att.sh...  5.52 us
  transfers between devices with their start and end apart: 23, of which 4 were waited for; matrix products, arithmetic and copies ran while one was open for 1% of the time, Pallas kernels for 61%

profile of v1, /device:TPU:0, one launch (start us, length us, event | category | flops | bytes accessed | tf_op | source)
XLA Modules:
  0.0 149.9 jit_solution(1453598062702344747)
XLA Ops:
  0.0 4.0 %collective-permute-start.3 = (bf16[512,128]{1,0:T(8,128)(2,1)}, bf16[512,128]{1,0:T(8,128)(2,1)S(1)}, u32[]{:S(2)}, u32[]{:S(2)}) collective-permute-start(bf16[512,128]{1,0:T(8,128)(2,1)} %bitcast.18), channel_id=1, source_target_pairs={{0,4},{1,5},{2,6},{3,7},{4,0},{5,1},{6,2},{7,3},{8,12},{9,13},{10,... | collective-permute-start | bytes 393224 | tf_op jit(solution)/shard_map/ppermute | solution.py:344
  7.4 4.8 %collective-permute-done.3.q_ref = bf16[512,128]{1,0:T(8,128)(2,1)S(1)} collective-permute-done((bf16[512,128]{1,0:T(8,128)(2,1)}, bf16[512,128]{1,0:T(8,128)(2,1)S(1)}, u32[]{:S(2)}, u32[]{:S(2)}) %collective-permute-start.3) | collective-permute-done | bytes 131104 | tf_op jit(solution)/shard_map/ppermute | solution.py:344
  12.2 2.2 %collective-permute-start.4 = (bf16[512,128]{1,0:T(8,128)(2,1)S(1)}, bf16[512,128]{1,0:T(8,128)(2,1)S(1)}, u32[]{:S(2)}, u32[]{:S(2)}) collective-permute-start(bf16[512,128]{1,0:T(8,128)(2,1)S(1)} %collective-permute-done.3.q_ref), channel_id=1, source_target_pairs={{0,1},{1,0},{2,3},{3,2},{4,5},{5,4},{6,7},{7,6},{8,9},{9,8},{10,11... | collective-permute-start | bytes 393224 | tf_op jit(solution)/shard_map/ppermute | solution.py:344
  17.7 2.5 %collective-permute-start.8 = (bf16[512,128]{1,0:T(8,128)(2,1)S(1)}, bf16[512,128]{1,0:T(8,128)(2,1)S(1)}, u32[]{:S(2)}, u32[]{:S(2)}) collective-permute-start(bf16[512,128]{1,0:T(8,128)(2,1)S(1)} %collective-permute-done.7.q_ref), channel_id=1, source_target_pairs={{0,1},{1,0},{2,3},{3,2},{4,5},{5,4},{6,7},{7,6},{8,9},{9,8},{10,11... | collective-permute-start | bytes 393224 | tf_op jit(solution)/shard_map/ppermute | solution.py:344
  20.2 4.6 %copy-done = bf16[64,8,96,128]{3,2,1,0:T(8,128)(2,1)S(1)} copy-done((bf16[64,8,96,128]{3,2,1,0:T(8,128)(2,1)S(1)}, bf16[64,8,96,128]{3,2,1,0:T(8,128)(2,1)}, u32[]{:S(2)}) %copy-start) | copy-done | bytes 12582936
  24.8 9.6 %shard_map.104 = bf16[528,128]{1,0:T(8,128)(2,1)S(1)} custom-call(s32[65]{0:T(128)S(1)} %get-tuple-element.28.sc_ref, bf16[512,128]{1,0:T(8,128)(2,1)S(1)} %collective-permute-done.4.q_ref, bf16[64,8,96,128]{3,2,1,0:T(8,128)(2,1)S(1)} %copy-done, bf16[64,8,96,128]{3,2,1,0:T(8,128)(2,1)} %v_ref.15), custom_call_target="tpu_custom_call" | custom-call | flops 201326592 | bytes 3145728 | tf_op jit(solution)/shard_map/pallas_call | solution.py:98
  34.6 4.6 %copy-done.1 = bf16[64,8,96,128]{3,2,1,0:T(8,128)(2,1)S(1)} copy-done((bf16[64,8,96,128]{3,2,1,0:T(8,128)(2,1)S(1)}, bf16[64,8,96,128]{3,2,1,0:T(8,128)(2,1)}, u32[]{:S(2)}) %copy-start.1) | copy-done | bytes 12582936
  39.1 9.6 %shard_map.101 = bf16[528,128]{1,0:T(8,128)(2,1)S(1)} custom-call(s32[65]{0:T(128)S(1)} %get-tuple-element.26.sc_ref, bf16[512,128]{1,0:T(8,128)(2,1)S(1)} %collective-permute-done.1.q_ref, bf16[64,8,96,128]{3,2,1,0:T(8,128)(2,1)S(1)} %copy-done.1, bf16[64,8,96,128]{3,2,1,0:T(8,128)(2,1)} %v_ref.15), custom_call_target="tpu_custom_call" | custom-call | flops 201326592 | bytes 3145728 | tf_op jit(solution)/shard_map/pallas_call | solution.py:98
  48.8 2.0 %collective-permute-start.2 = (bf16[528,128]{1,0:T(8,128)(2,1)S(1)}, bf16[528,128]{1,0:T(8,128)(2,1)S(1)}, u32[]{:S(2)}, u32[]{:S(2)}) collective-permute-start(bf16[528,128]{1,0:T(8,128)(2,1)S(1)} %shard_map.101), channel_id=1, source_target_pairs={{0,1},{1,0},{2,3},{3,2},{4,5},{5,4},{6,7},{7,6},{8,9},{9,8},{10,11... | collective-permute-start | bytes 405512 | tf_op jit(solution)/shard_map/ppermute | solution.py:344
  50.8 9.6 %shard_map.107 = bf16[528,128]{1,0:T(8,128)(2,1)S(1)} custom-call(s32[65]{0:T(128)S(1)} %get-tuple-element.30.sc_ref, bf16[512,128]{1,0:T(8,128)(2,1)S(1)} %collective-permute-done.8.q_ref, bf16[64,8,96,128]{3,2,1,0:T(8,128)(2,1)S(1)} %copy-done.1, bf16[64,8,96,128]{3,2,1,0:T(8,128)(2,1)} %v_ref.15), custom_call_target="tpu_custom_call" | custom-call | flops 201326592 | bytes 3145728 | tf_op jit(solution)/shard_map/pallas_call | solution.py:98
  60.5 9.6 %shard_map.110 = bf16[528,128]{1,0:T(8,128)(2,1)S(1)} custom-call(s32[65]{0:T(128)S(1)} %get-tuple-element.25.sc_ref, bf16[512,128]{1,0:T(8,128)(2,1)S(1)} %collective-permute-done.12.q_ref, bf16[64,8,96,128]{3,2,1,0:T(8,128)(2,1)S(1)} %copy-done.1, bf16[64,8,96,128]{3,2,1,0:T(8,128)(2,1)} %v_ref.15), custom_call_target="tpu_custom_call" | custom-call | flops 201326592 | bytes 3145728 | tf_op jit(solution)/shard_map/pallas_call | solution.py:98
  70.1 2.0 %collective-permute-start.13 = (bf16[528,128]{1,0:T(8,128)(2,1)S(1)}, bf16[528,128]{1,0:T(8,128)(2,1)S(1)}, u32[]{:S(2)}, u32[]{:S(2)}) collective-permute-start(bf16[528,128]{1,0:T(8,128)(2,1)S(1)} %shard_map.110), channel_id=1, source_target_pairs={{0,1},{1,0},{2,3},{3,2},{4,5},{5,4},{6,7},{7,6},{8,9},{9,8},{10,11... | collective-permute-start | bytes 405512 | tf_op jit(solution)/shard_map/ppermute | solution.py:344
  72.2 9.6 %shard_map.109.a_ref = bf16[528,128]{1,0:T(8,128)(2,1)S(1)} custom-call(s32[65]{0:T(128)S(1)} %get-tuple-element.31.sc_ref, bf16[512,128]{1,0:T(8,128)(2,1)S(1)} %collective-permute-done.11.q_ref, bf16[64,8,96,128]{3,2,1,0:T(8,128)(2,1)S(1)} %copy-done.1, bf16[64,8,96,128]{3,2,1,0:T(8,128)(2,1)} %v_ref.15), custom_call_target="tpu_custom_call" | custom-call | flops 201326592 | bytes 3145728 | tf_op jit(solution)/shard_map/pallas_call | solution.py:98
  81.8 9.6 %shard_map.103.a_ref = bf16[528,128]{1,0:T(8,128)(2,1)S(1)} custom-call(s32[65]{0:T(128)S(1)} %get-tuple-element.27.sc_ref, bf16[512,128]{1,0:T(8,128)(2,1)S(1)} %collective-permute-done.3.q_ref, bf16[64,8,96,128]{3,2,1,0:T(8,128)(2,1)S(1)} %copy-done.1, bf16[64,8,96,128]{3,2,1,0:T(8,128)(2,1)} %v_ref.15), custom_call_target="tpu_custom_call" | custom-call | flops 201326592 | bytes 3145728 | tf_op jit(solution)/shard_map/pallas_call | solution.py:98
  91.5 9.6 %shard_map.106.a_ref = bf16[528,128]{1,0:T(8,128)(2,1)S(1)} custom-call(s32[65]{0:T(128)S(1)} %get-tuple-element.29.sc_ref, bf16[512,128]{1,0:T(8,128)(2,1)S(1)} %collective-permute-done.7.q_ref, bf16[64,8,96,128]{3,2,1,0:T(8,128)(2,1)S(1)} %copy-done.1, bf16[64,8,96,128]{3,2,1,0:T(8,128)(2,1)} %v_ref.15), custom_call_target="tpu_custom_call" | custom-call | flops 201326592 | bytes 3145728 | tf_op jit(solution)/shard_map/pallas_call | solution.py:98
  102.5 2.2 %collective-permute-start.10 = (bf16[528,128]{1,0:T(8,128)(2,1)S(1)}, bf16[528,128]{1,0:T(8,128)(2,1)S(1)}, u32[]{:S(2)}, u32[]{:S(2)}) collective-permute-start(bf16[528,128]{1,0:T(8,128)(2,1)S(1)} %shard_map.108), channel_id=1, source_target_pairs={{0,6},{1,7},{2,4},{3,5},{4,2},{5,3},{6,0},{7,1},{8,14},{9,15},{10,... | collective-permute-start | bytes 405512 | tf_op jit(solution)/shard_map/ppermute | solution.py:344
  105.9 4.6 %copy-done.2 = bf16[64,8,96,128]{3,2,1,0:T(8,128)(2,1)S(1)} copy-done((bf16[64,8,96,128]{3,2,1,0:T(8,128)(2,1)S(1)}, bf16[64,8,96,128]{3,2,1,0:T(8,128)(2,1)}, u32[]{:S(2)}) %copy-start.2) | copy-done | bytes 12582936
  110.5 9.6 %shard_map.100.a_ref = bf16[528,128]{1,0:T(8,128)(2,1)S(1)} custom-call(s32[65]{0:T(128)S(1)} %get-tuple-element.32.sc_ref, bf16[512,128]{1,0:T(8,128)(2,1)S(1)} %bitcast.22, bf16[64,8,96,128]{3,2,1,0:T(8,128)(2,1)S(1)} %copy-done.2, bf16[64,8,96,128]{3,2,1,0:T(8,128)(2,1)} %v_ref.15), custom_call_target="tpu_custom_call" | custom-call | flops 201326592 | bytes 3145728 | tf_op jit(solution)/shard_map/pallas_call | solution.py:98
  120.7 6.7 %shard_map.112 = (bf16[64,1152]{1,0:T(8,128)(2,1)S(1)}, bf16[64,1152]{1,0:T(8,128)(2,1)S(1)}, bf16[64,1152]{1,0:T(8,128)(2,1)S(1)}, bf16[64,1152]{1,0:T(8,128)(2...) custom-call(s32[5]{0:T(128)S(1)} %pad_add_fusion.1.sc_ref, bf16[528,128]{1,0:T(8,128)(2,1)S(1)} %shard_map.102.refs_0_, ...), custom_call_target="tpu_custom_call" | custom-call | flops 536870912 | bytes 8388608 | tf_op jit(solution)/shard_map/pallas_call | solution.py:213
  127.5 2.0 %collective-permute-start.18 = (bf16[64,1152]{1,0:T(8,128)(2,1)S(1)}, bf16[64,1152]{1,0:T(8,128)(2,1)S(1)}, u32[]{:S(2)}, u32[]{:S(2)}) collective-permute-start(bf16[64,1152]{1,0:T(8,128)(2,1)S(1)} %get-tuple-element.20), channel_id=1, source_target_pairs={{0,1},{1,0},{2,3},{3,2},{4,5},{5,4},{6,7},{7,6},{8,9},{9,8},{10,11... | collective-permute-start | bytes 442376 | tf_op jit(solution)/shard_map/ppermute | solution.py:344
  131.6 5.5 %shard_map.113 = (f32[64,1152]{1,0:T(8,128)S(1)}, f32[64,1152]{1,0:T(8,128)S(1)}, f32[64,1152]{1,0:T(8,128)S(1)}, f32[64,1152]{1,0:T(8,128)S(1)}) custom-call(s32[5]{0:T(128)S(1)} %pad_add_fusion.sc_ref, bf16[64,1024]{1,0:T(8,128)(2,1)S(1)} %get-tuple-element.15.att_ref, bf16[64,128]{1,0:T(8,128)(2,1)S(1)} %get-tuple-element.16.shrink_ref, ...), custom_call_target="tpu_custom_call" | custom-call | flops 536870912 | bytes 8388608 | tf_op jit(solution)/shard_map/pallas_call | solution.py:245
  137.2 2.8 %collective-permute-start.19 = (bf16[64,1152]{1,0:T(8,128)(2,1)S(1)}, bf16[64,1152]{1,0:T(8,128)(2,1)S(1)}, u32[]{:S(2)}, u32[]{:S(2)}) collective-permute-start(bf16[64,1152]{1,0:T(8,128)(2,1)S(1)} %shard_map.115), channel_id=1, source_target_pairs={{0,6},{1,7},{2,4},{3,5},{4,2},{5,3},{6,0},{7,1},{8,14},{9,15},{10,... | collective-permute-start | bytes 442376 | tf_op jit(solution)/shard_map/ppermute | solution.py:344
  142.2 2.2 %collective-permute-done.19.refs_1_ = bf16[64,1152]{1,0:T(8,128)(2,1)S(1)} collective-permute-done((bf16[64,1152]{1,0:T(8,128)(2,1)S(1)}, bf16[64,1152]{1,0:T(8,128)(2,1)S(1)}, u32[]{:S(2)}, u32[]{:S(2)}) %collective-permute-start.19) | collective-permute-done | bytes 147488 | tf_op jit(solution)/shard_map/ppermute | solution.py:344
  144.4 4.3 %collective-permute-done.17.refs_0_ = bf16[64,1152]{1,0:T(8,128)(2,1)S(1)} collective-permute-done((bf16[64,1152]{1,0:T(8,128)(2,1)S(1)}, bf16[64,1152]{1,0:T(8,128)(2,1)S(1)}, u32[]{:S(2)}, u32[]{:S(2)}) %collective-permute-start.17) | collective-permute-done | bytes 147488 | tf_op jit(solution)/shard_map/ppermute | solution.py:344
  (67 shorter events, 15.8 us)
Async XLA Ops:
  0.0 12.2 %collective-permute-start.3 = (bf16[512,128]{1,0:T(8,128)(2,1)}, bf16[512,128]{1,0:T(8,128)(2,1)S(1)}, u32[]{:S(2)}, u32[]{:S(2)}) collective-permute-start(bf16[512,128]{1,0:T(8,128)(2,1)} %bitcast.18), channel_id=1, source_target_pairs={{0,4},{1,5},{2,6},{3,7},{4,0},{5,1},{6,2},{7,3},{8,12},{9,13},{10,... | collective-permute-start | bytes 393224 | tf_op jit(solution)/shard_map/ppermute | solution.py:344
  4.0 11.1 %collective-permute-start.11 = (bf16[512,128]{1,0:T(8,128)(2,1)}, bf16[512,128]{1,0:T(8,128)(2,1)S(1)}, u32[]{:S(2)}, u32[]{:S(2)}) collective-permute-start(bf16[512,128]{1,0:T(8,128)(2,1)} %bitcast.19), channel_id=1, source_target_pairs={{0,2},{1,3},{2,0},{3,1},{4,6},{5,7},{6,4},{7,5},{8,10},{9,11},{10,... | collective-permute-start | bytes 393224 | tf_op jit(solution)/shard_map/ppermute | solution.py:344
  5.6 9.5 %collective-permute-start.7 = (bf16[512,128]{1,0:T(8,128)(2,1)}, bf16[512,128]{1,0:T(8,128)(2,1)S(1)}, u32[]{:S(2)}, u32[]{:S(2)}) collective-permute-start(bf16[512,128]{1,0:T(8,128)(2,1)} %bitcast.20), channel_id=1, source_target_pairs={{0,6},{1,7},{2,4},{3,5},{4,2},{5,3},{6,0},{7,1},{8,14},{9,15},{10,... | collective-permute-start | bytes 393224 | tf_op jit(solution)/shard_map/ppermute | solution.py:344
  5.6 28.8 %collective-permute-start.1 = (bf16[512,128]{1,0:T(8,128)(2,1)}, bf16[512,128]{1,0:T(8,128)(2,1)S(1)}, u32[]{:S(2)}, u32[]{:S(2)}) collective-permute-start(bf16[512,128]{1,0:T(8,128)(2,1)} %bitcast.21), channel_id=1, source_target_pairs={{0,1},{1,0},{2,3},{3,2},{4,5},{5,4},{6,7},{7,6},{8,9},{9,8},{10,11... | collective-permute-start | bytes 393224 | tf_op jit(solution)/shard_map/ppermute | solution.py:344
  7.4 113.2 %collective-permute-start.15 = (bf16[512,1024]{1,0:T(8,128)(2,1)}, bf16[512,1024]{1,0:T(8,128)(2,1)S(1)}, u32[]{:S(2)}, u32[]{:S(2)}) collective-permute-start(bf16[512,1024]{1,0:T(8,128)(2,1)} %bitcast.14), channel_id=1, source_target_pairs={{0,8},{8,0},{1,9},{9,1},{2,10},{10,2},{3,11},{11,3},{4,12},{12,4},... | collective-permute-start | bytes 3145736 | tf_op jit(solution)/shard_map/ppermute | solution.py:347
  12.2 5.5 %collective-permute-start.4 = (bf16[512,128]{1,0:T(8,128)(2,1)S(1)}, bf16[512,128]{1,0:T(8,128)(2,1)S(1)}, u32[]{:S(2)}, u32[]{:S(2)}) collective-permute-start(bf16[512,128]{1,0:T(8,128)(2,1)S(1)} %collective-permute-done.3.q_ref), channel_id=1, source_target_pairs={{0,1},{1,0},{2,3},{3,2},{4,5},{5,4},{6,7},{7,6},{8,9},{9,8},{10,11... | collective-permute-start | bytes 393224 | tf_op jit(solution)/shard_map/ppermute | solution.py:344
  15.1 127.1 %collective-permute-start = (bf16[512,1024]{1,0:T(8,128)(2,1)}, bf16[512,1024]{1,0:T(8,128)(2,1)S(1)}, u32[]{:S(2)}, u32[]{:S(2)}) collective-permute-start(bf16[512,1024]{1,0:T(8,128)(2,1)} %bitcast.16), channel_id=1, source_target_pairs={{0,8},{8,0},{1,9},{9,1},{2,10},{10,2},{3,11},{11,3},{4,12},{12,4},... | collective-permute-start | bytes 3145736 | tf_op jit(solution)/shard_map/ppermute | solution.py:347
  15.1 45.2 %collective-permute-start.12 = (bf16[512,128]{1,0:T(8,128)(2,1)S(1)}, bf16[512,128]{1,0:T(8,128)(2,1)S(1)}, u32[]{:S(2)}, u32[]{:S(2)}) collective-permute-start(bf16[512,128]{1,0:T(8,128)(2,1)S(1)} %collective-permute-done.11.q_ref), channel_id=1, source_target_pairs={{0,1},{1,0},{2,3},{3,2},{4,5},{5,4},{6,7},{7,6},{8,9},{9,8},{10,11... | collective-permute-start | bytes 393224 | tf_op jit(solution)/shard_map/ppermute | solution.py:344
  17.7 31.0 %collective-permute-start.8 = (bf16[512,128]{1,0:T(8,128)(2,1)S(1)}, bf16[512,128]{1,0:T(8,128)(2,1)S(1)}, u32[]{:S(2)}, u32[]{:S(2)}) collective-permute-start(bf16[512,128]{1,0:T(8,128)(2,1)S(1)} %collective-permute-done.7.q_ref), channel_id=1, source_target_pairs={{0,1},{1,0},{2,3},{3,2},{4,5},{5,4},{6,7},{7,6},{8,9},{9,8},{10,11... | collective-permute-start | bytes 393224 | tf_op jit(solution)/shard_map/ppermute | solution.py:344
  34.4 35.7 %collective-permute-start.5 = (bf16[528,128]{1,0:T(8,128)(2,1)S(1)}, bf16[528,128]{1,0:T(8,128)(2,1)S(1)}, u32[]{:S(2)}, u32[]{:S(2)}) collective-permute-start(bf16[528,128]{1,0:T(8,128)(2,1)S(1)} %shard_map.104), channel_id=1, source_target_pairs={{0,1},{1,0},{2,3},{3,2},{4,5},{5,4},{6,7},{7,6},{8,9},{9,8},{10,11... | collective-permute-start | bytes 405512 | tf_op jit(solution)/shard_map/ppermute | solution.py:344
  48.8 56.3 %collective-permute-start.2 = (bf16[528,128]{1,0:T(8,128)(2,1)S(1)}, bf16[528,128]{1,0:T(8,128)(2,1)S(1)}, u32[]{:S(2)}, u32[]{:S(2)}) collective-permute-start(bf16[528,128]{1,0:T(8,128)(2,1)S(1)} %shard_map.101), channel_id=1, source_target_pairs={{0,1},{1,0},{2,3},{3,2},{4,5},{5,4},{6,7},{7,6},{8,9},{9,8},{10,11... | collective-permute-start | bytes 405512 | tf_op jit(solution)/shard_map/ppermute | solution.py:344
  60.4 41.1 %collective-permute-start.9 = (bf16[528,128]{1,0:T(8,128)(2,1)S(1)}, bf16[528,128]{1,0:T(8,128)(2,1)S(1)}, u32[]{:S(2)}, u32[]{:S(2)}) collective-permute-start(bf16[528,128]{1,0:T(8,128)(2,1)S(1)} %shard_map.107), channel_id=1, source_target_pairs={{0,1},{1,0},{2,3},{3,2},{4,5},{5,4},{6,7},{7,6},{8,9},{9,8},{10,11... | collective-permute-start | bytes 405512 | tf_op jit(solution)/shard_map/ppermute | solution.py:344
  70.1 32.3 %collective-permute-start.13 = (bf16[528,128]{1,0:T(8,128)(2,1)S(1)}, bf16[528,128]{1,0:T(8,128)(2,1)S(1)}, u32[]{:S(2)}, u32[]{:S(2)}) collective-permute-start(bf16[528,128]{1,0:T(8,128)(2,1)S(1)} %shard_map.110), channel_id=1, source_target_pairs={{0,1},{1,0},{2,3},{3,2},{4,5},{5,4},{6,7},{7,6},{8,9},{9,8},{10,11... | collective-permute-start | bytes 405512 | tf_op jit(solution)/shard_map/ppermute | solution.py:344
  101.5 19.1 %collective-permute-start.6 = (bf16[528,128]{1,0:T(8,128)(2,1)S(1)}, bf16[528,128]{1,0:T(8,128)(2,1)S(1)}, u32[]{:S(2)}, u32[]{:S(2)}) collective-permute-start(bf16[528,128]{1,0:T(8,128)(2,1)S(1)} %shard_map.105), channel_id=1, source_target_pairs={{0,4},{1,5},{2,6},{3,7},{4,0},{5,1},{6,2},{7,3},{8,12},{9,13},{10,... | collective-permute-start | bytes 405512 | tf_op jit(solution)/shard_map/ppermute | solution.py:344
  102.5 18.1 %collective-permute-start.10 = (bf16[528,128]{1,0:T(8,128)(2,1)S(1)}, bf16[528,128]{1,0:T(8,128)(2,1)S(1)}, u32[]{:S(2)}, u32[]{:S(2)}) collective-permute-start(bf16[528,128]{1,0:T(8,128)(2,1)S(1)} %shard_map.108), channel_id=1, source_target_pairs={{0,6},{1,7},{2,4},{3,5},{4,2},{5,3},{6,0},{7,1},{8,14},{9,15},{10,... | collective-permute-start | bytes 405512 | tf_op jit(solution)/shard_map/ppermute | solution.py:344
  105.0 15.5 %collective-permute-start.14 = (bf16[528,128]{1,0:T(8,128)(2,1)S(1)}, bf16[528,128]{1,0:T(8,128)(2,1)S(1)}, u32[]{:S(2)}, u32[]{:S(2)}) collective-permute-start(bf16[528,128]{1,0:T(8,128)(2,1)S(1)} %shard_map.111), channel_id=1, source_target_pairs={{0,2},{1,3},{2,0},{3,1},{4,6},{5,7},{6,4},{7,5},{8,10},{9,11},{10,... | collective-permute-start | bytes 405512 | tf_op jit(solution)/shard_map/ppermute | solution.py:344
  127.4 21.3 %copy-start.4 = (bf16[8,64,1024]{2,1,0:T(8,128)(2,1)S(1)}, bf16[8,64,1024]{2,1,0:T(8,128)(2,1)}, u32[]{:S(2)}) copy-start(bf16[8,64,1024]{2,1,0:T(8,128)(2,1)} %param.18) | copy-start | bytes 3145732
  127.4 12.6 %collective-permute-start.16 = (bf16[64,1152]{1,0:T(8,128)(2,1)S(1)}, bf16[64,1152]{1,0:T(8,128)(2,1)S(1)}, u32[]{:S(2)}, u32[]{:S(2)}) collective-permute-start(bf16[64,1152]{1,0:T(8,128)(2,1)S(1)} %get-tuple-element.18), channel_id=1, source_target_pairs={{0,1},{1,0},{2,3},{3,2},{4,5},{5,4},{6,7},{7,6},{8,9},{9,8},{10,11... | collective-permute-start | bytes 442376 | tf_op jit(solution)/shard_map/ppermute | solution.py:344
  127.5 9.6 %collective-permute-start.18 = (bf16[64,1152]{1,0:T(8,128)(2,1)S(1)}, bf16[64,1152]{1,0:T(8,128)(2,1)S(1)}, u32[]{:S(2)}, u32[]{:S(2)}) collective-permute-start(bf16[64,1152]{1,0:T(8,128)(2,1)S(1)} %get-tuple-element.20), channel_id=1, source_target_pairs={{0,1},{1,0},{2,3},{3,2},{4,5},{5,4},{6,7},{7,6},{8,9},{9,8},{10,11... | collective-permute-start | bytes 442376 | tf_op jit(solution)/shard_map/ppermute | solution.py:344
  129.5 10.8 %collective-permute-start.20 = (bf16[64,1152]{1,0:T(8,128)(2,1)S(1)}, bf16[64,1152]{1,0:T(8,128)(2,1)S(1)}, u32[]{:S(2)}, u32[]{:S(2)}) collective-permute-start(bf16[64,1152]{1,0:T(8,128)(2,1)S(1)} %get-tuple-element.22), channel_id=1, source_target_pairs={{0,1},{1,0},{2,3},{3,2},{4,5},{5,4},{6,7},{7,6},{8,9},{9,8},{10,11... | collective-permute-start | bytes 442376 | tf_op jit(solution)/shard_map/ppermute | solution.py:344
  129.6 12.4 %collective-permute-start.22 = (bf16[64,1152]{1,0:T(8,128)(2,1)S(1)}, bf16[64,1152]{1,0:T(8,128)(2,1)S(1)}, u32[]{:S(2)}, u32[]{:S(2)}) collective-permute-start(bf16[64,1152]{1,0:T(8,128)(2,1)S(1)} %get-tuple-element.24), channel_id=1, source_target_pairs={{0,1},{1,0},{2,3},{3,2},{4,5},{5,4},{6,7},{7,6},{8,9},{9,8},{10,11... | collective-permute-start | bytes 442376 | tf_op jit(solution)/shard_map/ppermute | solution.py:344
  137.2 7.1 %collective-permute-start.19 = (bf16[64,1152]{1,0:T(8,128)(2,1)S(1)}, bf16[64,1152]{1,0:T(8,128)(2,1)S(1)}, u32[]{:S(2)}, u32[]{:S(2)}) collective-permute-start(bf16[64,1152]{1,0:T(8,128)(2,1)S(1)} %shard_map.115), channel_id=1, source_target_pairs={{0,6},{1,7},{2,4},{3,5},{4,2},{5,3},{6,0},{7,1},{8,14},{9,15},{10,... | collective-permute-start | bytes 442376 | tf_op jit(solution)/shard_map/ppermute | solution.py:344
  140.1 8.5 %collective-permute-start.17 = (bf16[64,1152]{1,0:T(8,128)(2,1)S(1)}, bf16[64,1152]{1,0:T(8,128)(2,1)S(1)}, u32[]{:S(2)}, u32[]{:S(2)}) collective-permute-start(bf16[64,1152]{1,0:T(8,128)(2,1)S(1)} %shard_map.114), channel_id=1, source_target_pairs={{0,4},{1,5},{2,6},{3,7},{4,0},{5,1},{6,2},{7,3},{8,12},{9,13},{10,... | collective-permute-start | bytes 442376 | tf_op jit(solution)/shard_map/ppermute | solution.py:344
  140.3 8.3 %collective-permute-start.21 = (bf16[64,1152]{1,0:T(8,128)(2,1)S(1)}, bf16[64,1152]{1,0:T(8,128)(2,1)S(1)}, u32[]{:S(2)}, u32[]{:S(2)}) collective-permute-start(bf16[64,1152]{1,0:T(8,128)(2,1)S(1)} %shard_map.116), channel_id=1, source_target_pairs={{0,2},{1,3},{2,0},{3,1},{4,6},{5,7},{6,4},{7,5},{8,10},{9,11},{10,... | collective-permute-start | bytes 442376 | tf_op jit(solution)/shard_map/ppermute | solution.py:344
  (8 other events, 76.8 us)

commit v2 on v1

--- a/solution.py
+++ b/solution.py
@@ -12,7 +12,8 @@
 DEAD = -1e30
 LANES = 128
 TILE = 16
-VMEM_BYTES = 40 * 1024 * 1024
+SMALL = 8 * 1024 * 1024
+LARGE = 32 * 1024 * 1024
 
 
 def call(body, grid, in_specs, out_shape, out_specs, scratch=(), prefetch=1, cost=None):
@@ -26,7 +27,7 @@
             scratch_shapes=list(scratch),
         ),
         out_shape=out_shape,
-        compiler_params=pltpu.CompilerParams(vmem_limit_bytes=VMEM_BYTES),
+        compiler_params=pltpu.CompilerParams(vmem_limit_bytes=SMALL),
         cost_estimate=cost,
     )
 
@@ -44,69 +45,96 @@
     return lax.broadcasted_iota(jnp.int32, shape, dim)
 
 
-def attend_body(steps, heads, scale, sc_ref, q_ref, k_ref, v_ref, o_ref):
-    step = pl.program_id(0)
-    reqs, positions = k_ref.shape[0], k_ref.shape[2]
+def attend_part(heads, scale, q, live, keys, values, first_tile, o_ref):
+    rows, positions = keys.shape[0], keys.shape[1]
     per_tile = TILE // heads
-    tiles = reqs // per_tile
-    body_rows = steps * tiles * TILE
+    tiles = rows // per_tile
     row = iota((TILE, LANES), 0) // heads
     lane = iota((TILE, LANES), 1)
-    pos = iota((TILE, positions), 1)
-    prow = iota((TILE, positions), 0) // heads
+    scores = []
+    for g in range(tiles):
+        left = q[g * TILE : (g + 1) * TILE, :]
+        zero = jnp.zeros_like(left)
+        left = jnp.concatenate([jnp.where(row == a, left, zero) for a in range(per_tile)], axis=1)
+        right = jnp.concatenate([keys[g * per_tile + a] for a in range(per_tile)], axis=1)
+        scores.append(
+            lax.dot_general(left, right, (((1,), (1,)), ((), ())), preferred_element_type=F32)
+        )
+    s = jnp.concatenate(scores, axis=0) * scale
+    alive = iota(s.shape, 1) < live[:, :positions]
+    s = jnp.where(alive, s, DEAD)
+    high, mid = split2(jnp.max(s, axis=1, keepdims=True))
+    p = jnp.where(alive, jnp.exp(s - (high + mid)), 0.0)
+    lhigh, lmid = split2(jnp.sum(p, axis=1, keepdims=True))
+    p = p.astype(BF16)
     stat = jnp.zeros((TILE, LANES), F32)
     for g in range(tiles):
-        q = q_ref[pl.ds(g * TILE, TILE), :]
-        zero = jnp.zeros_like(q)
-        left = jnp.concatenate([jnp.where(row == a, q, zero) for a in range(per_tile)], axis=1)
-        right = jnp.concatenate([k_ref[g * per_tile + a, 0] for a in range(per_tile)], axis=1)
-        s = lax.dot_general(left, right, (((1,), (1,)), ((), ())), preferred_element_type=F32) * scale
-        first = step * reqs + g * per_tile
-        live = jnp.zeros((TILE, positions), jnp.int32)
-        for a in range(per_tile):
-            live = jnp.where(prow == a, sc_ref[1 + first + a], live)
-        alive = pos < live
-        s = jnp.where(alive, s, DEAD)
-        high, mid = split2(jnp.max(s, axis=1, keepdims=True))
-        p = jnp.where(alive, jnp.exp(s - (high + mid)), 0.0)
-        lhigh, lmid = split2(jnp.sum(p, axis=1, keepdims=True))
-        values = jnp.concatenate([v_ref[g * per_tile + a, 0] for a in range(per_tile)], axis=1)
-        wide = jnp.dot(p.astype(BF16), values, preferred_element_type=F32)
+        at = slice(g * TILE, (g + 1) * TILE)
+        right = jnp.concatenate([values[g * per_tile + a] for a in range(per_tile)], axis=1)
+        wide = jnp.dot(p[at], right, preferred_element_type=F32)
         acc = wide[:, :LANES]
         for a in range(1, per_tile):
             acc = jnp.where(row == a, wide[:, a * LANES : (a + 1) * LANES], acc)
-        o_ref[pl.ds(pl.multiple_of((step * tiles + g) * TILE, TILE), TILE), :] = acc.astype(BF16)
-        at = 4 * (step * tiles + g)
+        to = first_tile + g
+        o_ref[to * TILE : (to + 1) * TILE, :] = acc.astype(BF16)
         for n, val in enumerate((high, mid, lhigh, lmid)):
-            stat = jnp.where(lane == at + n, val, stat)
-
-    @pl.when(step == 0)
-    def _():
-        o_ref[pl.ds(body_rows, TILE), :] = stat.astype(BF16)
-
-    @pl.when(step > 0)
-    def _():
-        o_ref[pl.ds(body_rows, TILE), :] = (o_ref[pl.ds(body_rows, TILE), :].astype(F32) + stat).astype(BF16)
-
-
-def attend(scalars, q, keys, values, heads, scale):
+            stat = jnp.where(lane == 4 * to + n, val[at], stat)
+    return stat
+
+
+def attend_body(n, blocks, heads, scale, sc_ref, live_ref, k_hbm, v_hbm, *refs):
+    q_refs, o_refs = refs[:n], refs[n : 2 * n]
+    k_buf, v_buf, k_sem, v_sem = refs[2 * n :]
+    size = k_hbm.shape[0] // blocks
+    copies = []
+    for j in range(n):
+        kv = sc_ref[j]
+        for b in range(blocks):
+            at, i = pl.ds(b * size, size), j * blocks + b
+            copies.append(
+                (
+                    pltpu.make_async_copy(k_hbm.at[at, kv], k_buf.at[i], k_sem.at[i]),
+                    pltpu.make_async_copy(v_hbm.at[at, kv], v_buf.at[i], v_sem.at[i]),
+                )
+            )
+    for ck, cv in copies:
+        ck.start()
+        cv.start()
+    many = size * heads
+    for j in range(n):
+        stat = jnp.zeros((TILE, LANES), F32)
+        for b in range(blocks):
+            i = j * blocks + b
+            copies[i][0].wait()
+            copies[i][1].wait()
+            at = slice(b * many, (b + 1) * many)
+            stat = stat + attend_part(
+                heads, scale, q_refs[j][at, :], live_ref[at, :], k_buf.at[i], v_buf.at[i],
+                b * many // TILE, o_refs[j],
+            )
+        o_refs[j][many * blocks :, :] = stat.astype(BF16)
+
+
+def attend(which, queries, live, keys, values, heads, scale):
+    n, blocks = len(queries), 2
     rows, _, positions, width = keys.shape
-    steps = 4
-    block = rows // steps
-    kv = pl.BlockSpec((block, 1, positions, width), lambda i, sc: (i, sc[0], 0, 0))
-    n = rows * heads + TILE
-    return call(
-        functools.partial(attend_body, steps, heads, scale),
-        (steps,),
-        [pl.BlockSpec((block * heads, width), lambda i, sc: (i, 0)), kv, kv],
-        jax.ShapeDtypeStruct((n, width), BF16),
-        whole((n, width)),
-        cost=pl.CostEstimate(
-            flops=4 * rows * heads * positions * width * 8,
-            bytes_accessed=4 * rows * positions * width,
-            transcendentals=rows * heads * positions,
+    vmem = pl.BlockSpec(memory_space=pltpu.VMEM)
+    hbm = pl.BlockSpec(memory_space=pltpu.HBM)
+    buf = pltpu.VMEM((n * blocks, rows // blocks, positions, width), BF16)
+    sem = pltpu.SemaphoreType.DMA((n * blocks,))
+    return pl.pallas_call(
+        functools.partial(attend_body, n, blocks, heads, scale),
+        in_specs=[pl.BlockSpec(memory_space=pltpu.SMEM), vmem, hbm, hbm] + [vmem] * n,
+        out_specs=[vmem] * n,
+        out_shape=[jax.ShapeDtypeStruct((rows * heads + TILE, width), BF16)] * n,
+        scratch_shapes=[buf, buf, sem, sem],
+        compiler_params=pltpu.CompilerParams(vmem_limit_bytes=LARGE),
+        cost_estimate=pl.CostEstimate(
+            flops=32 * n * rows * heads * positions * width,
+            bytes_accessed=4 * n * rows * positions * width,
+            transcendentals=n * rows * heads * positions,
         ),
-    )(scalars, q, keys, values)
+    )(which, live, keys, values, *queries)
 
 
 def combine(stats):
@@ -145,7 +173,7 @@
     return pl.pallas_call(
         pair_body,
         out_shape=jax.ShapeDtypeStruct(a.shape, BF16),
-        compiler_params=pltpu.CompilerParams(vmem_limit_bytes=VMEM_BYTES),
+        compiler_params=pltpu.CompilerParams(vmem_limit_bytes=SMALL),
         cost_estimate=pl.CostEstimate(flops=3 * a.size, bytes_accessed=6 * a.size, transcendentals=0),
     )(a, b)
 
@@ -174,88 +202,93 @@
     return total
 
 
-def project_body(n_parts, n_out, heads, rank, sc_ref, *refs):
+def fetch(scalars, first, w_ref, buf, sem):
+    cols = buf.shape[2]
+    copies = []
+    for k in range(buf.shape[0]):
+        at = pl.ds(pl.multiple_of(scalars[first + k] * cols, cols), cols)
+        copies.append(pltpu.make_async_copy(w_ref.at[:, at], buf.at[k], sem.at[k]))
+        copies[-1].start()
+    return copies
+
+
+def project_body(n_parts, n_out, heads, rank, sc_ref, w_ref, *refs):
     parts = refs[:n_parts]
-    w_ref, slot_ref, down_a, down_b = refs[n_parts : n_parts + 4]
-    outs = refs[n_parts + 4 : n_parts + 4 + n_out]
-    att_ref, shrink_ref, att32 = refs[n_parts + 4 + n_out :]
-    step = pl.program_id(0)
-
-    @pl.when(step == 0)
-    def _():
-        finish_attention(parts, att32, att_ref, heads)
-        att = att_ref[...]
-        over = (((1,), (1,)), ((), ()))
-        own = lax.dot_general(att, down_a[...], over, preferred_element_type=F32)
-        other = lax.dot_general(att, down_b[...], over, preferred_element_type=F32)
-        slots = slot_ref[...]
-        per = down_a.shape[0] // rank
-        mine = sc_ref[0]
-        s = chosen(slots - mine * per, own, rank) + chosen(slots - (1 - mine) * per, other, rank)
-        s = s + pltpu.roll(s, rank, 1)
-        high, mid = split2(s)
-        shrink_ref[...] = jnp.where(iota(s.shape, 1) < rank, high, mid).astype(BF16)
-
-    for k in range(n_out):
-
-        @pl.when(step == k)
-        def _(k=k):
-            out = jnp.dot(att_ref[...], w_ref[...], preferred_element_type=F32)
-            outs[k][:, : out.shape[1]] = out.astype(BF16)
-            outs[k][:, out.shape[1] :] = shrink_ref[...]
+    slot_ref, down_a, down_b = refs[n_parts : n_parts + 3]
+    outs = refs[n_parts + 3 : n_parts + 3 + n_out]
+    att_ref, shrink_ref, att32, buf, sem = refs[n_parts + 3 + n_out :]
+    copies = fetch(sc_ref, 1, w_ref, buf, sem)
+    finish_attention(parts, att32, att_ref, heads)
+    att = att_ref[...]
+    over = (((1,), (1,)), ((), ()))
+    own = lax.dot_general(att, down_a[...], over, preferred_element_type=F32)
+    other = lax.dot_general(att, down_b[...], over, preferred_element_type=F32)
+    slots = slot_ref[...]
+    per = down_a.shape[0] // rank
+    mine = sc_ref[0]
+    s = chosen(slots - mine * per, own, rank) + chosen(slots - (1 - mine) * per, other, rank)
+    s = s + pltpu.roll(s, rank, 1)
+    high, mid = split2(s)
+    shrink = jnp.where(iota(s.shape, 1) < rank, high, mid).astype(BF16)
+    shrink_ref[...] = shrink
+    for k, out in enumerate(outs):
+        cols = buf.shape[2]
+        copies[k].wait()
+        out[:, :cols] = jnp.dot(att, buf[k], preferred_element_type=F32).astype(BF16)
+        out[:, cols:] = shrink
 
 
 def project(scalars, parts, weight, slots, down_a, down_b, heads, rank, cols):
     n_out = scalars.shape[0] - 1
     rows = slots.shape[0]
     width = weight.shape[0]
-    msg = jax.ShapeDtypeStruct((rows, cols + LANES), BF16)
-    outs = call(
+    vmem = pl.BlockSpec(memory_space=pltpu.VMEM)
+    outs = pl.pallas_call(
         functools.partial(project_body, len(parts), n_out, heads, rank),
-        (n_out,),
-        [whole(p.shape) for p in parts]
-        + [pl.BlockSpec((width, cols), lambda i, sc: (0, sc[1 + i]))]
-        + [whole(slots.shape), whole(down_a.shape), whole(down_b.shape)],
-        [msg] * n_out
+        in_specs=[pl.BlockSpec(memory_space=pltpu.SMEM), pl.BlockSpec(memory_space=pltpu.HBM)]
+        + [vmem] * (len(parts) + 3),
+        out_specs=[vmem] * (n_out + 2),
+        out_shape=[jax.ShapeDtypeStruct((rows, cols + LANES), BF16)] * n_out
         + [jax.ShapeDtypeStruct((rows, width), BF16), jax.ShapeDtypeStruct((rows, LANES), BF16)],
-        [whole(msg.shape)] * n_out + [whole((rows, width)), whole((rows, LANES))],
-        scratch=[pltpu.VMEM((rows * heads, LANES), F32)],
-        cost=pl.CostEstimate(
+        scratch_shapes=[
+            pltpu.VMEM((rows * heads, LANES), F32),
+            pltpu.VMEM((n_out, width, cols), BF16),
+            pltpu.SemaphoreType.DMA((n_out,)),
+        ],
+        compiler_params=pltpu.CompilerParams(vmem_limit_bytes=LARGE),
+        cost_estimate=pl.CostEstimate(
             flops=2 * rows * width * cols * n_out, bytes_accessed=2 * width * cols * n_out, transcendentals=0
         ),
-    )(scalars, *parts, weight, slots, down_a, down_b)
+    )(scalars, weight, *parts, slots, down_a, down_b)
     return outs[:n_out], outs[n_out], outs[n_out + 1]
 
 
-def project_more_body(n_out, sc_ref, att_ref, shrink_ref, w_ref, *outs):
-    step = pl.program_id(0)
-    for k in range(n_out):
-
-        @pl.when(step == k)
-        def _(k=k):
-            out = jnp.dot(att_ref[...], w_ref[...], preferred_element_type=F32)
-            outs[k][:, : out.shape[1]] = out
-            outs[k][:, out.shape[1] :] = shrink_ref[...].astype(F32)
+def project_more_body(n_out, sc_ref, w_ref, att_ref, shrink_ref, *refs):
+    outs = refs[:n_out]
+    buf, sem = refs[n_out:]
+    copies = fetch(sc_ref, 1, w_ref, buf, sem)
+    cols = buf.shape[2]
+    for k, out in enumerate(outs):
+        copies[k].wait()
+        out[:, :cols] = jnp.dot(att_ref[...], buf[k], preferred_element_type=F32)
+        out[:, cols:] = shrink_ref[...].astype(F32)
 
 
 def project_more(scalars, att, shrink, weight, cols):
     n_out = scalars.shape[0] - 1
     rows, width = att.shape
-    msg = jax.ShapeDtypeStruct((rows, cols + LANES), F32)
-    return call(
+    vmem = pl.BlockSpec(memory_space=pltpu.VMEM)
+    return pl.pallas_call(
         functools.partial(project_more_body, n_out),
-        (n_out,),
-        [
-            whole(att.shape),
-            whole(shrink.shape),
-            pl.BlockSpec((width, cols), lambda i, sc: (0, sc[1 + i])),
-        ],
-        [msg] * n_out,
-        [whole(msg.shape)] * n_out,
-        cost=pl.CostEstimate(
+        in_specs=[pl.BlockSpec(memory_space=pltpu.SMEM), pl.BlockSpec(memory_space=pltpu.HBM), vmem, vmem],
+        out_specs=[vmem] * n_out,
+        out_shape=[jax.ShapeDtypeStruct((rows, cols + LANES), F32)] * n_out,
+        scratch_shapes=[pltpu.VMEM((n_out, width, cols), BF16), pltpu.SemaphoreType.DMA((n_out,))],
+        compiler_params=pltpu.CompilerParams(vmem_limit_bytes=LARGE),
+        cost_estimate=pl.CostEstimate(
             flops=2 * rows * width * cols * n_out, bytes_accessed=2 * width * cols * n_out, transcendentals=0
         ),
-    )(scalars, att, shrink, weight)
+    )(scalars, weight, att, shrink)
 
 
 def shrink_sum(parts, rank):
@@ -275,7 +308,7 @@
     return pl.pallas_call(
         functools.partial(add_body, rank),
         out_shape=jax.ShapeDtypeStruct(a.shape, BF16),
-        compiler_params=pltpu.CompilerParams(vmem_limit_bytes=VMEM_BYTES),
+        compiler_params=pltpu.CompilerParams(vmem_limit_bytes=SMALL),
         cost_estimate=pl.CostEstimate(flops=a.size, bytes_accessed=8 * a.size, transcendentals=0),
     )(a, b)
 
@@ -362,15 +395,23 @@
     down_b, up_b = across(down_a), across(up_a)
 
     live = jnp.clip(cache_live_length - me * positions, 0, positions)
+    live = jnp.broadcast_to(jnp.repeat(live, heads)[:, None], (rows * heads, LANES)).astype(jnp.int32)
     scale = 1.0 / math.sqrt(width)
-
-    def attended(k):
-        head = ((me ^ k) * heads) // group
-        scalars = jnp.concatenate([head[None], live]).astype(jnp.int32)
-        return attend(scalars, held[k], cached_key_rows, cached_value_rows, heads, scale)
-
-    sent = {k: hop(attended(k ^ 1), 1) for k in [0] + far}
-    merged = {k: pair(attended(k), sent[k]) for k in [0] + far}
+    keys, values, weight = (
+        pltpu.with_memory_space_constraint(x, pltpu.HBM)
+        for x in (cached_key_rows, cached_value_rows, output_weight)
+    )
+
+    def attended(*ks):
+        which = jnp.stack([lax.div((me ^ k) * heads, group) for k in ks]).astype(jnp.int32)
+        return attend(which, [held[k] for k in ks], live, keys, values, heads, scale)
+
+    partial = dict(zip([1, 0], attended(1, 0)))
+    partial.update(zip(far, attended(*far)))
+    for k in far:
+        (partial[k ^ 1],) = attended(k ^ 1)
+    sent = {k: hop(partial[k ^ 1], 1) for k in [0] + far}
+    merged = {k: pair(partial[k], sent[k]) for k in [0] + far}
     parts = [merged[0]] + [hop(merged[k], k) for k in far]
 
     total_slots = adapter_slot_index.shape[0]
@@ -381,11 +422,9 @@
     order = jnp.array([k for k in outer], jnp.int32)
     to_pair = jnp.concatenate([mine[None], me ^ order ^ 1]).astype(jnp.int32)
     to_own = jnp.concatenate([mine[None], me ^ order]).astype(jnp.int32)
-    first, att, shrink = project(
-        to_pair, parts, output_weight, slots, down_a, down_b, heads, rank, cols
-    )
+    first, att, shrink = project(to_pair, parts, weight, slots, down_a, down_b, heads, rank, cols)
     arrived = [hop(x, 1) for x in first]
-    own = project_more(to_own, att, shrink, output_weight, cols)
+    own = project_more(to_own, att, shrink, weight, cols)
     summed = [add(a, b, rank) for a, b in zip(own, arrived)]
     final = [hop(x, k) if k else x for x, k in zip(summed, outer)]
     return last(mine[None].astype(jnp.int32), slots, up_a, up_b, final, rank)

time: 150 us -> 84.5 us (0.56)
  Pallas kernels: 92.1 us -> 30.3 us
  local copies, waits for them, and re-layouts: 13.8 us -> 0.38 us
  waiting for transfers between devices: 13 us -> 23.7 us
  starting transfers between devices: 29.6 us -> 28 us
    pallas_call x10 -> x7, Pallas kernels: 89.1 us -> 27.3 us  [the longest x5 16.9 us: attend(): pl.pallas_call(functools.partial(attend_body, n, blocks, heads, scale), i...]
    unnamed x18 -> x10, local copies, waits for them, and re-layouts: 13.7 us -> 0.02 us
    ppermute x21, waiting for transfers between devices: 13 us -> 23.7 us  [hop(): return lax.ppermute(x, 'tensor', [(i, i ^ k) for i in range(tensor)])]
    ppermute x21, starting transfers between devices: 29.6 us -> 27.5 us  [hop(): return lax.ppermute(x, 'tensor', [(i, i ^ k) for i in range(tensor)])]
  transfers between devices with their start and end apart: 23 -> 23, of which waited for: 4 -> 6; matrix products, arithmetic and copies ran while one was open for 1% -> 2% of each run, Pallas kernels for 61% -> 34%
where the time goes in v2:
time: 84.5 us; the launch traced here: 84.4 us
  Pallas kernels  30.3 us (36%)
  starting transfers between devices  28 us (33%)
  waiting for transfers between devices  23.7 us (28%)
  other arithmetic  1.7 us (2%)
    ppermute x21, starting transfers between devices, hop(): return lax.ppermute(x, 'tensor', [(i, i ^ k) for i in range(tensor)])  27.5 us
    ppermute x21, waiting for transfers between devices, hop(): return lax.ppermute(x, 'tensor', [(i, i ^ k) for i in range(tensor)])  23.7 us
    pallas_call x5, Pallas kernels, attend(): pl.pallas_call(functools.partial(attend_body, n, blocks, heads, scale), i...  16.9 us
    pallas_call x1, Pallas kernels, project(): pl.pallas_call(functools.partial(project_body, len(parts), n_out, heads,...  5.83 us
    pallas_call x1, Pallas kernels, project_more(): pl.pallas_call(functools.partial(project_more_body, n_out), in_specs=[pl....  4.55 us
  transfers between devices with their start and end apart: 23, of which 6 were waited for; matrix products, arithmetic and copies ran while one was open for 2% of the time, Pallas kernels for 34%

profile of v2, /device:TPU:0, one launch (start us, length us, event | category | flops | bytes accessed | tf_op | source)
XLA Modules:
  0.0 84.4 jit_solution(14332369110590405828)
XLA Ops:
  0.0 3.0 %collective-permute-start.5 = (bf16[512,128]{1,0:T(8,128)(2,1)}, bf16[512,128]{1,0:T(8,128)(2,1)S(1)}, u32[]{:S(2)}, u32[]{:S(2)}) collective-permute-start(bf16[512,128]{1,0:T(8,128)(2,1)} %bitcast.18), channel_id=1, source_target_pairs={{0,2},{1,3},{2,0},{3,1},{4,6},{5,7},{6,4},{7,5},{8,10},{9,11},{10,... | collective-permute-start | bytes 393224 | tf_op jit(solution)/shard_map/ppermute | solution.py:377
  3.0 2.5 %collective-permute-start.4 = (bf16[512,128]{1,0:T(8,128)(2,1)}, bf16[512,128]{1,0:T(8,128)(2,1)S(1)}, u32[]{:S(2)}, u32[]{:S(2)}) collective-permute-start(bf16[512,128]{1,0:T(8,128)(2,1)} %bitcast.19), channel_id=1, source_target_pairs={{0,6},{1,7},{2,4},{3,5},{4,2},{5,3},{6,0},{7,1},{8,14},{9,15},{10,... | collective-permute-start | bytes 393224 | tf_op jit(solution)/shard_map/ppermute | solution.py:377
  5.6 1.5 %collective-permute-start.1 = (bf16[512,128]{1,0:T(8,128)(2,1)}, bf16[512,128]{1,0:T(8,128)(2,1)S(1)}, u32[]{:S(2)}, u32[]{:S(2)}) collective-permute-start(bf16[512,128]{1,0:T(8,128)(2,1)} %bitcast.21), channel_id=1, source_target_pairs={{0,1},{1,0},{2,3},{3,2},{4,5},{5,4},{6,7},{7,6},{8,9},{9,8},{10,11... | collective-permute-start | bytes 393224 | tf_op jit(solution)/shard_map/ppermute | solution.py:377
  8.3 9.2 %collective-permute-done.3.refs_0_ = bf16[512,128]{1,0:T(8,128)(2,1)S(1)} collective-permute-done((bf16[512,128]{1,0:T(8,128)(2,1)}, bf16[512,128]{1,0:T(8,128)(2,1)S(1)}, u32[]{:S(2)}, u32[]{:S(2)}) %collective-permute-start.3) | collective-permute-done | bytes 131104 | tf_op jit(solution)/shard_map/ppermute | solution.py:377
  17.5 1.5 %collective-permute-start.6 = (bf16[512,128]{1,0:T(8,128)(2,1)S(1)}, bf16[512,128]{1,0:T(8,128)(2,1)S(1)}, u32[]{:S(2)}, u32[]{:S(2)}) collective-permute-start(bf16[512,128]{1,0:T(8,128)(2,1)S(1)} %collective-permute-done.3.refs_0_), channel_id=1, source_target_pairs={{0,1},{1,0},{2,3},{3,2},{4,5},{5,4},{6,7},{7,6},{8,9},{9,8},{10,11... | collective-permute-start | bytes 393224 | tf_op jit(solution)/shard_map/ppermute | solution.py:377
  20.4 3.2 %collective-permute-done.6.refs_0_ = bf16[512,128]{1,0:T(8,128)(2,1)S(1)} collective-permute-done((bf16[512,128]{1,0:T(8,128)(2,1)S(1)}, bf16[512,128]{1,0:T(8,128)(2,1)S(1)}, u32[]{:S(2)}, u32[]{:S(2)}) %collective-permute-start.6) | collective-permute-done | bytes 131104 | tf_op jit(solution)/shard_map/ppermute | solution.py:377
  23.6 1.7 %collective-permute-start.9 = (bf16[512,128]{1,0:T(8,128)(2,1)S(1)}, bf16[512,128]{1,0:T(8,128)(2,1)S(1)}, u32[]{:S(2)}, u32[]{:S(2)}) collective-permute-start(bf16[512,128]{1,0:T(8,128)(2,1)S(1)} %collective-permute-done.4.refs_1_), channel_id=1, source_target_pairs={{0,1},{1,0},{2,3},{3,2},{4,5},{5,4},{6,7},{7,6},{8,9},{9,8},{10,11... | collective-permute-start | bytes 393224 | tf_op jit(solution)/shard_map/ppermute | solution.py:377
  25.5 2.5 %shard_map.103 = bf16[528,128]{1,0:T(8,128)(2,1)S(1)} custom-call(s32[1]{0:T(128)} %bitcast.8.sc_ref, s32[512,128]{1,0:T(8,128)S(1)} %broadcast_in_dim.42.live_ref, bf16[64,8,96,128]{3,2,1,0:T(8,128)(2,1)} %k_hbm.9, bf16[64,8,96,128]{3,2,1,0:T(8,128)(2,1)} %v_hbm.9, bf16[512,128]{1,0:T(8,128)(2,1)S(1)} %collective-permute-done.6.refs_0_), custom_call_target="tpu_custom_call" | custom-call | flops 201326592 | bytes 3145728 | tf_op jit(solution)/shard_map/pallas_call | solution.py:125
  28.5 4.2 %shard_map.100 = (bf16[528,128]{1,0:T(8,128)(2,1)S(1)}, bf16[528,128]{1,0:T(8,128)(2,1)S(1)}) custom-call(s32[2]{0:T(128)S(1)} %pad_add_fusion.2.sc_ref, s32[512,128]{1,0:T(8,128)S(1)} %broadcast_in_dim.42.live_ref, bf16[64,8,96,128]{3,2,1,0:T(8,128)(2,1)} %k_hbm.9, bf16[64,8,96,128]{3,2,1,0:T(8,128)(2,1)} %v_hbm.9, ...), custom_call_target="tpu_custom_call" | custom-call | flops 402653184 | bytes 6291456 | tf_op jit(solution)/shard_map/pallas_call | solution.py:125
  32.7 1.7 %collective-permute-start.2 = (bf16[528,128]{1,0:T(8,128)(2,1)S(1)}, bf16[528,128]{1,0:T(8,128)(2,1)S(1)}, u32[]{:S(2)}, u32[]{:S(2)}) collective-permute-start(bf16[528,128]{1,0:T(8,128)(2,1)S(1)} %get-tuple-element.21), channel_id=1, source_target_pairs={{0,1},{1,0},{2,3},{3,2},{4,5},{5,4},{6,7},{7,6},{8,9},{9,8},{10,11... | collective-permute-start | bytes 405512 | tf_op jit(solution)/shard_map/ppermute | solution.py:377
  34.4 2.5 %shard_map.105 = bf16[528,128]{1,0:T(8,128)(2,1)S(1)} custom-call(s32[1]{0:T(128)} %bitcast.9.sc_ref, s32[512,128]{1,0:T(8,128)S(1)} %broadcast_in_dim.42.live_ref, bf16[64,8,96,128]{3,2,1,0:T(8,128)(2,1)} %k_hbm.9, bf16[64,8,96,128]{3,2,1,0:T(8,128)(2,1)} %v_hbm.9, bf16[512,128]{1,0:T(8,128)(2,1)S(1)} %collective-permute-done.9.refs_0_), custom_call_target="tpu_custom_call" | custom-call | flops 201326592 | bytes 3145728 | tf_op jit(solution)/shard_map/pallas_call | solution.py:125
  37.4 2.5 %shard_map.107 = bf16[528,128]{1,0:T(8,128)(2,1)S(1)} custom-call(s32[1]{0:T(128)} %bitcast.10.sc_ref, s32[512,128]{1,0:T(8,128)S(1)} %broadcast_in_dim.42.live_ref, bf16[64,8,96,128]{3,2,1,0:T(8,128)(2,1)} %k_hbm.9, bf16[64,8,96,128]{3,2,1,0:T(8,128)(2,1)} %v_hbm.9, bf16[512,128]{1,0:T(8,128)(2,1)S(1)} %collective-permute-done.12.refs_0_), custom_call_target="tpu_custom_call" | custom-call | flops 201326592 | bytes 3145728 | tf_op jit(solution)/shard_map/pallas_call | solution.py:125
  39.8 1.7 %collective-permute-start.13 = (bf16[528,128]{1,0:T(8,128)(2,1)S(1)}, bf16[528,128]{1,0:T(8,128)(2,1)S(1)}, u32[]{:S(2)}, u32[]{:S(2)}) collective-permute-start(bf16[528,128]{1,0:T(8,128)(2,1)S(1)} %shard_map.107), channel_id=1, source_target_pairs={{0,1},{1,0},{2,3},{3,2},{4,5},{5,4},{6,7},{7,6},{8,9},{9,8},{10,11... | collective-permute-start | bytes 405512 | tf_op jit(solution)/shard_map/ppermute | solution.py:377
  41.6 5.2 %shard_map.102 = (bf16[528,128]{1,0:T(8,128)(2,1)S(1)}, bf16[528,128]{1,0:T(8,128)(2,1)S(1)}, bf16[528,128]{1,0:T(8,128)(2,1)S(1)}) custom-call(s32[3]{0:T(128)S(1)} %pad_add_fusion.3.sc_ref, s32[512,128]{1,0:T(8,128)S(1)} %broadcast_in_dim.42.live_ref, bf16[64,8,96,128]{3,2,1,0:T(8,128)(2,1)} %k_hbm.9, bf16[64,8,96,128]{3,2,1,0:T(8,128)(2,1)} %v_hbm.9, ...), custom_call_target="tpu_custom_call" | custom-call | flops 603979776 | bytes 9437184 | tf_op jit(solution)/shard_map/pallas_call | solution.py:125
  47.6 2.6 %collective-permute-start.11 = (bf16[528,128]{1,0:T(8,128)(2,1)S(1)}, bf16[528,128]{1,0:T(8,128)(2,1)S(1)}, u32[]{:S(2)}, u32[]{:S(2)}) collective-permute-start(bf16[528,128]{1,0:T(8,128)(2,1)S(1)} %shard_map.106), channel_id=1, source_target_pairs={{0,6},{1,7},{2,4},{3,5},{4,2},{5,3},{6,0},{7,1},{8,14},{9,15},{10,... | collective-permute-start | bytes 405512 | tf_op jit(solution)/shard_map/ppermute | solution.py:377
  52.1 4.0 %collective-permute-done.8.refs_1_ = bf16[528,128]{1,0:T(8,128)(2,1)S(1)} collective-permute-done((bf16[528,128]{1,0:T(8,128)(2,1)S(1)}, bf16[528,128]{1,0:T(8,128)(2,1)S(1)}, u32[]{:S(2)}, u32[]{:S(2)}) %collective-permute-start.8) | collective-permute-done | bytes 135200 | tf_op jit(solution)/shard_map/ppermute | solution.py:377
  57.4 5.8 %shard_map.109 = (bf16[64,1152]{1,0:T(8,128)(2,1)S(1)}, bf16[64,1152]{1,0:T(8,128)(2,1)S(1)}, bf16[64,1152]{1,0:T(8,128)(2,1)S(1)}, bf16[64,1152]{1,0:T(8,128)(2...) custom-call(s32[5]{0:T(128)S(1)} %pad_add_fusion.1.sc_ref, bf16[1024,8192]{1,0:T(8,128)(2,1)} %w_ref.3, ...), custom_call_target="tpu_custom_call" | custom-call | flops 536870912 | bytes 8388608 | tf_op jit(solution)/shard_map/pallas_call | solution.py:246
  63.8 1.5 %collective-permute-start.18 = (bf16[64,1152]{1,0:T(8,128)(2,1)S(1)}, bf16[64,1152]{1,0:T(8,128)(2,1)S(1)}, u32[]{:S(2)}, u32[]{:S(2)}) collective-permute-start(bf16[64,1152]{1,0:T(8,128)(2,1)S(1)} %get-tuple-element.30), channel_id=1, source_target_pairs={{0,1},{1,0},{2,3},{3,2},{4,5},{5,4},{6,7},{7,6},{8,9},{9,8},{10,11... | collective-permute-start | bytes 442376 | tf_op jit(solution)/shard_map/ppermute | solution.py:377
  65.9 1.5 %collective-permute-start.22 = (bf16[64,1152]{1,0:T(8,128)(2,1)S(1)}, bf16[64,1152]{1,0:T(8,128)(2,1)S(1)}, u32[]{:S(2)}, u32[]{:S(2)}) collective-permute-start(bf16[64,1152]{1,0:T(8,128)(2,1)S(1)} %get-tuple-element.34), channel_id=1, source_target_pairs={{0,1},{1,0},{2,3},{3,2},{4,5},{5,4},{6,7},{7,6},{8,9},{9,8},{10,11... | collective-permute-start | bytes 442376 | tf_op jit(solution)/shard_map/ppermute | solution.py:377
  67.5 4.6 %shard_map.110 = (f32[64,1152]{1,0:T(8,128)S(1)}, f32[64,1152]{1,0:T(8,128)S(1)}, f32[64,1152]{1,0:T(8,128)S(1)}, f32[64,1152]{1,0:T(8,128)S(1)}) custom-call(s32[5]{0:T(128)S(1)} %pad_add_fusion.sc_ref, bf16[1024,8192]{1,0:T(8,128)(2,1)} %w_ref.3, bf16[64,1024]{1,0:T(8,128)(2,1)S(1)} %get-tuple-element.25.att_ref, ...), custom_call_target="tpu_custom_call" | custom-call | flops 536870912 | bytes 8388608 | tf_op jit(solution)/shard_map/pallas_call | solution.py:281
  72.1 1.6 %collective-permute-start.19 = (bf16[64,1152]{1,0:T(8,128)(2,1)S(1)}, bf16[64,1152]{1,0:T(8,128)(2,1)S(1)}, u32[]{:S(2)}, u32[]{:S(2)}) collective-permute-start(bf16[64,1152]{1,0:T(8,128)(2,1)S(1)} %shard_map.112), channel_id=1, source_target_pairs={{0,6},{1,7},{2,4},{3,5},{4,2},{5,3},{6,0},{7,1},{8,14},{9,15},{10,... | collective-permute-start | bytes 442376 | tf_op jit(solution)/shard_map/ppermute | solution.py:377
  73.9 1.6 %collective-permute-start.17 = (bf16[64,1152]{1,0:T(8,128)(2,1)S(1)}, bf16[64,1152]{1,0:T(8,128)(2,1)S(1)}, u32[]{:S(2)}, u32[]{:S(2)}) collective-permute-start(bf16[64,1152]{1,0:T(8,128)(2,1)S(1)} %shard_map.111), channel_id=1, source_target_pairs={{0,4},{1,5},{2,6},{3,7},{4,0},{5,1},{6,2},{7,3},{8,12},{9,13},{10,... | collective-permute-start | bytes 442376 | tf_op jit(solution)/shard_map/ppermute | solution.py:377
  77.1 2.2 %collective-permute-done.19.refs_1_ = bf16[64,1152]{1,0:T(8,128)(2,1)S(1)} collective-permute-done((bf16[64,1152]{1,0:T(8,128)(2,1)S(1)}, bf16[64,1152]{1,0:T(8,128)(2,1)S(1)}, u32[]{:S(2)}, u32[]{:S(2)}) %collective-permute-start.19) | collective-permute-done | bytes 147488 | tf_op jit(solution)/shard_map/ppermute | solution.py:377
  79.3 3.9 %collective-permute-done.17.refs_0_ = bf16[64,1152]{1,0:T(8,128)(2,1)S(1)} collective-permute-done((bf16[64,1152]{1,0:T(8,128)(2,1)S(1)}, bf16[64,1152]{1,0:T(8,128)(2,1)S(1)}, u32[]{:S(2)}, u32[]{:S(2)}) %collective-permute-start.17) | collective-permute-done | bytes 147488 | tf_op jit(solution)/shard_map/ppermute | solution.py:377
  (59 shorter events, 11.9 us)
Async XLA Ops:
  0.0 7.8 %collective-permute-start.5 = (bf16[512,128]{1,0:T(8,128)(2,1)}, bf16[512,128]{1,0:T(8,128)(2,1)S(1)}, u32[]{:S(2)}, u32[]{:S(2)}) collective-permute-start(bf16[512,128]{1,0:T(8,128)(2,1)} %bitcast.18), channel_id=1, source_target_pairs={{0,2},{1,3},{2,0},{3,1},{4,6},{5,7},{6,4},{7,5},{8,10},{9,11},{10,... | collective-permute-start | bytes 393224 | tf_op jit(solution)/shard_map/ppermute | solution.py:377
  3.0 16.8 %collective-permute-start.4 = (bf16[512,128]{1,0:T(8,128)(2,1)}, bf16[512,128]{1,0:T(8,128)(2,1)S(1)}, u32[]{:S(2)}, u32[]{:S(2)}) collective-permute-start(bf16[512,128]{1,0:T(8,128)(2,1)} %bitcast.19), channel_id=1, source_target_pairs={{0,6},{1,7},{2,4},{3,5},{4,2},{5,3},{6,0},{7,1},{8,14},{9,15},{10,... | collective-permute-start | bytes 393224 | tf_op jit(solution)/shard_map/ppermute | solution.py:377
  5.5 12.0 %collective-permute-start.3 = (bf16[512,128]{1,0:T(8,128)(2,1)}, bf16[512,128]{1,0:T(8,128)(2,1)S(1)}, u32[]{:S(2)}, u32[]{:S(2)}) collective-permute-start(bf16[512,128]{1,0:T(8,128)(2,1)} %bitcast.20), channel_id=1, source_target_pairs={{0,4},{1,5},{2,6},{3,7},{4,0},{5,1},{6,2},{7,3},{8,12},{9,13},{10,... | collective-permute-start | bytes 393224 | tf_op jit(solution)/shard_map/ppermute | solution.py:377
  5.6 22.4 %collective-permute-start.1 = (bf16[512,128]{1,0:T(8,128)(2,1)}, bf16[512,128]{1,0:T(8,128)(2,1)S(1)}, u32[]{:S(2)}, u32[]{:S(2)}) collective-permute-start(bf16[512,128]{1,0:T(8,128)(2,1)} %bitcast.21), channel_id=1, source_target_pairs={{0,1},{1,0},{2,3},{3,2},{4,5},{5,4},{6,7},{7,6},{8,9},{9,8},{10,11... | collective-permute-start | bytes 393224 | tf_op jit(solution)/shard_map/ppermute | solution.py:377
  7.1 50.2 %collective-permute-start.15 = (bf16[512,1024]{1,0:T(8,128)(2,1)}, bf16[512,1024]{1,0:T(8,128)(2,1)S(1)}, u32[]{:S(2)}, u32[]{:S(2)}) collective-permute-start(bf16[512,1024]{1,0:T(8,128)(2,1)} %bitcast.14), channel_id=1, source_target_pairs={{0,8},{8,0},{1,9},{9,1},{2,10},{10,2},{3,11},{11,3},{4,12},{12,4},... | collective-permute-start | bytes 3145736 | tf_op jit(solution)/shard_map/ppermute | solution.py:380
  7.8 69.3 %collective-permute-start = (bf16[512,1024]{1,0:T(8,128)(2,1)}, bf16[512,1024]{1,0:T(8,128)(2,1)S(1)}, u32[]{:S(2)}, u32[]{:S(2)}) collective-permute-start(bf16[512,1024]{1,0:T(8,128)(2,1)} %bitcast.16), channel_id=1, source_target_pairs={{0,8},{8,0},{1,9},{9,1},{2,10},{10,2},{3,11},{11,3},{4,12},{12,4},... | collective-permute-start | bytes 3145736 | tf_op jit(solution)/shard_map/ppermute | solution.py:380
  17.5 6.1 %collective-permute-start.6 = (bf16[512,128]{1,0:T(8,128)(2,1)S(1)}, bf16[512,128]{1,0:T(8,128)(2,1)S(1)}, u32[]{:S(2)}, u32[]{:S(2)}) collective-permute-start(bf16[512,128]{1,0:T(8,128)(2,1)S(1)} %collective-permute-done.3.refs_0_), channel_id=1, source_target_pairs={{0,1},{1,0},{2,3},{3,2},{4,5},{5,4},{6,7},{7,6},{8,9},{9,8},{10,11... | collective-permute-start | bytes 393224 | tf_op jit(solution)/shard_map/ppermute | solution.py:377
  19.9 17.0 %collective-permute-start.12 = (bf16[512,128]{1,0:T(8,128)(2,1)S(1)}, bf16[512,128]{1,0:T(8,128)(2,1)S(1)}, u32[]{:S(2)}, u32[]{:S(2)}) collective-permute-start(bf16[512,128]{1,0:T(8,128)(2,1)S(1)} %collective-permute-done.5.refs_2_), channel_id=1, source_target_pairs={{0,1},{1,0},{2,3},{3,2},{4,5},{5,4},{6,7},{7,6},{8,9},{9,8},{10,11... | collective-permute-start | bytes 393224 | tf_op jit(solution)/shard_map/ppermute | solution.py:377
  23.6 9.1 %collective-permute-start.9 = (bf16[512,128]{1,0:T(8,128)(2,1)S(1)}, bf16[512,128]{1,0:T(8,128)(2,1)S(1)}, u32[]{:S(2)}, u32[]{:S(2)}) collective-permute-start(bf16[512,128]{1,0:T(8,128)(2,1)S(1)} %collective-permute-done.4.refs_1_), channel_id=1, source_target_pairs={{0,1},{1,0},{2,3},{3,2},{4,5},{5,4},{6,7},{7,6},{8,9},{9,8},{10,11... | collective-permute-start | bytes 393224 | tf_op jit(solution)/shard_map/ppermute | solution.py:377
  28.0 11.8 %collective-permute-start.7 = (bf16[528,128]{1,0:T(8,128)(2,1)S(1)}, bf16[528,128]{1,0:T(8,128)(2,1)S(1)}, u32[]{:S(2)}, u32[]{:S(2)}) collective-permute-start(bf16[528,128]{1,0:T(8,128)(2,1)S(1)} %shard_map.103), channel_id=1, source_target_pairs={{0,1},{1,0},{2,3},{3,2},{4,5},{5,4},{6,7},{7,6},{8,9},{9,8},{10,11... | collective-permute-start | bytes 405512 | tf_op jit(solution)/shard_map/ppermute | solution.py:377
  32.7 17.8 %collective-permute-start.2 = (bf16[528,128]{1,0:T(8,128)(2,1)S(1)}, bf16[528,128]{1,0:T(8,128)(2,1)S(1)}, u32[]{:S(2)}, u32[]{:S(2)}) collective-permute-start(bf16[528,128]{1,0:T(8,128)(2,1)S(1)} %get-tuple-element.21), channel_id=1, source_target_pairs={{0,1},{1,0},{2,3},{3,2},{4,5},{5,4},{6,7},{7,6},{8,9},{9,8},{10,11... | collective-permute-start | bytes 405512 | tf_op jit(solution)/shard_map/ppermute | solution.py:377
  36.9 10.3 %collective-permute-start.10 = (bf16[528,128]{1,0:T(8,128)(2,1)S(1)}, bf16[528,128]{1,0:T(8,128)(2,1)S(1)}, u32[]{:S(2)}, u32[]{:S(2)}) collective-permute-start(bf16[528,128]{1,0:T(8,128)(2,1)S(1)} %shard_map.105), channel_id=1, source_target_pairs={{0,1},{1,0},{2,3},{3,2},{4,5},{5,4},{6,7},{7,6},{8,9},{9,8},{10,11... | collective-permute-start | bytes 405512 | tf_op jit(solution)/shard_map/ppermute | solution.py:377
  39.8 7.8 %collective-permute-start.13 = (bf16[528,128]{1,0:T(8,128)(2,1)S(1)}, bf16[528,128]{1,0:T(8,128)(2,1)S(1)}, u32[]{:S(2)}, u32[]{:S(2)}) collective-permute-start(bf16[528,128]{1,0:T(8,128)(2,1)S(1)} %shard_map.107), channel_id=1, source_target_pairs={{0,1},{1,0},{2,3},{3,2},{4,5},{5,4},{6,7},{7,6},{8,9},{9,8},{10,11... | collective-permute-start | bytes 405512 | tf_op jit(solution)/shard_map/ppermute | solution.py:377
  47.2 8.9 %collective-permute-start.8 = (bf16[528,128]{1,0:T(8,128)(2,1)S(1)}, bf16[528,128]{1,0:T(8,128)(2,1)S(1)}, u32[]{:S(2)}, u32[]{:S(2)}) collective-permute-start(bf16[528,128]{1,0:T(8,128)(2,1)S(1)} %shard_map.104), channel_id=1, source_target_pairs={{0,4},{1,5},{2,6},{3,7},{4,0},{5,1},{6,2},{7,3},{8,12},{9,13},{10,... | collective-permute-start | bytes 405512 | tf_op jit(solution)/shard_map/ppermute | solution.py:377
  47.6 8.5 %collective-permute-start.11 = (bf16[528,128]{1,0:T(8,128)(2,1)S(1)}, bf16[528,128]{1,0:T(8,128)(2,1)S(1)}, u32[]{:S(2)}, u32[]{:S(2)}) collective-permute-start(bf16[528,128]{1,0:T(8,128)(2,1)S(1)} %shard_map.106), channel_id=1, source_target_pairs={{0,6},{1,7},{2,4},{3,5},{4,2},{5,3},{6,0},{7,1},{8,14},{9,15},{10,... | collective-permute-start | bytes 405512 | tf_op jit(solution)/shard_map/ppermute | solution.py:377
  50.5 6.8 %collective-permute-start.14 = (bf16[528,128]{1,0:T(8,128)(2,1)S(1)}, bf16[528,128]{1,0:T(8,128)(2,1)S(1)}, u32[]{:S(2)}, u32[]{:S(2)}) collective-permute-start(bf16[528,128]{1,0:T(8,128)(2,1)S(1)} %shard_map.108), channel_id=1, source_target_pairs={{0,2},{1,3},{2,0},{3,1},{4,6},{5,7},{6,4},{7,5},{8,10},{9,11},{10,... | collective-permute-start | bytes 405512 | tf_op jit(solution)/shard_map/ppermute | solution.py:377
  63.3 19.9 %copy-start.1 = (bf16[8,64,1024]{2,1,0:T(8,128)(2,1)S(1)}, bf16[8,64,1024]{2,1,0:T(8,128)(2,1)}, u32[]{:S(2)}) copy-start(bf16[8,64,1024]{2,1,0:T(8,128)(2,1)} %param.18) | copy-start | bytes 3145732
  63.3 10.5 %collective-permute-start.16 = (bf16[64,1152]{1,0:T(8,128)(2,1)S(1)}, bf16[64,1152]{1,0:T(8,128)(2,1)S(1)}, u32[]{:S(2)}, u32[]{:S(2)}) collective-permute-start(bf16[64,1152]{1,0:T(8,128)(2,1)S(1)} %get-tuple-element.28), channel_id=1, source_target_pairs={{0,1},{1,0},{2,3},{3,2},{4,5},{5,4},{6,7},{7,6},{8,9},{9,8},{10,11... | collective-permute-start | bytes 442376 | tf_op jit(solution)/shard_map/ppermute | solution.py:377
  63.8 8.2 %collective-permute-start.18 = (bf16[64,1152]{1,0:T(8,128)(2,1)S(1)}, bf16[64,1152]{1,0:T(8,128)(2,1)S(1)}, u32[]{:S(2)}, u32[]{:S(2)}) collective-permute-start(bf16[64,1152]{1,0:T(8,128)(2,1)S(1)} %get-tuple-element.30), channel_id=1, source_target_pairs={{0,1},{1,0},{2,3},{3,2},{4,5},{5,4},{6,7},{7,6},{8,9},{9,8},{10,11... | collective-permute-start | bytes 442376 | tf_op jit(solution)/shard_map/ppermute | solution.py:377
  65.4 10.1 %collective-permute-start.20 = (bf16[64,1152]{1,0:T(8,128)(2,1)S(1)}, bf16[64,1152]{1,0:T(8,128)(2,1)S(1)}, u32[]{:S(2)}, u32[]{:S(2)}) collective-permute-start(bf16[64,1152]{1,0:T(8,128)(2,1)S(1)} %get-tuple-element.32), channel_id=1, source_target_pairs={{0,1},{1,0},{2,3},{3,2},{4,5},{5,4},{6,7},{7,6},{8,9},{9,8},{10,11... | collective-permute-start | bytes 442376 | tf_op jit(solution)/shard_map/ppermute | solution.py:377
  65.9 11.1 %collective-permute-start.22 = (bf16[64,1152]{1,0:T(8,128)(2,1)S(1)}, bf16[64,1152]{1,0:T(8,128)(2,1)S(1)}, u32[]{:S(2)}, u32[]{:S(2)}) collective-permute-start(bf16[64,1152]{1,0:T(8,128)(2,1)S(1)} %get-tuple-element.34), channel_id=1, source_target_pairs={{0,1},{1,0},{2,3},{3,2},{4,5},{5,4},{6,7},{7,6},{8,9},{9,8},{10,11... | collective-permute-start | bytes 442376 | tf_op jit(solution)/shard_map/ppermute | solution.py:377
  72.1 7.1 %collective-permute-start.19 = (bf16[64,1152]{1,0:T(8,128)(2,1)S(1)}, bf16[64,1152]{1,0:T(8,128)(2,1)S(1)}, u32[]{:S(2)}, u32[]{:S(2)}) collective-permute-start(bf16[64,1152]{1,0:T(8,128)(2,1)S(1)} %shard_map.112), channel_id=1, source_target_pairs={{0,6},{1,7},{2,4},{3,5},{4,2},{5,3},{6,0},{7,1},{8,14},{9,15},{10,... | collective-permute-start | bytes 442376 | tf_op jit(solution)/shard_map/ppermute | solution.py:377
  73.9 9.3 %collective-permute-start.17 = (bf16[64,1152]{1,0:T(8,128)(2,1)S(1)}, bf16[64,1152]{1,0:T(8,128)(2,1)S(1)}, u32[]{:S(2)}, u32[]{:S(2)}) collective-permute-start(bf16[64,1152]{1,0:T(8,128)(2,1)S(1)} %shard_map.111), channel_id=1, source_target_pairs={{0,4},{1,5},{2,6},{3,7},{4,0},{5,1},{6,2},{7,3},{8,12},{9,13},{10,... | collective-permute-start | bytes 442376 | tf_op jit(solution)/shard_map/ppermute | solution.py:377
  75.6 7.6 %collective-permute-start.21 = (bf16[64,1152]{1,0:T(8,128)(2,1)S(1)}, bf16[64,1152]{1,0:T(8,128)(2,1)S(1)}, u32[]{:S(2)}, u32[]{:S(2)}) collective-permute-start(bf16[64,1152]{1,0:T(8,128)(2,1)S(1)} %shard_map.113), channel_id=1, source_target_pairs={{0,2},{1,3},{2,0},{3,1},{4,6},{5,7},{6,4},{7,5},{8,10},{9,11},{10,... | collective-permute-start | bytes 442376 | tf_op jit(solution)/shard_map/ppermute | solution.py:377
  (4 other events, 38.9 us)

commit v3 on v2

--- a/solution.py
+++ b/solution.py
@@ -13,7 +13,19 @@
 LANES = 128
 TILE = 16
 SMALL = 8 * 1024 * 1024
-LARGE = 32 * 1024 * 1024
+LARGE = 16 * 1024 * 1024
+
+
+PLAN = [
+    ("send", 4, 2, 1),
+    ("attend", 0),
+    ("forward", 5, 6, 3),
+    ("attend", 1, 2, 4),
+    ("forward", 7),
+    ("attend", 3, 5),
+    ("attend", 7),
+    ("attend", 6),
+]
 
 
 def call(body, grid, in_specs, out_shape, out_specs, scratch=(), prefetch=1, cost=None):
@@ -45,14 +57,19 @@
     return lax.broadcasted_iota(jnp.int32, shape, dim)
 
 
-def attend_part(heads, scale, q, live, keys, values, first_tile, o_ref):
+def attend_part(heads, scale, q, lengths, keys, values, first_tile, o_ref):
     rows, positions = keys.shape[0], keys.shape[1]
     per_tile = TILE // heads
     tiles = rows // per_tile
     row = iota((TILE, LANES), 0) // heads
     lane = iota((TILE, LANES), 1)
-    scores = []
+    owner = iota((TILE, positions), 0) // heads
+    scores, live = [], []
     for g in range(tiles):
+        bound = jnp.zeros((TILE, positions), jnp.int32)
+        for a in range(per_tile):
+            bound = jnp.where(owner == a, lengths[(first_tile + g) * per_tile + a], bound)
+        live.append(bound)
         left = q[g * TILE : (g + 1) * TILE, :]
         zero = jnp.zeros_like(left)
         left = jnp.concatenate([jnp.where(row == a, left, zero) for a in range(per_tile)], axis=1)
@@ -61,7 +78,7 @@
             lax.dot_general(left, right, (((1,), (1,)), ((), ())), preferred_element_type=F32)
         )
     s = jnp.concatenate(scores, axis=0) * scale
-    alive = iota(s.shape, 1) < live[:, :positions]
+    alive = iota(s.shape, 1) < jnp.concatenate(live, axis=0)
     s = jnp.where(alive, s, DEAD)
     high, mid = split2(jnp.max(s, axis=1, keepdims=True))
     p = jnp.where(alive, jnp.exp(s - (high + mid)), 0.0)
@@ -82,13 +99,16 @@
     return stat
 
 
-def attend_body(n, blocks, heads, scale, sc_ref, live_ref, k_hbm, v_hbm, *refs):
-    q_refs, o_refs = refs[:n], refs[n : 2 * n]
-    k_buf, v_buf, k_sem, v_sem = refs[2 * n :]
+def attend_body(n, blocks, heads, scale, sc_ref, len_ref, k_hbm, v_hbm, *refs):
+    q_refs = refs[:n]
+    o_refs = refs[-6 - n : -6]
+    q_buf, k_buf, v_buf, q_sem, k_sem, v_sem = refs[-6:]
     size = k_hbm.shape[0] // blocks
-    copies = []
+    many = size * heads
+    first, copies = [], []
     for j in range(n):
         kv = sc_ref[j]
+        first.append(pltpu.make_async_copy(q_refs[j], q_buf.at[j], q_sem.at[j]))
         for b in range(blocks):
             at, i = pl.ds(b * size, size), j * blocks + b
             copies.append(
@@ -97,44 +117,76 @@
                     pltpu.make_async_copy(v_hbm.at[at, kv], v_buf.at[i], v_sem.at[i]),
                 )
             )
+    for c in first:
+        c.start()
     for ck, cv in copies:
         ck.start()
         cv.start()
-    many = size * heads
+    for c in first:
+        c.wait()
     for j in range(n):
         stat = jnp.zeros((TILE, LANES), F32)
         for b in range(blocks):
             i = j * blocks + b
             copies[i][0].wait()
             copies[i][1].wait()
-            at = slice(b * many, (b + 1) * many)
             stat = stat + attend_part(
-                heads, scale, q_refs[j][at, :], live_ref[at, :], k_buf.at[i], v_buf.at[i],
+                heads, scale, q_buf[j, b * many : (b + 1) * many, :], len_ref, k_buf.at[i], v_buf.at[i],
                 b * many // TILE, o_refs[j],
             )
         o_refs[j][many * blocks :, :] = stat.astype(BF16)
 
 
-def attend(which, queries, live, keys, values, heads, scale):
+def attend(which, queries, live, keys, values, heads, scale, after):
     n, blocks = len(queries), 2
     rows, _, positions, width = keys.shape
     vmem = pl.BlockSpec(memory_space=pltpu.VMEM)
+    smem = pl.BlockSpec(memory_space=pltpu.SMEM)
     hbm = pl.BlockSpec(memory_space=pltpu.HBM)
+    anywhere = pl.BlockSpec(memory_space=pl.ANY)
     buf = pltpu.VMEM((n * blocks, rows // blocks, positions, width), BF16)
     sem = pltpu.SemaphoreType.DMA((n * blocks,))
     return pl.pallas_call(
         functools.partial(attend_body, n, blocks, heads, scale),
-        in_specs=[pl.BlockSpec(memory_space=pltpu.SMEM), vmem, hbm, hbm] + [vmem] * n,
+        in_specs=[smem, smem, hbm, hbm] + [anywhere] * (n + len(after)),
         out_specs=[vmem] * n,
         out_shape=[jax.ShapeDtypeStruct((rows * heads + TILE, width), BF16)] * n,
-        scratch_shapes=[buf, buf, sem, sem],
+        scratch_shapes=[
+            pltpu.VMEM((n, rows * heads, width), BF16), buf, buf, pltpu.SemaphoreType.DMA((n,)), sem, sem
+        ],
         compiler_params=pltpu.CompilerParams(vmem_limit_bytes=LARGE),
         cost_estimate=pl.CostEstimate(
             flops=32 * n * rows * heads * positions * width,
             bytes_accessed=4 * n * rows * positions * width,
             transcendentals=n * rows * heads * positions,
         ),
-    )(which, live, keys, values, *queries)
+    )(which, live, keys, values, *queries, *after)
+
+
+def load_body(blocks, source, *refs):
+    target, sem = refs[-2:]
+    size = source.shape[0] // blocks
+    copies = [
+        pltpu.make_async_copy(source.at[pl.ds(b * size, size)], target.at[pl.ds(b * size, size)], sem.at[b])
+        for b in range(blocks)
+    ]
+    for c in copies:
+        c.start()
+    for c in copies:
+        c.wait()
+
+
+def load(array, after):
+    blocks = 4
+    return pl.pallas_call(
+        functools.partial(load_body, blocks),
+        in_specs=[pl.BlockSpec(memory_space=pltpu.HBM)] + [pl.BlockSpec(memory_space=pl.ANY)] * len(after),
+        out_specs=pl.BlockSpec(memory_space=pltpu.VMEM),
+        out_shape=pltpu.VMEM(array.shape, array.dtype),
+        scratch_shapes=[pltpu.SemaphoreType.DMA((blocks,))],
+        compiler_params=pltpu.CompilerParams(vmem_limit_bytes=SMALL),
+        cost_estimate=pl.CostEstimate(flops=0, bytes_accessed=2 * array.size, transcendentals=0),
+    )(array, *after)
 
 
 def combine(stats):
@@ -202,22 +254,11 @@
     return total
 
 
-def fetch(scalars, first, w_ref, buf, sem):
-    cols = buf.shape[2]
-    copies = []
-    for k in range(buf.shape[0]):
-        at = pl.ds(pl.multiple_of(scalars[first + k] * cols, cols), cols)
-        copies.append(pltpu.make_async_copy(w_ref.at[:, at], buf.at[k], sem.at[k]))
-        copies[-1].start()
-    return copies
-
-
-def project_body(n_parts, n_out, heads, rank, sc_ref, w_ref, *refs):
+def project_body(n_parts, n_out, heads, rank, sc_ref, *refs):
     parts = refs[:n_parts]
-    slot_ref, down_a, down_b = refs[n_parts : n_parts + 3]
-    outs = refs[n_parts + 3 : n_parts + 3 + n_out]
-    att_ref, shrink_ref, att32, buf, sem = refs[n_parts + 3 + n_out :]
-    copies = fetch(sc_ref, 1, w_ref, buf, sem)
+    w_ref, slot_ref, down_a, down_b = refs[n_parts : n_parts + 4]
+    outs = refs[n_parts + 4 : n_parts + 4 + n_out]
+    att_ref, att32 = refs[n_parts + 4 + n_out :]
     finish_attention(parts, att32, att_ref, heads)
     att = att_ref[...]
     over = (((1,), (1,)), ((), ()))
@@ -229,13 +270,12 @@
     s = chosen(slots - mine * per, own, rank) + chosen(slots - (1 - mine) * per, other, rank)
     s = s + pltpu.roll(s, rank, 1)
     high, mid = split2(s)
-    shrink = jnp.where(iota(s.shape, 1) < rank, high, mid).astype(BF16)
-    shrink_ref[...] = shrink
+    shrink = jnp.where(iota(s.shape, 1) < rank, high, mid)
     for k, out in enumerate(outs):
-        cols = buf.shape[2]
-        copies[k].wait()
-        out[:, :cols] = jnp.dot(att, buf[k], preferred_element_type=F32).astype(BF16)
-        out[:, cols:] = shrink
+        cols = out.shape[1] - LANES
+        at = pl.ds(pl.multiple_of(sc_ref[1 + k] * cols, cols), cols)
+        out[:, :cols] = jnp.dot(att, w_ref[:, at], preferred_element_type=F32).astype(out.dtype)
+        out[:, cols:] = shrink.astype(out.dtype)
 
 
 def project(scalars, parts, weight, slots, down_a, down_b, heads, rank, cols):
@@ -243,52 +283,20 @@
     rows = slots.shape[0]
     width = weight.shape[0]
     vmem = pl.BlockSpec(memory_space=pltpu.VMEM)
-    outs = pl.pallas_call(
+    return pl.pallas_call(
         functools.partial(project_body, len(parts), n_out, heads, rank),
-        in_specs=[pl.BlockSpec(memory_space=pltpu.SMEM), pl.BlockSpec(memory_space=pltpu.HBM)]
-        + [vmem] * (len(parts) + 3),
-        out_specs=[vmem] * (n_out + 2),
-        out_shape=[jax.ShapeDtypeStruct((rows, cols + LANES), BF16)] * n_out
-        + [jax.ShapeDtypeStruct((rows, width), BF16), jax.ShapeDtypeStruct((rows, LANES), BF16)],
-        scratch_shapes=[
-            pltpu.VMEM((rows * heads, LANES), F32),
-            pltpu.VMEM((n_out, width, cols), BF16),
-            pltpu.SemaphoreType.DMA((n_out,)),
+        in_specs=[pl.BlockSpec(memory_space=pltpu.SMEM)] + [vmem] * (len(parts) + 4),
+        out_specs=[vmem] * n_out,
+        out_shape=[
+            jax.ShapeDtypeStruct((rows, cols + LANES), BF16 if k < n_out // 2 else F32)
+            for k in range(n_out)
         ],
-        compiler_params=pltpu.CompilerParams(vmem_limit_bytes=LARGE),
+        scratch_shapes=[pltpu.VMEM((rows, width), BF16), pltpu.VMEM((rows * heads, LANES), F32)],
+        compiler_params=pltpu.CompilerParams(vmem_limit_bytes=SMALL),
         cost_estimate=pl.CostEstimate(
             flops=2 * rows * width * cols * n_out, bytes_accessed=2 * width * cols * n_out, transcendentals=0
         ),
-    )(scalars, weight, *parts, slots, down_a, down_b)
-    return outs[:n_out], outs[n_out], outs[n_out + 1]
-
-
-def project_more_body(n_out, sc_ref, w_ref, att_ref, shrink_ref, *refs):
-    outs = refs[:n_out]
-    buf, sem = refs[n_out:]
-    copies = fetch(sc_ref, 1, w_ref, buf, sem)
-    cols = buf.shape[2]
-    for k, out in enumerate(outs):
-        copies[k].wait()
-        out[:, :cols] = jnp.dot(att_ref[...], buf[k], preferred_element_type=F32)
-        out[:, cols:] = shrink_ref[...].astype(F32)
-
-
-def project_more(scalars, att, shrink, weight, cols):
-    n_out = scalars.shape[0] - 1
-    rows, width = att.shape
-    vmem = pl.BlockSpec(memory_space=pltpu.VMEM)
-    return pl.pallas_call(
-        functools.partial(project_more_body, n_out),
-        in_specs=[pl.BlockSpec(memory_space=pltpu.SMEM), pl.BlockSpec(memory_space=pltpu.HBM), vmem, vmem],
-        out_specs=[vmem] * n_out,
-        out_shape=[jax.ShapeDtypeStruct((rows, cols + LANES), F32)] * n_out,
-        scratch_shapes=[pltpu.VMEM((n_out, width, cols), BF16), pltpu.SemaphoreType.DMA((n_out,))],
-        compiler_params=pltpu.CompilerParams(vmem_limit_bytes=LARGE),
-        cost_estimate=pl.CostEstimate(
-            flops=2 * rows * width * cols * n_out, bytes_accessed=2 * width * cols * n_out, transcendentals=0
-        ),
-    )(scalars, weight, att, shrink)
+    )(scalars, *parts, weight, slots, down_a, down_b)
 
 
 def shrink_sum(parts, rank):
@@ -382,34 +390,31 @@
     far = sorted(range(2, tensor, 2), key=lambda k: -min(k, 4))
     outer = far + [0]
 
-    q = queries.reshape(rows * heads, width)
-    held = {0: q}
-    held[1] = hop(q, 1)
-    for k in far:
-        held[k] = hop(q, k)
-    for k in far:
-        held[k ^ 1] = hop(held[k], 1)
-
     down_a = jnp.swapaxes(adapter_down_weight, 1, 2).reshape(slots_here * rank, -1)
     up_a = adapter_up_weight.reshape(slots_here * rank, cols)
     down_b, up_b = across(down_a), across(up_a)
 
-    live = jnp.clip(cache_live_length - me * positions, 0, positions)
-    live = jnp.broadcast_to(jnp.repeat(live, heads)[:, None], (rows * heads, LANES)).astype(jnp.int32)
+    live = jnp.clip(cache_live_length - me * positions, 0, positions).astype(jnp.int32)
     scale = 1.0 / math.sqrt(width)
     keys, values, weight = (
         pltpu.with_memory_space_constraint(x, pltpu.HBM)
         for x in (cached_key_rows, cached_value_rows, output_weight)
     )
 
-    def attended(*ks):
-        which = jnp.stack([lax.div((me ^ k) * heads, group) for k in ks]).astype(jnp.int32)
-        return attend(which, [held[k] for k in ks], live, keys, values, heads, scale)
-
-    partial = dict(zip([1, 0], attended(1, 0)))
-    partial.update(zip(far, attended(*far)))
-    for k in far:
-        (partial[k ^ 1],) = attended(k ^ 1)
+    held, partial, token = {0: queries.reshape(rows * heads, width)}, {}, ()
+    for kind, *ks in PLAN + [(kind, k) for k in range(8, tensor) for kind in ("forward", "attend")]:
+        if kind == "attend":
+            which = jnp.stack([lax.div((me ^ k) * heads, group) for k in ks]).astype(jnp.int32)
+            outs = attend(which, [held[k] for k in ks], live, keys, values, heads, scale, token)
+            partial.update(zip(ks, outs))
+            token = [outs[0]]
+            continue
+        for k in ks:
+            bit = 2 if k & 3 == 3 and k > 3 else k & -k
+            source = held[k ^ bit]
+            if kind == "forward" and token:
+                source, token[0] = lax.optimization_barrier((source, token[0]))
+            held[k] = hop(source, bit)
     sent = {k: hop(partial[k ^ 1], 1) for k in [0] + far}
     merged = {k: pair(partial[k], sent[k]) for k in [0] + far}
     parts = [merged[0]] + [hop(merged[k], k) for k in far]
@@ -420,11 +425,11 @@
     slots = jnp.broadcast_to(slot[:, None], (rows, LANES)).astype(jnp.int32)
 
     order = jnp.array([k for k in outer], jnp.int32)
-    to_pair = jnp.concatenate([mine[None], me ^ order ^ 1]).astype(jnp.int32)
-    to_own = jnp.concatenate([mine[None], me ^ order]).astype(jnp.int32)
-    first, att, shrink = project(to_pair, parts, weight, slots, down_a, down_b, heads, rank, cols)
+    scalars = jnp.concatenate([mine[None], me ^ order ^ 1, me ^ order]).astype(jnp.int32)
+    weight = load(weight, [merged[k] for k in far])
+    outs = project(scalars, parts, weight, slots, down_a, down_b, heads, rank, cols)
+    first, own = outs[: len(outer)], outs[len(outer) :]
     arrived = [hop(x, 1) for x in first]
-    own = project_more(to_own, att, shrink, weight, cols)
     summed = [add(a, b, rank) for a, b in zip(own, arrived)]
     final = [hop(x, k) if k else x for x, k in zip(summed, outer)]
     return last(mine[None].astype(jnp.int32), slots, up_a, up_b, final, rank)

time: 84.5 us -> 77.9 us (0.922)
  waiting for transfers between devices: 23.7 us -> 9.99 us
  Pallas kernels: 30.3 us -> 33.8 us
  starting transfers between devices: 28 us -> 31.1 us
  local copies, waits for them, and re-layouts: 0.38 us -> 1.65 us
    ppermute x21, waiting for transfers between devices: 23.7 us -> 9.99 us  [hop(): return lax.ppermute(x, 'tensor', [(i, i ^ k) for i in range(tensor)])]
    pallas_call x5, Pallas kernels: 16.9 us -> 20.1 us  [attend(): pl.pallas_call(functools.partial(attend_body, n, blocks, heads, scale), i...]
    ppermute x21, starting transfers between devices: 27.5 us -> 30.6 us  [hop(): return lax.ppermute(x, 'tensor', [(i, i ^ k) for i in range(tensor)])]
    unnamed x10 -> x16, local copies, waits for them, and re-layouts: 0.02 us -> 1.58 us
    pallas_call x1, Pallas kernels: 4.55 us -> 5.96 us  [load(): pl.pallas_call(functools.partial(load_body, blocks), in_specs=[pl.BlockSp...]
    pallas_call x1, Pallas kernels: 5.83 us -> 4.76 us  [project(): pl.pallas_call(functools.partial(project_body, len(parts), n_out, heads,...]
  transfers between devices with their start and end apart: 23 -> 23, of which waited for: 6 -> 5; matrix products, arithmetic and copies ran while one was open for 2% -> 1% of each run, Pallas kernels for 34% -> 42%
where the time goes in v3:
time: 77.9 us; the launch traced here: 77.8 us
  Pallas kernels  33.8 us (43%)
  starting transfers between devices  31.1 us (40%)
  waiting for transfers between devices  9.99 us (13%)
  local copies, waits for them, and re-layouts  1.65 us (2%)
  other arithmetic  0.98 us (1%)
    ppermute x21, starting transfers between devices, hop(): return lax.ppermute(x, 'tensor', [(i, i ^ k) for i in range(tensor)])  30.6 us
    pallas_call x5, Pallas kernels, attend(): pl.pallas_call(functools.partial(attend_body, n, blocks, heads, scale), i...  20.1 us
    ppermute x21, waiting for transfers between devices, hop(): return lax.ppermute(x, 'tensor', [(i, i ^ k) for i in range(tensor)])  9.99 us
    pallas_call x1, Pallas kernels, load(): pl.pallas_call(functools.partial(load_body, blocks), in_specs=[pl.BlockSp...  5.96 us
    pallas_call x1, Pallas kernels, project(): pl.pallas_call(functools.partial(project_body, len(parts), n_out, heads,...  4.76 us
    unnamed x16, local copies, waits for them, and re-layouts  1.58 us
  transfers between devices with their start and end apart: 23, of which 5 were waited for; matrix products, arithmetic and copies ran while one was open for 1% of the time, Pallas kernels for 42%

profile of v3, /device:TPU:0, one launch (start us, length us, event | category | flops | bytes accessed | tf_op | source)
XLA Modules:
  0.0 77.8 jit_solution(17867261552799443061)
XLA Ops:
  0.0 4.0 %collective-permute-start.3 = (bf16[512,128]{1,0:T(8,128)(2,1)}, bf16[512,128]{1,0:T(8,128)(2,1)S(1)}, u32[]{:S(2)}, u32[]{:S(2)}) collective-permute-start(bf16[512,128]{1,0:T(8,128)(2,1)} %bitcast.18), channel_id=1, source_target_pairs={{0,4},{1,5},{2,6},{3,7},{4,0},{5,1},{6,2},{7,3},{8,12},{9,13},{10,... | collective-permute-start | bytes 393224 | tf_op jit(solution)/shard_map/ppermute | solution.py:385
  4.0 1.6 %collective-permute-start.2 = (bf16[512,128]{1,0:T(8,128)(2,1)}, bf16[512,128]{1,0:T(8,128)(2,1)S(1)}, u32[]{:S(2)}, u32[]{:S(2)}) collective-permute-start(bf16[512,128]{1,0:T(8,128)(2,1)} %bitcast.19), channel_id=1, source_target_pairs={{0,2},{1,3},{2,0},{3,1},{4,6},{5,7},{6,4},{7,5},{8,10},{9,11},{10,... | collective-permute-start | bytes 393224 | tf_op jit(solution)/shard_map/ppermute | solution.py:385
  5.6 1.5 %collective-permute-start.1 = (bf16[512,128]{1,0:T(8,128)(2,1)}, bf16[512,128]{1,0:T(8,128)(2,1)S(1)}, u32[]{:S(2)}, u32[]{:S(2)}) collective-permute-start(bf16[512,128]{1,0:T(8,128)(2,1)} %bitcast.20), channel_id=1, source_target_pairs={{0,1},{1,0},{2,3},{3,2},{4,5},{5,4},{6,7},{7,6},{8,9},{9,8},{10,11... | collective-permute-start | bytes 393224 | tf_op jit(solution)/shard_map/ppermute | solution.py:385
  9.3 3.2 %shard_map.100.refs_3_.a_ref = bf16[528,128]{1,0:T(8,128)(2,1)S(1)} custom-call(s32[1]{0:T(128)} %bitcast.2.sc_ref, s32[64]{0:T(128)S(1)} %subtract_clamp_fusion.len_ref, bf16[64,8,96,128]{3,2,1,0:T(8,128)(2,1)} %k_hbm.9, bf16[64,8,96,128]{3,2,1,0:T(8,128)(2,1)} %v_hbm.9, bf16[512,128]{1,0:T(8,128)(2,1)S(1)} %bitcast.21), custom_call_target="tpu_custom_call" | custom-call | flops 201326592 | bytes 3145728 | tf_op jit(solution)/shard_map/pallas_call | solution.py:149
  13.2 1.4 %collective-permute-start.5 = (bf16[512,128]{1,0:T(8,128)(2,1)S(1)}, bf16[512,128]{1,0:T(8,128)(2,1)S(1)}, u32[]{:S(2)}, u32[]{:S(2)}) collective-permute-start(bf16[512,128]{1,0:T(8,128)(2,1)S(1)} %collective-permute-done.2.refs_1_), channel_id=1, source_target_pairs={{0,1},{1,0},{2,3},{3,2},{4,5},{5,4},{6,7},{7,6},{8,9},{9,8},{10,11... | collective-permute-start | bytes 393224 | tf_op jit(solution)/shard_map/ppermute | solution.py:385
  14.7 5.9 %shard_map.101 = (bf16[528,128]{1,0:T(8,128)(2,1)S(1)}, bf16[528,128]{1,0:T(8,128)(2,1)S(1)}, bf16[528,128]{1,0:T(8,128)(2,1)S(1)}) custom-call(s32[3]{0:T(128)S(1)} %pad_add_fusion.1.sc_ref, s32[64]{0:T(128)S(1)} %subtract_clamp_fusion.len_ref, bf16[64,8,96,128]{3,2,1,0:T(8,128)(2,1)} %k_hbm.9, bf16[64,8,96,128]{3,2,1,0:T(8,128)(2,1)} %v_hbm.9, ...), custom_call_target="tpu_custom_call" | custom-call | flops 603979776 | bytes 9437184 | tf_op jit(solution)/shard_map/pallas_call | solution.py:149
  21.0 4.5 %shard_map.103 = (bf16[528,128]{1,0:T(8,128)(2,1)S(1)}, bf16[528,128]{1,0:T(8,128)(2,1)S(1)}) custom-call(s32[2]{0:T(128)S(1)} %pad_add_fusion.2.sc_ref, s32[64]{0:T(128)S(1)} %subtract_clamp_fusion.len_ref, bf16[64,8,96,128]{3,2,1,0:T(8,128)(2,1)} %k_hbm.9, bf16[64,8,96,128]{3,2,1,0:T(8,128)(2,1)} %v_hbm.9, ...), custom_call_target="tpu_custom_call" | custom-call | flops 402653184 | bytes 6291456 | tf_op jit(solution)/shard_map/pallas_call | solution.py:149
  26.9 1.4 %collective-permute-start.9 = (bf16[512,128]{1,0:T(8,128)(2,1)S(1)}, bf16[512,128]{1,0:T(8,128)(2,1)S(1)}, u32[]{:S(2)}, u32[]{:S(2)}) collective-permute-start(bf16[512,128]{1,0:T(8,128)(2,1)S(1)} %collective-permute-done.3.refs_2_), channel_id=1, source_target_pairs={{0,2},{1,3},{2,0},{3,1},{4,6},{5,7},{6,4},{7,5},{8,10},{9,11},{10,... | collective-permute-start | bytes 393224 | tf_op jit(solution)/shard_map/ppermute | solution.py:385
  28.3 1.6 %collective-permute-start.4 = (bf16[528,128]{1,0:T(8,128)(2,1)S(1)}, bf16[528,128]{1,0:T(8,128)(2,1)S(1)}, u32[]{:S(2)}, u32[]{:S(2)}) collective-permute-start(bf16[528,128]{1,0:T(8,128)(2,1)S(1)} %get-tuple-element.33.refs_2_), channel_id=1, source_target_pairs={{0,1},{1,0},{2,3},{3,2},{4,5},{5,4},{6,7},{7,6},{8,9},{9,8},{10,11... | collective-permute-start | bytes 405512 | tf_op jit(solution)/shard_map/ppermute | solution.py:385
  29.9 3.2 %shard_map.105.refs_1_ = bf16[528,128]{1,0:T(8,128)(2,1)S(1)} custom-call(s32[1]{0:T(128)} %bitcast.10.sc_ref, s32[64]{0:T(128)S(1)} %subtract_clamp_fusion.len_ref, bf16[64,8,96,128]{3,2,1,0:T(8,128)(2,1)} %k_hbm.9, bf16[64,8,96,128]{3,2,1,0:T(8,128)(2,1)} %v_hbm.9, bf16[512,128]{1,0:T(8,128)(2,1)S(1)} %collective-permute-done.10.refs_0_, ...), custom_call_target="tpu_custom_call" | custom-call | flops 201326592 | bytes 3145728 | tf_op jit(solution)/shard_map/pallas_call | solution.py:149
  33.6 1.6 %collective-permute-start.11 = (bf16[528,128]{1,0:T(8,128)(2,1)S(1)}, bf16[528,128]{1,0:T(8,128)(2,1)S(1)}, u32[]{:S(2)}, u32[]{:S(2)}) collective-permute-start(bf16[528,128]{1,0:T(8,128)(2,1)S(1)} %shard_map.105.refs_1_), channel_id=1, source_target_pairs={{0,1},{1,0},{2,3},{3,2},{4,5},{5,4},{6,7},{7,6},{8,9},{9,8},{10,11... | collective-permute-start | bytes 405512 | tf_op jit(solution)/shard_map/ppermute | solution.py:385
  35.3 3.4 %shard_map.106.a_ref = bf16[528,128]{1,0:T(8,128)(2,1)S(1)} custom-call(s32[1]{0:T(128)} %bitcast.9.sc_ref, s32[64]{0:T(128)S(1)} %subtract_clamp_fusion.len_ref, bf16[64,8,96,128]{3,2,1,0:T(8,128)(2,1)} %k_hbm.9, bf16[64,8,96,128]{3,2,1,0:T(8,128)(2,1)} %v_hbm.9, bf16[512,128]{1,0:T(8,128)(2,1)S(1)} %collective-permute-done.9.refs_0_, ...), custom_call_target="tpu_custom_call" | custom-call | flops 201326592 | bytes 3145728 | tf_op jit(solution)/shard_map/pallas_call | solution.py:149
  40.1 1.3 %collective-permute-start.8 = (bf16[528,128]{1,0:T(8,128)(2,1)S(1)}, bf16[528,128]{1,0:T(8,128)(2,1)S(1)}, u32[]{:S(2)}, u32[]{:S(2)}) collective-permute-start(bf16[528,128]{1,0:T(8,128)(2,1)S(1)} %shard_map.104.refs_0_), channel_id=1, source_target_pairs={{0,4},{1,5},{2,6},{3,7},{4,0},{5,1},{6,2},{7,3},{8,12},{9,13},{10,... | collective-permute-start | bytes 405512 | tf_op jit(solution)/shard_map/ppermute | solution.py:385
  41.8 2.5 %collective-permute-start.12 = (bf16[528,128]{1,0:T(8,128)(2,1)S(1)}, bf16[528,128]{1,0:T(8,128)(2,1)S(1)}, u32[]{:S(2)}, u32[]{:S(2)}) collective-permute-start(bf16[528,128]{1,0:T(8,128)(2,1)S(1)} %shard_map.107.refs_1_), channel_id=1, source_target_pairs={{0,6},{1,7},{2,4},{3,5},{4,2},{5,3},{6,0},{7,1},{8,14},{9,15},{10,... | collective-permute-start | bytes 405512 | tf_op jit(solution)/shard_map/ppermute | solution.py:385
  44.8 6.0 %shard_map.109.refs_4_ = bf16[1024,8192]{1,0:T(8,128)(2,1)S(1)} custom-call(bf16[1024,8192]{1,0:T(8,128)(2,1)} %source.1, bf16[528,128]{1,0:T(8,128)(2,1)S(1)} %shard_map.104.refs_0_, bf16[528,128]{1,0:T(8,128)(2,1)S(1)} %shard_map.107.refs_1_, bf16[528,128]{1,0:T(8,128)(2,1)S(1)} %shard_map.108.refs_2_), custom_call_target="tpu_custom_call" | custom-call | bytes 16777216 | tf_op jit(solution)/shard_map/pallas_call | solution.py:181
  51.1 4.8 %shard_map.110 = (bf16[64,1152]{1,0:T(8,128)(2,1)S(1)}, bf16[64,1152]{1,0:T(8,128)(2,1)S(1)}, bf16[64,1152]{1,0:T(8,128)(2,1)S(1)}, bf16[64,1152]{1,0:T(8,128)(2...) custom-call(s32[9]{0:T(128)S(1)} %pad_add_fusion.sc_ref, ...), custom_call_target="tpu_custom_call" | custom-call | flops 1073741824 | bytes 16777216 | tf_op jit(solution)/shard_map/pallas_call | solution.py:286
  55.8 1.3 %collective-permute-start.20 = (bf16[64,1152]{1,0:T(8,128)(2,1)S(1)}, bf16[64,1152]{1,0:T(8,128)(2,1)S(1)}, u32[]{:S(2)}, u32[]{:S(2)}) collective-permute-start(bf16[64,1152]{1,0:T(8,128)(2,1)S(1)} %get-tuple-element.44), channel_id=1, source_target_pairs={{0,1},{1,0},{2,3},{3,2},{4,5},{5,4},{6,7},{7,6},{8,9},{9,8},{10,11... | collective-permute-start | bytes 442376 | tf_op jit(solution)/shard_map/ppermute | solution.py:385
  57.9 1.2 %collective-permute-start.16 = (bf16[64,1152]{1,0:T(8,128)(2,1)S(1)}, bf16[64,1152]{1,0:T(8,128)(2,1)S(1)}, u32[]{:S(2)}, u32[]{:S(2)}) collective-permute-start(bf16[64,1152]{1,0:T(8,128)(2,1)S(1)} %get-tuple-element.40), channel_id=1, source_target_pairs={{0,1},{1,0},{2,3},{3,2},{4,5},{5,4},{6,7},{7,6},{8,9},{9,8},{10,11... | collective-permute-start | bytes 442376 | tf_op jit(solution)/shard_map/ppermute | solution.py:385
  59.9 2.7 %collective-permute-done.20.b_ref = bf16[64,1152]{1,0:T(8,128)(2,1)S(1)} collective-permute-done((bf16[64,1152]{1,0:T(8,128)(2,1)S(1)}, bf16[64,1152]{1,0:T(8,128)(2,1)S(1)}, u32[]{:S(2)}, u32[]{:S(2)}) %collective-permute-start.20) | collective-permute-done | bytes 147488 | tf_op jit(solution)/shard_map/ppermute | solution.py:385
  62.8 2.1 %collective-permute-start.21 = (bf16[64,1152]{1,0:T(8,128)(2,1)S(1)}, bf16[64,1152]{1,0:T(8,128)(2,1)S(1)}, u32[]{:S(2)}, u32[]{:S(2)}) collective-permute-start(bf16[64,1152]{1,0:T(8,128)(2,1)S(1)} %shard_map.113), channel_id=1, source_target_pairs={{0,2},{1,3},{2,0},{3,1},{4,6},{5,7},{6,4},{7,5},{8,10},{9,11},{10,... | collective-permute-start | bytes 442376 | tf_op jit(solution)/shard_map/ppermute | solution.py:385
  65.5 1.6 %collective-permute-start.19 = (bf16[64,1152]{1,0:T(8,128)(2,1)S(1)}, bf16[64,1152]{1,0:T(8,128)(2,1)S(1)}, u32[]{:S(2)}, u32[]{:S(2)}) collective-permute-start(bf16[64,1152]{1,0:T(8,128)(2,1)S(1)} %shard_map.112), channel_id=1, source_target_pairs={{0,6},{1,7},{2,4},{3,5},{4,2},{5,3},{6,0},{7,1},{8,14},{9,15},{10,... | collective-permute-start | bytes 442376 | tf_op jit(solution)/shard_map/ppermute | solution.py:385
  67.2 2.8 %collective-permute-start.17 = (bf16[64,1152]{1,0:T(8,128)(2,1)S(1)}, bf16[64,1152]{1,0:T(8,128)(2,1)S(1)}, u32[]{:S(2)}, u32[]{:S(2)}) collective-permute-start(bf16[64,1152]{1,0:T(8,128)(2,1)S(1)} %shard_map.111), channel_id=1, source_target_pairs={{0,4},{1,5},{2,6},{3,7},{4,0},{5,1},{6,2},{7,3},{8,12},{9,13},{10,... | collective-permute-start | bytes 442376 | tf_op jit(solution)/shard_map/ppermute | solution.py:385
  70.1 2.5 %collective-permute-done.19.refs_1_ = bf16[64,1152]{1,0:T(8,128)(2,1)S(1)} collective-permute-done((bf16[64,1152]{1,0:T(8,128)(2,1)S(1)}, bf16[64,1152]{1,0:T(8,128)(2,1)S(1)}, u32[]{:S(2)}, u32[]{:S(2)}) %collective-permute-start.19) | collective-permute-done | bytes 147488 | tf_op jit(solution)/shard_map/ppermute | solution.py:385
  72.6 4.0 %collective-permute-done.17.refs_0_ = bf16[64,1152]{1,0:T(8,128)(2,1)S(1)} collective-permute-done((bf16[64,1152]{1,0:T(8,128)(2,1)S(1)}, bf16[64,1152]{1,0:T(8,128)(2,1)S(1)}, u32[]{:S(2)}, u32[]{:S(2)}) %collective-permute-start.17) | collective-permute-done | bytes 147488 | tf_op jit(solution)/shard_map/ppermute | solution.py:385
  (61 shorter events, 11.7 us)
Async XLA Ops:
  0.0 12.5 %collective-permute-start.3 = (bf16[512,128]{1,0:T(8,128)(2,1)}, bf16[512,128]{1,0:T(8,128)(2,1)S(1)}, u32[]{:S(2)}, u32[]{:S(2)}) collective-permute-start(bf16[512,128]{1,0:T(8,128)(2,1)} %bitcast.18), channel_id=1, source_target_pairs={{0,4},{1,5},{2,6},{3,7},{4,0},{5,1},{6,2},{7,3},{8,12},{9,13},{10,... | collective-permute-start | bytes 393224 | tf_op jit(solution)/shard_map/ppermute | solution.py:385
  4.0 8.5 %collective-permute-start.2 = (bf16[512,128]{1,0:T(8,128)(2,1)}, bf16[512,128]{1,0:T(8,128)(2,1)S(1)}, u32[]{:S(2)}, u32[]{:S(2)}) collective-permute-start(bf16[512,128]{1,0:T(8,128)(2,1)} %bitcast.19), channel_id=1, source_target_pairs={{0,2},{1,3},{2,0},{3,1},{4,6},{5,7},{6,4},{7,5},{8,10},{9,11},{10,... | collective-permute-start | bytes 393224 | tf_op jit(solution)/shard_map/ppermute | solution.py:385
  5.6 9.1 %collective-permute-start.1 = (bf16[512,128]{1,0:T(8,128)(2,1)}, bf16[512,128]{1,0:T(8,128)(2,1)S(1)}, u32[]{:S(2)}, u32[]{:S(2)}) collective-permute-start(bf16[512,128]{1,0:T(8,128)(2,1)} %bitcast.20), channel_id=1, source_target_pairs={{0,1},{1,0},{2,3},{3,2},{4,5},{5,4},{6,7},{7,6},{8,9},{9,8},{10,11... | collective-permute-start | bytes 393224 | tf_op jit(solution)/shard_map/ppermute | solution.py:385
  7.1 43.9 %collective-permute-start.15 = (bf16[512,1024]{1,0:T(8,128)(2,1)}, bf16[512,1024]{1,0:T(8,128)(2,1)S(1)}, u32[]{:S(2)}, u32[]{:S(2)}) collective-permute-start(bf16[512,1024]{1,0:T(8,128)(2,1)} %bitcast.14), channel_id=1, source_target_pairs={{0,8},{8,0},{1,9},{9,1},{2,10},{10,2},{3,11},{11,3},{4,12},{12,4},... | collective-permute-start | bytes 3145736 | tf_op jit(solution)/shard_map/ppermute | solution.py:388
  7.1 62.9 %collective-permute-start = (bf16[512,1024]{1,0:T(8,128)(2,1)}, bf16[512,1024]{1,0:T(8,128)(2,1)S(1)}, u32[]{:S(2)}, u32[]{:S(2)}) collective-permute-start(bf16[512,1024]{1,0:T(8,128)(2,1)} %bitcast.16), channel_id=1, source_target_pairs={{0,8},{8,0},{1,9},{9,1},{2,10},{10,2},{3,11},{11,3},{4,12},{12,4},... | collective-permute-start | bytes 3145736 | tf_op jit(solution)/shard_map/ppermute | solution.py:388
  12.5 8.0 %collective-permute-start.6 = (bf16[512,128]{1,0:T(8,128)(2,1)S(1)}, bf16[512,128]{1,0:T(8,128)(2,1)S(1)}, u32[]{:S(2)}, u32[]{:S(2)}) collective-permute-start(bf16[512,128]{1,0:T(8,128)(2,1)S(1)} %collective-permute-done.3.refs_2_), channel_id=1, source_target_pairs={{0,1},{1,0},{2,3},{3,2},{4,5},{5,4},{6,7},{7,6},{8,9},{9,8},{10,11... | collective-permute-start | bytes 393224 | tf_op jit(solution)/shard_map/ppermute | solution.py:385
  13.2 7.8 %collective-permute-start.5 = (bf16[512,128]{1,0:T(8,128)(2,1)S(1)}, bf16[512,128]{1,0:T(8,128)(2,1)S(1)}, u32[]{:S(2)}, u32[]{:S(2)}) collective-permute-start(bf16[512,128]{1,0:T(8,128)(2,1)S(1)} %collective-permute-done.2.refs_1_), channel_id=1, source_target_pairs={{0,1},{1,0},{2,3},{3,2},{4,5},{5,4},{6,7},{7,6},{8,9},{9,8},{10,11... | collective-permute-start | bytes 393224 | tf_op jit(solution)/shard_map/ppermute | solution.py:385
  20.6 7.7 %collective-permute-start.10 = (bf16[512,128]{1,0:T(8,128)(2,1)S(1)}, bf16[512,128]{1,0:T(8,128)(2,1)S(1)}, u32[]{:S(2)}, u32[]{:S(2)}) collective-permute-start(bf16[512,128]{1,0:T(8,128)(2,1)S(1)} %collective-permute-done.6.refs_1_), channel_id=1, source_target_pairs={{0,2},{1,3},{2,0},{3,1},{4,6},{5,7},{6,4},{7,5},{8,10},{9,11},{10,... | collective-permute-start | bytes 393224 | tf_op jit(solution)/shard_map/ppermute | solution.py:385
  26.1 7.5 %collective-permute-start.13 = (bf16[528,128]{1,0:T(8,128)(2,1)S(1)}, bf16[528,128]{1,0:T(8,128)(2,1)S(1)}, u32[]{:S(2)}, u32[]{:S(2)}) collective-permute-start(bf16[528,128]{1,0:T(8,128)(2,1)S(1)} %get-tuple-element.37.refs_1_), channel_id=1, source_target_pairs={{0,1},{1,0},{2,3},{3,2},{4,5},{5,4},{6,7},{7,6},{8,9},{9,8},{10,11... | collective-permute-start | bytes 405512 | tf_op jit(solution)/shard_map/ppermute | solution.py:385
  26.9 6.2 %collective-permute-start.9 = (bf16[512,128]{1,0:T(8,128)(2,1)S(1)}, bf16[512,128]{1,0:T(8,128)(2,1)S(1)}, u32[]{:S(2)}, u32[]{:S(2)}) collective-permute-start(bf16[512,128]{1,0:T(8,128)(2,1)S(1)} %collective-permute-done.3.refs_2_), channel_id=1, source_target_pairs={{0,2},{1,3},{2,0},{3,1},{4,6},{5,7},{6,4},{7,5},{8,10},{9,11},{10,... | collective-permute-start | bytes 393224 | tf_op jit(solution)/shard_map/ppermute | solution.py:385
  28.3 13.5 %collective-permute-start.4 = (bf16[528,128]{1,0:T(8,128)(2,1)S(1)}, bf16[528,128]{1,0:T(8,128)(2,1)S(1)}, u32[]{:S(2)}, u32[]{:S(2)}) collective-permute-start(bf16[528,128]{1,0:T(8,128)(2,1)S(1)} %get-tuple-element.33.refs_2_), channel_id=1, source_target_pairs={{0,1},{1,0},{2,3},{3,2},{4,5},{5,4},{6,7},{7,6},{8,9},{9,8},{10,11... | collective-permute-start | bytes 405512 | tf_op jit(solution)/shard_map/ppermute | solution.py:385
  33.2 5.8 %collective-permute-start.7 = (bf16[528,128]{1,0:T(8,128)(2,1)S(1)}, bf16[528,128]{1,0:T(8,128)(2,1)S(1)}, u32[]{:S(2)}, u32[]{:S(2)}) collective-permute-start(bf16[528,128]{1,0:T(8,128)(2,1)S(1)} %copy-done.4), channel_id=1, source_target_pairs={{0,1},{1,0},{2,3},{3,2},{4,5},{5,4},{6,7},{7,6},{8,9},{9,8},{10,11... | collective-permute-start | bytes 405512 | tf_op jit(solution)/shard_map/ppermute | solution.py:385
  33.6 6.5 %collective-permute-start.11 = (bf16[528,128]{1,0:T(8,128)(2,1)S(1)}, bf16[528,128]{1,0:T(8,128)(2,1)S(1)}, u32[]{:S(2)}, u32[]{:S(2)}) collective-permute-start(bf16[528,128]{1,0:T(8,128)(2,1)S(1)} %shard_map.105.refs_1_), channel_id=1, source_target_pairs={{0,1},{1,0},{2,3},{3,2},{4,5},{5,4},{6,7},{7,6},{8,9},{9,8},{10,11... | collective-permute-start | bytes 405512 | tf_op jit(solution)/shard_map/ppermute | solution.py:385
  39.0 11.8 %collective-permute-start.14 = (bf16[528,128]{1,0:T(8,128)(2,1)S(1)}, bf16[528,128]{1,0:T(8,128)(2,1)S(1)}, u32[]{:S(2)}, u32[]{:S(2)}) collective-permute-start(bf16[528,128]{1,0:T(8,128)(2,1)S(1)} %shard_map.108.refs_2_), channel_id=1, source_target_pairs={{0,2},{1,3},{2,0},{3,1},{4,6},{5,7},{6,4},{7,5},{8,10},{9,11},{10,... | collective-permute-start | bytes 405512 | tf_op jit(solution)/shard_map/ppermute | solution.py:385
  40.1 10.8 %collective-permute-start.8 = (bf16[528,128]{1,0:T(8,128)(2,1)S(1)}, bf16[528,128]{1,0:T(8,128)(2,1)S(1)}, u32[]{:S(2)}, u32[]{:S(2)}) collective-permute-start(bf16[528,128]{1,0:T(8,128)(2,1)S(1)} %shard_map.104.refs_0_), channel_id=1, source_target_pairs={{0,4},{1,5},{2,6},{3,7},{4,0},{5,1},{6,2},{7,3},{8,12},{9,13},{10,... | collective-permute-start | bytes 405512 | tf_op jit(solution)/shard_map/ppermute | solution.py:385
  41.8 9.2 %collective-permute-start.12 = (bf16[528,128]{1,0:T(8,128)(2,1)S(1)}, bf16[528,128]{1,0:T(8,128)(2,1)S(1)}, u32[]{:S(2)}, u32[]{:S(2)}) collective-permute-start(bf16[528,128]{1,0:T(8,128)(2,1)S(1)} %shard_map.107.refs_1_), channel_id=1, source_target_pairs={{0,6},{1,7},{2,4},{3,5},{4,2},{5,3},{6,0},{7,1},{8,14},{9,15},{10,... | collective-permute-start | bytes 405512 | tf_op jit(solution)/shard_map/ppermute | solution.py:385
  50.8 25.8 %copy-start.1 = (bf16[8,64,1024]{2,1,0:T(8,128)(2,1)S(1)}, bf16[8,64,1024]{2,1,0:T(8,128)(2,1)}, u32[]{:S(2)}) copy-start(bf16[8,64,1024]{2,1,0:T(8,128)(2,1)} %param.18) | copy-start | bytes 3145732
  55.8 6.9 %collective-permute-start.20 = (bf16[64,1152]{1,0:T(8,128)(2,1)S(1)}, bf16[64,1152]{1,0:T(8,128)(2,1)S(1)}, u32[]{:S(2)}, u32[]{:S(2)}) collective-permute-start(bf16[64,1152]{1,0:T(8,128)(2,1)S(1)} %get-tuple-element.44), channel_id=1, source_target_pairs={{0,1},{1,0},{2,3},{3,2},{4,5},{5,4},{6,7},{7,6},{8,9},{9,8},{10,11... | collective-permute-start | bytes 442376 | tf_op jit(solution)/shard_map/ppermute | solution.py:385
  57.1 8.3 %collective-permute-start.18 = (bf16[64,1152]{1,0:T(8,128)(2,1)S(1)}, bf16[64,1152]{1,0:T(8,128)(2,1)S(1)}, u32[]{:S(2)}, u32[]{:S(2)}) collective-permute-start(bf16[64,1152]{1,0:T(8,128)(2,1)S(1)} %get-tuple-element.42), channel_id=1, source_target_pairs={{0,1},{1,0},{2,3},{3,2},{4,5},{5,4},{6,7},{7,6},{8,9},{9,8},{10,11... | collective-permute-start | bytes 442376 | tf_op jit(solution)/shard_map/ppermute | solution.py:385
  57.9 9.2 %collective-permute-start.16 = (bf16[64,1152]{1,0:T(8,128)(2,1)S(1)}, bf16[64,1152]{1,0:T(8,128)(2,1)S(1)}, u32[]{:S(2)}, u32[]{:S(2)}) collective-permute-start(bf16[64,1152]{1,0:T(8,128)(2,1)S(1)} %get-tuple-element.40), channel_id=1, source_target_pairs={{0,1},{1,0},{2,3},{3,2},{4,5},{5,4},{6,7},{7,6},{8,9},{9,8},{10,11... | collective-permute-start | bytes 442376 | tf_op jit(solution)/shard_map/ppermute | solution.py:385
  59.1 10.8 %collective-permute-start.22 = (bf16[64,1152]{1,0:T(8,128)(2,1)S(1)}, bf16[64,1152]{1,0:T(8,128)(2,1)S(1)}, u32[]{:S(2)}, u32[]{:S(2)}) collective-permute-start(bf16[64,1152]{1,0:T(8,128)(2,1)S(1)} %get-tuple-element.46), channel_id=1, source_target_pairs={{0,1},{1,0},{2,3},{3,2},{4,5},{5,4},{6,7},{7,6},{8,9},{9,8},{10,11... | collective-permute-start | bytes 442376 | tf_op jit(solution)/shard_map/ppermute | solution.py:385
  62.8 7.3 %collective-permute-start.21 = (bf16[64,1152]{1,0:T(8,128)(2,1)S(1)}, bf16[64,1152]{1,0:T(8,128)(2,1)S(1)}, u32[]{:S(2)}, u32[]{:S(2)}) collective-permute-start(bf16[64,1152]{1,0:T(8,128)(2,1)S(1)} %shard_map.113), channel_id=1, source_target_pairs={{0,2},{1,3},{2,0},{3,1},{4,6},{5,7},{6,4},{7,5},{8,10},{9,11},{10,... | collective-permute-start | bytes 442376 | tf_op jit(solution)/shard_map/ppermute | solution.py:385
  65.5 7.1 %collective-permute-start.19 = (bf16[64,1152]{1,0:T(8,128)(2,1)S(1)}, bf16[64,1152]{1,0:T(8,128)(2,1)S(1)}, u32[]{:S(2)}, u32[]{:S(2)}) collective-permute-start(bf16[64,1152]{1,0:T(8,128)(2,1)S(1)} %shard_map.112), channel_id=1, source_target_pairs={{0,6},{1,7},{2,4},{3,5},{4,2},{5,3},{6,0},{7,1},{8,14},{9,15},{10,... | collective-permute-start | bytes 442376 | tf_op jit(solution)/shard_map/ppermute | solution.py:385
  67.2 9.4 %collective-permute-start.17 = (bf16[64,1152]{1,0:T(8,128)(2,1)S(1)}, bf16[64,1152]{1,0:T(8,128)(2,1)S(1)}, u32[]{:S(2)}, u32[]{:S(2)}) collective-permute-start(bf16[64,1152]{1,0:T(8,128)(2,1)S(1)} %shard_map.111), channel_id=1, source_target_pairs={{0,4},{1,5},{2,6},{3,7},{4,0},{5,1},{6,2},{7,3},{8,12},{9,13},{10,... | collective-permute-start | bytes 442376 | tf_op jit(solution)/shard_map/ppermute | solution.py:385
  (7 other events, 44.2 us)

commit v4 on v3

--- a/solution.py
+++ b/solution.py
@@ -23,29 +23,8 @@
     ("attend", 1, 2, 4),
     ("forward", 7),
     ("attend", 3, 5),
-    ("attend", 7),
-    ("attend", 6),
+    ("attend", 7, 6),
 ]
-
-
-def call(body, grid, in_specs, out_shape, out_specs, scratch=(), prefetch=1, cost=None):
-    return pl.pallas_call(
-        body,
-        grid_spec=pltpu.PrefetchScalarGridSpec(
-            num_scalar_prefetch=prefetch,
-            grid=grid,
-            in_specs=in_specs,
-            out_specs=out_specs,
-            scratch_shapes=list(scratch),
-        ),
-        out_shape=out_shape,
-        compiler_params=pltpu.CompilerParams(vmem_limit_bytes=SMALL),
-        cost_estimate=cost,
-    )
-
-
-def whole(shape):
-    return pl.BlockSpec(shape, lambda i, *_: (0,) * len(shape))
 
 
 def split2(x):
@@ -99,16 +78,17 @@
     return stat
 
 
-def attend_body(n, blocks, heads, scale, sc_ref, len_ref, k_hbm, v_hbm, *refs):
+def attend_body(which, group, blocks, heads, scale, len_ref, k_hbm, v_hbm, *refs):
+    n = len(which)
+    me = lax.axis_index("tensor")
     q_refs = refs[:n]
-    o_refs = refs[-6 - n : -6]
-    q_buf, k_buf, v_buf, q_sem, k_sem, v_sem = refs[-6:]
+    o_refs = refs[-4 - n : -4]
+    k_buf, v_buf, k_sem, v_sem = refs[-4:]
     size = k_hbm.shape[0] // blocks
     many = size * heads
-    first, copies = [], []
+    copies = []
     for j in range(n):
-        kv = sc_ref[j]
-        first.append(pltpu.make_async_copy(q_refs[j], q_buf.at[j], q_sem.at[j]))
+        kv = lax.div((me ^ which[j]) * heads, group)
         for b in range(blocks):
             at, i = pl.ds(b * size, size), j * blocks + b
             copies.append(
@@ -117,13 +97,9 @@
                     pltpu.make_async_copy(v_hbm.at[at, kv], v_buf.at[i], v_sem.at[i]),
                 )
             )
-    for c in first:
-        c.start()
     for ck, cv in copies:
         ck.start()
         cv.start()
-    for c in first:
-        c.wait()
     for j in range(n):
         stat = jnp.zeros((TILE, LANES), F32)
         for b in range(blocks):
@@ -131,13 +107,13 @@
             copies[i][0].wait()
             copies[i][1].wait()
             stat = stat + attend_part(
-                heads, scale, q_buf[j, b * many : (b + 1) * many, :], len_ref, k_buf.at[i], v_buf.at[i],
+                heads, scale, q_refs[j][b * many : (b + 1) * many, :], len_ref, k_buf.at[i], v_buf.at[i],
                 b * many // TILE, o_refs[j],
             )
         o_refs[j][many * blocks :, :] = stat.astype(BF16)
 
 
-def attend(which, queries, live, keys, values, heads, scale, after):
+def attend(which, group, queries, live, keys, values, heads, scale, after):
     n, blocks = len(queries), 2
     rows, _, positions, width = keys.shape
     vmem = pl.BlockSpec(memory_space=pltpu.VMEM)
@@ -147,20 +123,18 @@
     buf = pltpu.VMEM((n * blocks, rows // blocks, positions, width), BF16)
     sem = pltpu.SemaphoreType.DMA((n * blocks,))
     return pl.pallas_call(
-        functools.partial(attend_body, n, blocks, heads, scale),
-        in_specs=[smem, smem, hbm, hbm] + [anywhere] * (n + len(after)),
+        functools.partial(attend_body, which, group, blocks, heads, scale),
+        in_specs=[smem, hbm, hbm] + [vmem] * n + [anywhere] * len(after),
         out_specs=[vmem] * n,
         out_shape=[jax.ShapeDtypeStruct((rows * heads + TILE, width), BF16)] * n,
-        scratch_shapes=[
-            pltpu.VMEM((n, rows * heads, width), BF16), buf, buf, pltpu.SemaphoreType.DMA((n,)), sem, sem
-        ],
+        scratch_shapes=[buf, buf, sem, sem],
         compiler_params=pltpu.CompilerParams(vmem_limit_bytes=LARGE),
         cost_estimate=pl.CostEstimate(
             flops=32 * n * rows * heads * positions * width,
             bytes_accessed=4 * n * rows * positions * width,
             transcendentals=n * rows * heads * positions,
         ),
-    )(which, live, keys, values, *queries, *after)
+    )(live, keys, values, *queries, *after)
 
 
 def load_body(blocks, source, *refs):
@@ -254,11 +228,12 @@
     return total
 
 
-def project_body(n_parts, n_out, heads, rank, sc_ref, *refs):
+def project_body(n_parts, blocks, heads, rank, *refs):
     parts = refs[:n_parts]
     w_ref, slot_ref, down_a, down_b = refs[n_parts : n_parts + 4]
-    outs = refs[n_parts + 4 : n_parts + 4 + n_out]
-    att_ref, att32 = refs[n_parts + 4 + n_out :]
+    outs = refs[n_parts + 4 : -2]
+    att_ref, att32 = refs[-2:]
+    me, mine = lax.axis_index("tensor"), lax.axis_index("dp")
     finish_attention(parts, att32, att_ref, heads)
     att = att_ref[...]
     over = (((1,), (1,)), ((), ()))
@@ -266,26 +241,25 @@
     other = lax.dot_general(att, down_b[...], over, preferred_element_type=F32)
     slots = slot_ref[...]
     per = down_a.shape[0] // rank
-    mine = sc_ref[0]
     s = chosen(slots - mine * per, own, rank) + chosen(slots - (1 - mine) * per, other, rank)
     s = s + pltpu.roll(s, rank, 1)
     high, mid = split2(s)
     shrink = jnp.where(iota(s.shape, 1) < rank, high, mid)
     for k, out in enumerate(outs):
         cols = out.shape[1] - LANES
-        at = pl.ds(pl.multiple_of(sc_ref[1 + k] * cols, cols), cols)
+        at = pl.ds(pl.multiple_of((me ^ blocks[k]) * cols, cols), cols)
         out[:, :cols] = jnp.dot(att, w_ref[:, at], preferred_element_type=F32).astype(out.dtype)
         out[:, cols:] = shrink.astype(out.dtype)
 
 
-def project(scalars, parts, weight, slots, down_a, down_b, heads, rank, cols):
-    n_out = scalars.shape[0] - 1
+def project(blocks, parts, weight, slots, down_a, down_b, heads, rank, cols):
+    n_out = len(blocks)
     rows = slots.shape[0]
     width = weight.shape[0]
     vmem = pl.BlockSpec(memory_space=pltpu.VMEM)
     return pl.pallas_call(
-        functools.partial(project_body, len(parts), n_out, heads, rank),
-        in_specs=[pl.BlockSpec(memory_space=pltpu.SMEM)] + [vmem] * (len(parts) + 4),
+        functools.partial(project_body, len(parts), blocks, heads, rank),
+        in_specs=[vmem] * (len(parts) + 4),
         out_specs=[vmem] * n_out,
         out_shape=[
             jax.ShapeDtypeStruct((rows, cols + LANES), BF16 if k < n_out // 2 else F32)
@@ -296,7 +270,7 @@
         cost_estimate=pl.CostEstimate(
             flops=2 * rows * width * cols * n_out, bytes_accessed=2 * width * cols * n_out, transcendentals=0
         ),
-    )(scalars, *parts, weight, slots, down_a, down_b)
+    )(*parts, weight, slots, down_a, down_b)
 
 
 def shrink_sum(parts, rank):
@@ -333,13 +307,13 @@
     )
 
 
-def last_body(rank, n_parts, mine_ref, slot_ref, up_a, up_b, *refs):
+def last_body(rank, n_parts, slot_ref, up_a, up_b, *refs):
     parts, o_ref = refs[:n_parts], refs[n_parts]
     cols = o_ref.shape[1]
     base = sum(p[:, :cols].astype(F32) for p in parts)
     shrink = shrink_sum([p[:, cols:].astype(F32) for p in parts], rank).astype(BF16).astype(F32)
     slots = slot_ref[...]
-    mine = mine_ref[0]
+    mine = lax.axis_index("dp")
     per = up_a.shape[0] // rank
     xa = expanded(slots - mine * per, shrink, rank, up_a.shape[0])
     xb = expanded(slots - (1 - mine) * per, shrink, rank, up_b.shape[0])
@@ -349,16 +323,14 @@
     o_ref[...] = (base + lora).astype(BF16)
 
 
-def last(mine, slots, up_a, up_b, parts, rank):
+def last(slots, up_a, up_b, parts, rank):
     rows, cols = slots.shape[0], up_a.shape[1]
-    return call(
+    return pl.pallas_call(
         functools.partial(last_body, rank, len(parts)),
-        (1,),
-        [whole(slots.shape), whole(up_a.shape), whole(up_b.shape)] + [whole(p.shape) for p in parts],
-        jax.ShapeDtypeStruct((rows, cols), BF16),
-        whole((rows, cols)),
-        cost=pl.CostEstimate(flops=4 * rows * up_a.size // rows, bytes_accessed=4 * up_a.size, transcendentals=0),
-    )(mine, slots, up_a, up_b, *parts)
+        out_shape=jax.ShapeDtypeStruct((rows, cols), BF16),
+        compiler_params=pltpu.CompilerParams(vmem_limit_bytes=LARGE),
+        cost_estimate=pl.CostEstimate(flops=4 * up_a.size, bytes_accessed=4 * up_a.size, transcendentals=0),
+    )(slots, up_a, up_b, *parts)
 
 
 def on_device(
@@ -379,7 +351,6 @@
     slots_here, _, rank = adapter_down_weight.shape
     cols = adapter_up_weight.shape[2]
     me = lax.axis_index("tensor")
-    mine = lax.axis_index("dp")
 
     def hop(x, k):
         return lax.ppermute(x, "tensor", [(i, i ^ k) for i in range(tensor)])
@@ -388,7 +359,7 @@
         return lax.ppermute(x, "dp", [(0, 1), (1, 0)])
 
     far = sorted(range(2, tensor, 2), key=lambda k: -min(k, 4))
-    outer = far + [0]
+    outer = far[::-1] + [0]
 
     down_a = jnp.swapaxes(adapter_down_weight, 1, 2).reshape(slots_here * rank, -1)
     up_a = adapter_up_weight.reshape(slots_here * rank, cols)
@@ -401,11 +372,11 @@
         for x in (cached_key_rows, cached_value_rows, output_weight)
     )
 
-    held, partial, token = {0: queries.reshape(rows * heads, width)}, {}, ()
+    q = queries.reshape(rows * heads, width)
+    held, partial, token = {0: q}, {}, ()
     for kind, *ks in PLAN + [(kind, k) for k in range(8, tensor) for kind in ("forward", "attend")]:
         if kind == "attend":
-            which = jnp.stack([lax.div((me ^ k) * heads, group) for k in ks]).astype(jnp.int32)
-            outs = attend(which, [held[k] for k in ks], live, keys, values, heads, scale, token)
+            outs = attend(ks, group, [held[k] for k in ks], live, keys, values, heads, scale, token)
             partial.update(zip(ks, outs))
             token = [outs[0]]
             continue
@@ -424,15 +395,14 @@
     slot = jnp.sum(jnp.where(match, adapter_slot_index[None, :], 0), axis=1)
     slots = jnp.broadcast_to(slot[:, None], (rows, LANES)).astype(jnp.int32)
 
-    order = jnp.array([k for k in outer], jnp.int32)
-    scalars = jnp.concatenate([mine[None], me ^ order ^ 1, me ^ order]).astype(jnp.int32)
+    blocks = [k ^ 1 for k in outer] + list(outer)
     weight = load(weight, [merged[k] for k in far])
-    outs = project(scalars, parts, weight, slots, down_a, down_b, heads, rank, cols)
+    outs = project(blocks, parts, weight, slots, down_a, down_b, heads, rank, cols)
     first, own = outs[: len(outer)], outs[len(outer) :]
     arrived = [hop(x, 1) for x in first]
     summed = [add(a, b, rank) for a, b in zip(own, arrived)]
     final = [hop(x, k) if k else x for x, k in zip(summed, outer)]
-    return last(mine[None].astype(jnp.int32), slots, up_a, up_b, final, rank)
+    return last(slots, up_a, up_b, final, rank)
 
 
 def solution(mesh):

time: 77.9 us -> 72.2 us (0.927)
  Pallas kernels: 33.8 us -> 29.8 us
    pallas_call x7 -> x6, Pallas kernels: 26 us -> 22 us  [the longest x4 16.6 us: attend(): pl.pallas_call(functools.partial(attend_body, which, group, blocks, heads...]
    unnamed x16 -> x10, local copies, waits for them, and re-layouts: 1.58 us -> 0.93 us
  transfers between devices with their start and end apart: 23 -> 23, of which waited for: 5 -> 6; matrix products, arithmetic and copies ran while one was open for 1% -> 1% of each run, Pallas kernels for 42% -> 40%
where the time goes in v4:
time: 72.2 us; the launch traced here: 72.1 us
  starting transfers between devices  30.7 us (43%)
  Pallas kernels  29.8 us (41%)
  waiting for transfers between devices  9.65 us (13%)
  local copies, waits for them, and re-layouts  1 us (1%)
  other arithmetic  0.75 us (1%)
    ppermute x21, starting transfers between devices, hop(): return lax.ppermute(x, 'tensor', [(i, i ^ k) for i in range(tensor)])  30.3 us
    pallas_call x4, Pallas kernels, attend(): pl.pallas_call(functools.partial(attend_body, which, group, blocks, heads...  16.6 us
    ppermute x21, waiting for transfers between devices, hop(): return lax.ppermute(x, 'tensor', [(i, i ^ k) for i in range(tensor)])  9.65 us
    pallas_call x1, Pallas kernels, load(): pl.pallas_call(functools.partial(load_body, blocks), in_specs=[pl.BlockSp...  5.96 us
    pallas_call x1, Pallas kernels, project(): pl.pallas_call(functools.partial(project_body, len(parts), blocks, heads,...  4.22 us
  transfers between devices with their start and end apart: 23, of which 6 were waited for; matrix products, arithmetic and copies ran while one was open for 1% of the time, Pallas kernels for 40%

profile of v4, /device:TPU:0, one launch (start us, length us, event | category | flops | bytes accessed | tf_op | source)
XLA Modules:
  0.0 72.1 jit_solution(2883877478593923217)
XLA Ops:
  0.5 3.6 %collective-permute-start.3 = (bf16[512,128]{1,0:T(8,128)(2,1)}, bf16[512,128]{1,0:T(8,128)(2,1)S(1)}, u32[]{:S(2)}, u32[]{:S(2)}) collective-permute-start(bf16[512,128]{1,0:T(8,128)(2,1)} %bitcast.9), channel_id=1, source_target_pairs={{0,4},{1,5},{2,6},{3,7},{4,0},{5,1},{6,2},{7,3},{8,12},{9,13},{10,... | collective-permute-start | bytes 393224 | tf_op jit(solution)/shard_map/ppermute | solution.py:356
  4.0 1.6 %collective-permute-start.2 = (bf16[512,128]{1,0:T(8,128)(2,1)}, bf16[512,128]{1,0:T(8,128)(2,1)S(1)}, u32[]{:S(2)}, u32[]{:S(2)}) collective-permute-start(bf16[512,128]{1,0:T(8,128)(2,1)} %bitcast.10), channel_id=1, source_target_pairs={{0,2},{1,3},{2,0},{3,1},{4,6},{5,7},{6,4},{7,5},{8,10},{9,11},{10,... | collective-permute-start | bytes 393224 | tf_op jit(solution)/shard_map/ppermute | solution.py:356
  5.6 1.5 %collective-permute-start.1 = (bf16[512,128]{1,0:T(8,128)(2,1)}, bf16[512,128]{1,0:T(8,128)(2,1)S(1)}, u32[]{:S(2)}, u32[]{:S(2)}) collective-permute-start(bf16[512,128]{1,0:T(8,128)(2,1)} %bitcast.11), channel_id=1, source_target_pairs={{0,1},{1,0},{2,3},{3,2},{4,5},{5,4},{6,7},{7,6},{8,9},{9,8},{10,11... | collective-permute-start | bytes 393224 | tf_op jit(solution)/shard_map/ppermute | solution.py:356
  8.7 3.0 %shard_map.91.refs_3_.a_ref = bf16[528,128]{1,0:T(8,128)(2,1)S(1)} custom-call(s32[64]{0:T(128)S(1)} %subtract_clamp_fusion.len_ref, bf16[64,8,96,128]{3,2,1,0:T(8,128)(2,1)} %k_hbm.7, bf16[64,8,96,128]{3,2,1,0:T(8,128)(2,1)} %v_hbm.7, bf16[512,128]{1,0:T(8,128)(2,1)S(1)} %bitcast.12), custom_call_target="tpu_custom_call" | custom-call | flops 201326592 | bytes 3145728 | tf_op jit(solution)/shard_map/pallas_call | solution.py:125
  14.5 5.3 %shard_map.92 = (bf16[528,128]{1,0:T(8,128)(2,1)S(1)}, bf16[528,128]{1,0:T(8,128)(2,1)S(1)}, bf16[528,128]{1,0:T(8,128)(2,1)S(1)}) custom-call(s32[64]{0:T(128)S(1)} %subtract_clamp_fusion.len_ref, bf16[64,8,96,128]{3,2,1,0:T(8,128)(2,1)} %k_hbm.7, bf16[64,8,96,128]{3,2,1,0:T(8,128)(2,1)} %v_hbm.7, bf16[512,128]{1,0:T(8,128)(2,1)S(1)} %collective-permute-done.1.refs_0_, ...), custom_call_target="tpu_custom_call" | custom-call | flops 603979776 | bytes 9437184 | tf_op jit(solution)/shard_map/pallas_call | solution.py:125
  19.9 1.3 %collective-permute-start.9 = (bf16[512,128]{1,0:T(8,128)(2,1)S(1)}, bf16[512,128]{1,0:T(8,128)(2,1)S(1)}, u32[]{:S(2)}, u32[]{:S(2)}) collective-permute-start(bf16[512,128]{1,0:T(8,128)(2,1)S(1)} %collective-permute-done.6.refs_1_), channel_id=1, source_target_pairs={{0,2},{1,3},{2,0},{3,1},{4,6},{5,7},{6,4},{7,5},{8,10},{9,11},{10,... | collective-permute-start | bytes 393224 | tf_op jit(solution)/shard_map/ppermute | solution.py:356
  21.2 4.1 %shard_map.94 = (bf16[528,128]{1,0:T(8,128)(2,1)S(1)}, bf16[528,128]{1,0:T(8,128)(2,1)S(1)}) custom-call(s32[64]{0:T(128)S(1)} %subtract_clamp_fusion.len_ref, bf16[64,8,96,128]{3,2,1,0:T(8,128)(2,1)} %k_hbm.7, bf16[64,8,96,128]{3,2,1,0:T(8,128)(2,1)} %v_hbm.7, bf16[512,128]{1,0:T(8,128)(2,1)S(1)} %collective-permute-done.5.refs_0_, ...), custom_call_target="tpu_custom_call" | custom-call | flops 402653184 | bytes 6291456 | tf_op jit(solution)/shard_map/pallas_call | solution.py:125
  25.4 1.2 %collective-permute-start.13 = (bf16[528,128]{1,0:T(8,128)(2,1)S(1)}, bf16[528,128]{1,0:T(8,128)(2,1)S(1)}, u32[]{:S(2)}, u32[]{:S(2)}) collective-permute-start(bf16[528,128]{1,0:T(8,128)(2,1)S(1)} %get-tuple-element.39.refs_2_), channel_id=1, source_target_pairs={{0,1},{1,0},{2,3},{3,2},{4,5},{5,4},{6,7},{7,6},{8,9},{9,8},{10,11... | collective-permute-start | bytes 405512 | tf_op jit(solution)/shard_map/ppermute | solution.py:356
  27.5 4.1 %shard_map.96 = (bf16[528,128]{1,0:T(8,128)(2,1)S(1)}, bf16[528,128]{1,0:T(8,128)(2,1)S(1)}) custom-call(s32[64]{0:T(128)S(1)} %subtract_clamp_fusion.len_ref, bf16[64,8,96,128]{3,2,1,0:T(8,128)(2,1)} %k_hbm.7, bf16[64,8,96,128]{3,2,1,0:T(8,128)(2,1)} %v_hbm.7, bf16[512,128]{1,0:T(8,128)(2,1)S(1)} %collective-permute-done.9.refs_0_, ...), custom_call_target="tpu_custom_call" | custom-call | flops 402653184 | bytes 6291456 | tf_op jit(solution)/shard_map/pallas_call | solution.py:125
  31.6 1.2 %collective-permute-start.11 = (bf16[528,128]{1,0:T(8,128)(2,1)S(1)}, bf16[528,128]{1,0:T(8,128)(2,1)S(1)}, u32[]{:S(2)}, u32[]{:S(2)}) collective-permute-start(bf16[528,128]{1,0:T(8,128)(2,1)S(1)} %get-tuple-element.41), channel_id=1, source_target_pairs={{0,1},{1,0},{2,3},{3,2},{4,5},{5,4},{6,7},{7,6},{8,9},{9,8},{10,11... | collective-permute-start | bytes 405512 | tf_op jit(solution)/shard_map/ppermute | solution.py:356
  35.4 2.2 %collective-permute-done.11.b_ref = bf16[528,128]{1,0:T(8,128)(2,1)S(1)} collective-permute-done((bf16[528,128]{1,0:T(8,128)(2,1)S(1)}, bf16[528,128]{1,0:T(8,128)(2,1)S(1)}, u32[]{:S(2)}, u32[]{:S(2)}) %collective-permute-start.11) | collective-permute-done | bytes 135200 | tf_op jit(solution)/shard_map/ppermute | solution.py:356
  37.6 1.4 %collective-permute-start.8 = (bf16[528,128]{1,0:T(8,128)(2,1)S(1)}, bf16[528,128]{1,0:T(8,128)(2,1)S(1)}, u32[]{:S(2)}, u32[]{:S(2)}) collective-permute-start(bf16[528,128]{1,0:T(8,128)(2,1)S(1)} %shard_map.95.refs_0_), channel_id=1, source_target_pairs={{0,4},{1,5},{2,6},{3,7},{4,0},{5,1},{6,2},{7,3},{8,12},{9,13},{10,... | collective-permute-start | bytes 405512 | tf_op jit(solution)/shard_map/ppermute | solution.py:356
  39.3 2.3 %collective-permute-start.12 = (bf16[528,128]{1,0:T(8,128)(2,1)S(1)}, bf16[528,128]{1,0:T(8,128)(2,1)S(1)}, u32[]{:S(2)}, u32[]{:S(2)}) collective-permute-start(bf16[528,128]{1,0:T(8,128)(2,1)S(1)} %shard_map.97.refs_1_), channel_id=1, source_target_pairs={{0,6},{1,7},{2,4},{3,5},{4,2},{5,3},{6,0},{7,1},{8,14},{9,15},{10,... | collective-permute-start | bytes 405512 | tf_op jit(solution)/shard_map/ppermute | solution.py:356
  42.0 6.0 %shard_map.99.refs_4_ = bf16[1024,8192]{1,0:T(8,128)(2,1)S(1)} custom-call(bf16[1024,8192]{1,0:T(8,128)(2,1)} %source.1, bf16[528,128]{1,0:T(8,128)(2,1)S(1)} %shard_map.95.refs_0_, bf16[528,128]{1,0:T(8,128)(2,1)S(1)} %shard_map.97.refs_1_, bf16[528,128]{1,0:T(8,128)(2,1)S(1)} %shard_map.98.refs_2_), custom_call_target="tpu_custom_call" | custom-call | bytes 16777216 | tf_op jit(solution)/shard_map/pallas_call | solution.py:155
  48.2 4.2 %shard_map.100 = (bf16[64,1152]{1,0:T(8,128)(2,1)S(1)}, bf16[64,1152]{1,0:T(8,128)(2,1)S(1)}, bf16[64,1152]{1,0:T(8,128)(2,1)S(1)}, bf16[64,1152]{1,0:T(8,128)(2...) custom-call(bf16[528,128]{1,0:T(8,128)(2,1)S(1)} %shard_map.93.refs_, ...), custom_call_target="tpu_custom_call" | custom-call | flops 1073741824 | bytes 16777216 | tf_op jit(solution)/shard_map/pallas_call | solution.py:260
  52.4 1.5 %collective-permute-start.20 = (bf16[64,1152]{1,0:T(8,128)(2,1)S(1)}, bf16[64,1152]{1,0:T(8,128)(2,1)S(1)}, u32[]{:S(2)}, u32[]{:S(2)}) collective-permute-start(bf16[64,1152]{1,0:T(8,128)(2,1)S(1)} %get-tuple-element.48), channel_id=1, source_target_pairs={{0,1},{1,0},{2,3},{3,2},{4,5},{5,4},{6,7},{7,6},{8,9},{9,8},{10,11... | collective-permute-start | bytes 442376 | tf_op jit(solution)/shard_map/ppermute | solution.py:356
  54.5 1.4 %collective-permute-start.16 = (bf16[64,1152]{1,0:T(8,128)(2,1)S(1)}, bf16[64,1152]{1,0:T(8,128)(2,1)S(1)}, u32[]{:S(2)}, u32[]{:S(2)}) collective-permute-start(bf16[64,1152]{1,0:T(8,128)(2,1)S(1)} %get-tuple-element.44), channel_id=1, source_target_pairs={{0,1},{1,0},{2,3},{3,2},{4,5},{5,4},{6,7},{7,6},{8,9},{9,8},{10,11... | collective-permute-start | bytes 442376 | tf_op jit(solution)/shard_map/ppermute | solution.py:356
  56.5 2.7 %collective-permute-done.20.b_ref = bf16[64,1152]{1,0:T(8,128)(2,1)S(1)} collective-permute-done((bf16[64,1152]{1,0:T(8,128)(2,1)S(1)}, bf16[64,1152]{1,0:T(8,128)(2,1)S(1)}, u32[]{:S(2)}, u32[]{:S(2)}) %collective-permute-start.20) | collective-permute-done | bytes 147488 | tf_op jit(solution)/shard_map/ppermute | solution.py:356
  59.4 2.9 %collective-permute-start.21 = (bf16[64,1152]{1,0:T(8,128)(2,1)S(1)}, bf16[64,1152]{1,0:T(8,128)(2,1)S(1)}, u32[]{:S(2)}, u32[]{:S(2)}) collective-permute-start(bf16[64,1152]{1,0:T(8,128)(2,1)S(1)} %shard_map.103), channel_id=1, source_target_pairs={{0,4},{1,5},{2,6},{3,7},{4,0},{5,1},{6,2},{7,3},{8,12},{9,13},{10,... | collective-permute-start | bytes 442376 | tf_op jit(solution)/shard_map/ppermute | solution.py:356
  62.4 1.6 %collective-permute-start.19 = (bf16[64,1152]{1,0:T(8,128)(2,1)S(1)}, bf16[64,1152]{1,0:T(8,128)(2,1)S(1)}, u32[]{:S(2)}, u32[]{:S(2)}) collective-permute-start(bf16[64,1152]{1,0:T(8,128)(2,1)S(1)} %shard_map.102), channel_id=1, source_target_pairs={{0,6},{1,7},{2,4},{3,5},{4,2},{5,3},{6,0},{7,1},{8,14},{9,15},{10,... | collective-permute-start | bytes 442376 | tf_op jit(solution)/shard_map/ppermute | solution.py:356
  64.1 2.1 %collective-permute-start.17 = (bf16[64,1152]{1,0:T(8,128)(2,1)S(1)}, bf16[64,1152]{1,0:T(8,128)(2,1)S(1)}, u32[]{:S(2)}, u32[]{:S(2)}) collective-permute-start(bf16[64,1152]{1,0:T(8,128)(2,1)S(1)} %shard_map.101), channel_id=1, source_target_pairs={{0,2},{1,3},{2,0},{3,1},{4,6},{5,7},{6,4},{7,5},{8,10},{9,11},{10,... | collective-permute-start | bytes 442376 | tf_op jit(solution)/shard_map/ppermute | solution.py:356
  67.2 2.4 %collective-permute-done.19.refs_1_ = bf16[64,1152]{1,0:T(8,128)(2,1)S(1)} collective-permute-done((bf16[64,1152]{1,0:T(8,128)(2,1)S(1)}, bf16[64,1152]{1,0:T(8,128)(2,1)S(1)}, u32[]{:S(2)}, u32[]{:S(2)}) %collective-permute-start.19) | collective-permute-done | bytes 147488 | tf_op jit(solution)/shard_map/ppermute | solution.py:356
  69.6 1.3 %collective-permute-done.17.refs_0_ = bf16[64,1152]{1,0:T(8,128)(2,1)S(1)} collective-permute-done((bf16[64,1152]{1,0:T(8,128)(2,1)S(1)}, bf16[64,1152]{1,0:T(8,128)(2,1)S(1)}, u32[]{:S(2)}, u32[]{:S(2)}) %collective-permute-start.17) | collective-permute-done | bytes 147488 | tf_op jit(solution)/shard_map/ppermute | solution.py:356
  70.9 1.2 %shard_map.105 = bf16[64,1024]{1,0:T(8,128)(2,1)} custom-call(s32[64,128]{1,0:T(8,128)S(1)} %broadcast_in_dim.23.refs_5_.slot_ref, bf16[512,1024]{1,0:T(8,128)(2,1)S(1)} %bitcast.8, bf16[512,1024]{1,0:T(8,128)(2,1)S(1)} %collective-permute-done.up_b, bf16[64,1152]{1,0:T(8,128)(2,1)S(1)} %collective-permute-done.17.refs_0_, ...), custom_call_target="tpu_custom_call" | custom-call | flops 2097152 | bytes 2097152 | tf_op jit(solution)/shard_map/pallas_call | solution.py:328
  (50 shorter events, 11.9 us)
Async XLA Ops:
  0.0 48.1 %collective-permute-start.15 = (bf16[512,1024]{1,0:T(8,128)(2,1)}, bf16[512,1024]{1,0:T(8,128)(2,1)S(1)}, u32[]{:S(2)}, u32[]{:S(2)}) collective-permute-start(bf16[512,1024]{1,0:T(8,128)(2,1)} %bitcast.5), channel_id=1, source_target_pairs={{0,8},{8,0},{1,9},{9,1},{2,10},{10,2},{3,11},{11,3},{4,12},{12,4},... | collective-permute-start | bytes 3145736 | tf_op jit(solution)/shard_map/ppermute | solution.py:359
  0.5 11.3 %collective-permute-start.3 = (bf16[512,128]{1,0:T(8,128)(2,1)}, bf16[512,128]{1,0:T(8,128)(2,1)S(1)}, u32[]{:S(2)}, u32[]{:S(2)}) collective-permute-start(bf16[512,128]{1,0:T(8,128)(2,1)} %bitcast.9), channel_id=1, source_target_pairs={{0,4},{1,5},{2,6},{3,7},{4,0},{5,1},{6,2},{7,3},{8,12},{9,13},{10,... | collective-permute-start | bytes 393224 | tf_op jit(solution)/shard_map/ppermute | solution.py:356
  4.0 8.9 %collective-permute-start.2 = (bf16[512,128]{1,0:T(8,128)(2,1)}, bf16[512,128]{1,0:T(8,128)(2,1)S(1)}, u32[]{:S(2)}, u32[]{:S(2)}) collective-permute-start(bf16[512,128]{1,0:T(8,128)(2,1)} %bitcast.10), channel_id=1, source_target_pairs={{0,2},{1,3},{2,0},{3,1},{4,6},{5,7},{6,4},{7,5},{8,10},{9,11},{10,... | collective-permute-start | bytes 393224 | tf_op jit(solution)/shard_map/ppermute | solution.py:356
  5.6 8.2 %collective-permute-start.1 = (bf16[512,128]{1,0:T(8,128)(2,1)}, bf16[512,128]{1,0:T(8,128)(2,1)S(1)}, u32[]{:S(2)}, u32[]{:S(2)}) collective-permute-start(bf16[512,128]{1,0:T(8,128)(2,1)} %bitcast.11), channel_id=1, source_target_pairs={{0,1},{1,0},{2,3},{3,2},{4,5},{5,4},{6,7},{7,6},{8,9},{9,8},{10,11... | collective-permute-start | bytes 393224 | tf_op jit(solution)/shard_map/ppermute | solution.py:356
  7.1 59.2 %collective-permute-start = (bf16[512,1024]{1,0:T(8,128)(2,1)}, bf16[512,1024]{1,0:T(8,128)(2,1)S(1)}, u32[]{:S(2)}, u32[]{:S(2)}) collective-permute-start(bf16[512,1024]{1,0:T(8,128)(2,1)} %bitcast.7), channel_id=1, source_target_pairs={{0,8},{8,0},{1,9},{9,1},{2,10},{10,2},{3,11},{11,3},{4,12},{12,4},... | collective-permute-start | bytes 3145736 | tf_op jit(solution)/shard_map/ppermute | solution.py:359
  11.8 8.1 %collective-permute-start.6 = (bf16[512,128]{1,0:T(8,128)(2,1)S(1)}, bf16[512,128]{1,0:T(8,128)(2,1)S(1)}, u32[]{:S(2)}, u32[]{:S(2)}) collective-permute-start(bf16[512,128]{1,0:T(8,128)(2,1)S(1)} %collective-permute-done.3.refs_2_), channel_id=1, source_target_pairs={{0,1},{1,0},{2,3},{3,2},{4,5},{5,4},{6,7},{7,6},{8,9},{9,8},{10,11... | collective-permute-start | bytes 393224 | tf_op jit(solution)/shard_map/ppermute | solution.py:356
  12.9 8.3 %collective-permute-start.5 = (bf16[512,128]{1,0:T(8,128)(2,1)S(1)}, bf16[512,128]{1,0:T(8,128)(2,1)S(1)}, u32[]{:S(2)}, u32[]{:S(2)}) collective-permute-start(bf16[512,128]{1,0:T(8,128)(2,1)S(1)} %collective-permute-done.2.refs_1_), channel_id=1, source_target_pairs={{0,1},{1,0},{2,3},{3,2},{4,5},{5,4},{6,7},{7,6},{8,9},{9,8},{10,11... | collective-permute-start | bytes 393224 | tf_op jit(solution)/shard_map/ppermute | solution.py:356
  13.9 12.7 %collective-permute-start.10 = (bf16[512,128]{1,0:T(8,128)(2,1)S(1)}, bf16[512,128]{1,0:T(8,128)(2,1)S(1)}, u32[]{:S(2)}, u32[]{:S(2)}) collective-permute-start(bf16[512,128]{1,0:T(8,128)(2,1)S(1)} %collective-permute-done.3.refs_2_), channel_id=1, source_target_pairs={{0,2},{1,3},{2,0},{3,1},{4,6},{5,7},{6,4},{7,5},{8,10},{9,11},{10,... | collective-permute-start | bytes 393224 | tf_op jit(solution)/shard_map/ppermute | solution.py:356
  19.9 7.6 %collective-permute-start.9 = (bf16[512,128]{1,0:T(8,128)(2,1)S(1)}, bf16[512,128]{1,0:T(8,128)(2,1)S(1)}, u32[]{:S(2)}, u32[]{:S(2)}) collective-permute-start(bf16[512,128]{1,0:T(8,128)(2,1)S(1)} %collective-permute-done.6.refs_1_), channel_id=1, source_target_pairs={{0,2},{1,3},{2,0},{3,1},{4,6},{5,7},{6,4},{7,5},{8,10},{9,11},{10,... | collective-permute-start | bytes 393224 | tf_op jit(solution)/shard_map/ppermute | solution.py:356
  25.4 7.4 %collective-permute-start.13 = (bf16[528,128]{1,0:T(8,128)(2,1)S(1)}, bf16[528,128]{1,0:T(8,128)(2,1)S(1)}, u32[]{:S(2)}, u32[]{:S(2)}) collective-permute-start(bf16[528,128]{1,0:T(8,128)(2,1)S(1)} %get-tuple-element.39.refs_2_), channel_id=1, source_target_pairs={{0,1},{1,0},{2,3},{3,2},{4,5},{5,4},{6,7},{7,6},{8,9},{9,8},{10,11... | collective-permute-start | bytes 405512 | tf_op jit(solution)/shard_map/ppermute | solution.py:356
  26.6 7.5 %collective-permute-start.7 = (bf16[528,128]{1,0:T(8,128)(2,1)S(1)}, bf16[528,128]{1,0:T(8,128)(2,1)S(1)}, u32[]{:S(2)}, u32[]{:S(2)}) collective-permute-start(bf16[528,128]{1,0:T(8,128)(2,1)S(1)} %get-tuple-element.36), channel_id=1, source_target_pairs={{0,1},{1,0},{2,3},{3,2},{4,5},{5,4},{6,7},{7,6},{8,9},{9,8},{10,11... | collective-permute-start | bytes 405512 | tf_op jit(solution)/shard_map/ppermute | solution.py:356
  31.6 5.9 %collective-permute-start.11 = (bf16[528,128]{1,0:T(8,128)(2,1)S(1)}, bf16[528,128]{1,0:T(8,128)(2,1)S(1)}, u32[]{:S(2)}, u32[]{:S(2)}) collective-permute-start(bf16[528,128]{1,0:T(8,128)(2,1)S(1)} %get-tuple-element.41), channel_id=1, source_target_pairs={{0,1},{1,0},{2,3},{3,2},{4,5},{5,4},{6,7},{7,6},{8,9},{9,8},{10,11... | collective-permute-start | bytes 405512 | tf_op jit(solution)/shard_map/ppermute | solution.py:356
  32.8 6.5 %collective-permute-start.4 = (bf16[528,128]{1,0:T(8,128)(2,1)S(1)}, bf16[528,128]{1,0:T(8,128)(2,1)S(1)}, u32[]{:S(2)}, u32[]{:S(2)}) collective-permute-start(bf16[528,128]{1,0:T(8,128)(2,1)S(1)} %get-tuple-element.35.refs_2_), channel_id=1, source_target_pairs={{0,1},{1,0},{2,3},{3,2},{4,5},{5,4},{6,7},{7,6},{8,9},{9,8},{10,11... | collective-permute-start | bytes 405512 | tf_op jit(solution)/shard_map/ppermute | solution.py:356
  34.1 13.9 %collective-permute-start.14 = (bf16[528,128]{1,0:T(8,128)(2,1)S(1)}, bf16[528,128]{1,0:T(8,128)(2,1)S(1)}, u32[]{:S(2)}, u32[]{:S(2)}) collective-permute-start(bf16[528,128]{1,0:T(8,128)(2,1)S(1)} %shard_map.98.refs_2_), channel_id=1, source_target_pairs={{0,2},{1,3},{2,0},{3,1},{4,6},{5,7},{6,4},{7,5},{8,10},{9,11},{10,... | collective-permute-start | bytes 405512 | tf_op jit(solution)/shard_map/ppermute | solution.py:356
  37.6 10.6 %collective-permute-start.8 = (bf16[528,128]{1,0:T(8,128)(2,1)S(1)}, bf16[528,128]{1,0:T(8,128)(2,1)S(1)}, u32[]{:S(2)}, u32[]{:S(2)}) collective-permute-start(bf16[528,128]{1,0:T(8,128)(2,1)S(1)} %shard_map.95.refs_0_), channel_id=1, source_target_pairs={{0,4},{1,5},{2,6},{3,7},{4,0},{5,1},{6,2},{7,3},{8,12},{9,13},{10,... | collective-permute-start | bytes 405512 | tf_op jit(solution)/shard_map/ppermute | solution.py:356
  39.3 8.8 %collective-permute-start.12 = (bf16[528,128]{1,0:T(8,128)(2,1)S(1)}, bf16[528,128]{1,0:T(8,128)(2,1)S(1)}, u32[]{:S(2)}, u32[]{:S(2)}) collective-permute-start(bf16[528,128]{1,0:T(8,128)(2,1)S(1)} %shard_map.97.refs_1_), channel_id=1, source_target_pairs={{0,6},{1,7},{2,4},{3,5},{4,2},{5,3},{6,0},{7,1},{8,14},{9,15},{10,... | collective-permute-start | bytes 405512 | tf_op jit(solution)/shard_map/ppermute | solution.py:356
  48.0 23.0 %copy-start.1 = (bf16[8,64,1024]{2,1,0:T(8,128)(2,1)S(1)}, bf16[8,64,1024]{2,1,0:T(8,128)(2,1)}, u32[]{:S(2)}) copy-start(bf16[8,64,1024]{2,1,0:T(8,128)(2,1)} %param.17) | copy-start | bytes 3145732
  52.4 6.8 %collective-permute-start.20 = (bf16[64,1152]{1,0:T(8,128)(2,1)S(1)}, bf16[64,1152]{1,0:T(8,128)(2,1)S(1)}, u32[]{:S(2)}, u32[]{:S(2)}) collective-permute-start(bf16[64,1152]{1,0:T(8,128)(2,1)S(1)} %get-tuple-element.48), channel_id=1, source_target_pairs={{0,1},{1,0},{2,3},{3,2},{4,5},{5,4},{6,7},{7,6},{8,9},{9,8},{10,11... | collective-permute-start | bytes 442376 | tf_op jit(solution)/shard_map/ppermute | solution.py:356
  53.9 8.4 %collective-permute-start.18 = (bf16[64,1152]{1,0:T(8,128)(2,1)S(1)}, bf16[64,1152]{1,0:T(8,128)(2,1)S(1)}, u32[]{:S(2)}, u32[]{:S(2)}) collective-permute-start(bf16[64,1152]{1,0:T(8,128)(2,1)S(1)} %get-tuple-element.46), channel_id=1, source_target_pairs={{0,1},{1,0},{2,3},{3,2},{4,5},{5,4},{6,7},{7,6},{8,9},{9,8},{10,11... | collective-permute-start | bytes 442376 | tf_op jit(solution)/shard_map/ppermute | solution.py:356
  54.5 9.5 %collective-permute-start.16 = (bf16[64,1152]{1,0:T(8,128)(2,1)S(1)}, bf16[64,1152]{1,0:T(8,128)(2,1)S(1)}, u32[]{:S(2)}, u32[]{:S(2)}) collective-permute-start(bf16[64,1152]{1,0:T(8,128)(2,1)S(1)} %get-tuple-element.44), channel_id=1, source_target_pairs={{0,1},{1,0},{2,3},{3,2},{4,5},{5,4},{6,7},{7,6},{8,9},{9,8},{10,11... | collective-permute-start | bytes 442376 | tf_op jit(solution)/shard_map/ppermute | solution.py:356
  55.9 10.3 %collective-permute-start.22 = (bf16[64,1152]{1,0:T(8,128)(2,1)S(1)}, bf16[64,1152]{1,0:T(8,128)(2,1)S(1)}, u32[]{:S(2)}, u32[]{:S(2)}) collective-permute-start(bf16[64,1152]{1,0:T(8,128)(2,1)S(1)} %get-tuple-element.50), channel_id=1, source_target_pairs={{0,1},{1,0},{2,3},{3,2},{4,5},{5,4},{6,7},{7,6},{8,9},{9,8},{10,11... | collective-permute-start | bytes 442376 | tf_op jit(solution)/shard_map/ppermute | solution.py:356
  59.4 7.8 %collective-permute-start.21 = (bf16[64,1152]{1,0:T(8,128)(2,1)S(1)}, bf16[64,1152]{1,0:T(8,128)(2,1)S(1)}, u32[]{:S(2)}, u32[]{:S(2)}) collective-permute-start(bf16[64,1152]{1,0:T(8,128)(2,1)S(1)} %shard_map.103), channel_id=1, source_target_pairs={{0,4},{1,5},{2,6},{3,7},{4,0},{5,1},{6,2},{7,3},{8,12},{9,13},{10,... | collective-permute-start | bytes 442376 | tf_op jit(solution)/shard_map/ppermute | solution.py:356
  62.4 7.1 %collective-permute-start.19 = (bf16[64,1152]{1,0:T(8,128)(2,1)S(1)}, bf16[64,1152]{1,0:T(8,128)(2,1)S(1)}, u32[]{:S(2)}, u32[]{:S(2)}) collective-permute-start(bf16[64,1152]{1,0:T(8,128)(2,1)S(1)} %shard_map.102), channel_id=1, source_target_pairs={{0,6},{1,7},{2,4},{3,5},{4,2},{5,3},{6,0},{7,1},{8,14},{9,15},{10,... | collective-permute-start | bytes 442376 | tf_op jit(solution)/shard_map/ppermute | solution.py:356
  64.1 6.8 %collective-permute-start.17 = (bf16[64,1152]{1,0:T(8,128)(2,1)S(1)}, bf16[64,1152]{1,0:T(8,128)(2,1)S(1)}, u32[]{:S(2)}, u32[]{:S(2)}) collective-permute-start(bf16[64,1152]{1,0:T(8,128)(2,1)S(1)} %shard_map.101), channel_id=1, source_target_pairs={{0,2},{1,3},{2,0},{3,1},{4,6},{5,7},{6,4},{7,5},{8,10},{9,11},{10,... | collective-permute-start | bytes 442376 | tf_op jit(solution)/shard_map/ppermute | solution.py:356
  (4 other events, 39.5 us)

commit v5 on v4

--- a/solution.py
+++ b/solution.py
@@ -36,7 +36,7 @@
     return lax.broadcasted_iota(jnp.int32, shape, dim)
 
 
-def attend_part(heads, scale, q, lengths, keys, values, first_tile, o_ref):
+def attend_part(heads, scale, q, lengths, begin, keys, values, first_tile, o_ref):
     rows, positions = keys.shape[0], keys.shape[1]
     per_tile = TILE // heads
     tiles = rows // per_tile
@@ -47,7 +47,7 @@
     for g in range(tiles):
         bound = jnp.zeros((TILE, positions), jnp.int32)
         for a in range(per_tile):
-            bound = jnp.where(owner == a, lengths[(first_tile + g) * per_tile + a], bound)
+            bound = jnp.where(owner == a, lengths[(first_tile + g) * per_tile + a] - begin, bound)
         live.append(bound)
         left = q[g * TILE : (g + 1) * TILE, :]
         zero = jnp.zeros_like(left)
@@ -86,6 +86,7 @@
     k_buf, v_buf, k_sem, v_sem = refs[-4:]
     size = k_hbm.shape[0] // blocks
     many = size * heads
+    begin = me * k_hbm.shape[2]
     copies = []
     for j in range(n):
         kv = lax.div((me ^ which[j]) * heads, group)
@@ -107,7 +108,7 @@
             copies[i][0].wait()
             copies[i][1].wait()
             stat = stat + attend_part(
-                heads, scale, q_refs[j][b * many : (b + 1) * many, :], len_ref, k_buf.at[i], v_buf.at[i],
+                heads, scale, q_refs[j][b * many : (b + 1) * many, :], len_ref, begin, k_buf.at[i], v_buf.at[i],
                 b * many // TILE, o_refs[j],
             )
         o_refs[j][many * blocks :, :] = stat.astype(BF16)
@@ -231,8 +232,8 @@
 def project_body(n_parts, blocks, heads, rank, *refs):
     parts = refs[:n_parts]
     w_ref, slot_ref, down_a, down_b = refs[n_parts : n_parts + 4]
-    outs = refs[n_parts + 4 : -2]
-    att_ref, att32 = refs[-2:]
+    outs = refs[n_parts + 4 : n_parts + 4 + len(blocks)]
+    att_ref, shrink_ref, _, att32 = refs[n_parts + 4 + len(blocks) :]
     me, mine = lax.axis_index("tensor"), lax.axis_index("dp")
     finish_attention(parts, att32, att_ref, heads)
     att = att_ref[...]
@@ -244,33 +245,67 @@
     s = chosen(slots - mine * per, own, rank) + chosen(slots - (1 - mine) * per, other, rank)
     s = s + pltpu.roll(s, rank, 1)
     high, mid = split2(s)
-    shrink = jnp.where(iota(s.shape, 1) < rank, high, mid)
+    shrink = jnp.where(iota(s.shape, 1) < rank, high, mid).astype(BF16)
+    shrink_ref[...] = shrink
     for k, out in enumerate(outs):
-        cols = out.shape[1] - LANES
+        cols = outs[-1].shape[1]
         at = pl.ds(pl.multiple_of((me ^ blocks[k]) * cols, cols), cols)
-        out[:, :cols] = jnp.dot(att, w_ref[:, at], preferred_element_type=F32).astype(out.dtype)
-        out[:, cols:] = shrink.astype(out.dtype)
+        out[:, :cols] = jnp.dot(att, w_ref[:, at], preferred_element_type=F32).astype(BF16)
+        if k == 0:
+            out[:, cols:] = shrink
 
 
 def project(blocks, parts, weight, slots, down_a, down_b, heads, rank, cols):
-    n_out = len(blocks)
     rows = slots.shape[0]
     width = weight.shape[0]
     vmem = pl.BlockSpec(memory_space=pltpu.VMEM)
     return pl.pallas_call(
         functools.partial(project_body, len(parts), blocks, heads, rank),
         in_specs=[vmem] * (len(parts) + 4),
-        out_specs=[vmem] * n_out,
+        out_specs=[vmem] * (len(blocks) + 3),
         out_shape=[
-            jax.ShapeDtypeStruct((rows, cols + LANES), BF16 if k < n_out // 2 else F32)
-            for k in range(n_out)
+            jax.ShapeDtypeStruct((rows, cols + LANES if k == 0 else cols), BF16)
+            for k in range(len(blocks))
+        ]
+        + [
+            jax.ShapeDtypeStruct((rows, width), BF16),
+            jax.ShapeDtypeStruct((rows, LANES), BF16),
+            pltpu.VMEM(weight.shape, BF16),
         ],
-        scratch_shapes=[pltpu.VMEM((rows, width), BF16), pltpu.VMEM((rows * heads, LANES), F32)],
+        input_output_aliases={len(parts): len(blocks) + 2},
+        scratch_shapes=[pltpu.VMEM((rows * heads, LANES), F32)],
         compiler_params=pltpu.CompilerParams(vmem_limit_bytes=SMALL),
         cost_estimate=pl.CostEstimate(
-            flops=2 * rows * width * cols * n_out, bytes_accessed=2 * width * cols * n_out, transcendentals=0
+            flops=2 * rows * width * cols * len(blocks),
+            bytes_accessed=2 * width * cols * len(blocks),
+            transcendentals=0,
         ),
     )(*parts, weight, slots, down_a, down_b)
+
+
+def project_more_body(blocks, kinds, w_ref, att_ref, *outs):
+    me = lax.axis_index("tensor")
+    for k, out in zip(blocks, outs):
+        cols = out.shape[1]
+        at = pl.ds(pl.multiple_of((me ^ k) * cols, cols), cols)
+        out[...] = jnp.dot(att_ref[...], w_ref[:, at], preferred_element_type=F32).astype(out.dtype)
+
+
+def project_more(blocks, kinds, att, weight, cols):
+    rows, width = att.shape
+    vmem = pl.BlockSpec(memory_space=pltpu.VMEM)
+    return pl.pallas_call(
+        functools.partial(project_more_body, blocks, kinds),
+        in_specs=[vmem, vmem],
+        out_specs=[vmem] * len(blocks),
+        out_shape=[jax.ShapeDtypeStruct((rows, cols), kind) for kind in kinds],
+        compiler_params=pltpu.CompilerParams(vmem_limit_bytes=SMALL),
+        cost_estimate=pl.CostEstimate(
+            flops=2 * rows * width * cols * len(blocks),
+            bytes_accessed=2 * width * cols * len(blocks),
+            transcendentals=0,
+        ),
+    )(weight, att)
 
 
 def shrink_sum(parts, rank):
@@ -278,21 +313,21 @@
     return both + pltpu.roll(both, rank, 1)
 
 
-def add_body(rank, a_ref, b_ref, o_ref):
-    cols = a_ref.shape[1] - LANES
-    o_ref[:, :cols] = (a_ref[:, :cols] + b_ref[:, :cols].astype(F32)).astype(BF16)
-    s = shrink_sum([a_ref[:, cols:], b_ref[:, cols:].astype(F32)], rank)
+def add_body(rank, a_ref, b_ref, mine_ref, first_ref, o_ref):
+    cols = a_ref.shape[1]
+    o_ref[:, :cols] = (a_ref[...] + b_ref[:, :cols].astype(F32)).astype(BF16)
+    s = shrink_sum([mine_ref[...].astype(F32), first_ref[:, cols:].astype(F32)], rank)
     high, mid = split2(s)
     o_ref[:, cols:] = jnp.where(iota(s.shape, 1) < rank, high, mid).astype(BF16)
 
 
-def add(a, b, rank):
+def add(a, b, mine, first, rank):
     return pl.pallas_call(
         functools.partial(add_body, rank),
-        out_shape=jax.ShapeDtypeStruct(a.shape, BF16),
+        out_shape=jax.ShapeDtypeStruct(first.shape, BF16),
         compiler_params=pltpu.CompilerParams(vmem_limit_bytes=SMALL),
         cost_estimate=pl.CostEstimate(flops=a.size, bytes_accessed=8 * a.size, transcendentals=0),
-    )(a, b)
+    )(a, b, mine, first)
 
 
 def expanded(rel, shrink, rank, width):
@@ -365,7 +400,7 @@
     up_a = adapter_up_weight.reshape(slots_here * rank, cols)
     down_b, up_b = across(down_a), across(up_a)
 
-    live = jnp.clip(cache_live_length - me * positions, 0, positions).astype(jnp.int32)
+    live = cache_live_length.astype(jnp.int32)
     scale = 1.0 / math.sqrt(width)
     keys, values, weight = (
         pltpu.with_memory_space_constraint(x, pltpu.HBM)
@@ -395,12 +430,19 @@
     slot = jnp.sum(jnp.where(match, adapter_slot_index[None, :], 0), axis=1)
     slots = jnp.broadcast_to(slot[:, None], (rows, LANES)).astype(jnp.int32)
 
-    blocks = [k ^ 1 for k in outer] + list(outer)
     weight = load(weight, [merged[k] for k in far])
-    outs = project(blocks, parts, weight, slots, down_a, down_b, heads, rank, cols)
-    first, own = outs[: len(outer)], outs[len(outer) :]
-    arrived = [hop(x, 1) for x in first]
-    summed = [add(a, b, rank) for a, b in zip(own, arrived)]
+    order = far + [0]
+    ahead = 2
+    pairs = [k ^ 1 for k in order]
+    *first, att, shrink, weight = project(
+        pairs[:ahead], parts, weight, slots, down_a, down_b, heads, rank, cols
+    )
+    rest = pairs[ahead:] + order
+    kinds = [BF16] * (len(pairs) - ahead) + [F32] * len(order)
+    more = project_more(rest, kinds, att, weight, cols)
+    out = dict(zip(pairs + order, first + list(more)))
+    arrived = {k: hop(out[k ^ 1], 1) for k in outer}
+    summed = [add(out[k], arrived[k], shrink, arrived[order[0]], rank) for k in outer]
     final = [hop(x, k) if k else x for x, k in zip(summed, outer)]
     return last(slots, up_a, up_b, final, rank)
 

time: 72.2 us -> 70.1 us (0.971)
  waiting for transfers between devices: 9.65 us -> 7.73 us
    pallas_call x0 -> x1, Pallas kernels: none -> 2.29 us  [project_more(): pl.pallas_call(functools.partial(project_more_body, blocks, kinds), in_sp...]
    pallas_call x1, Pallas kernels: 4.22 us -> 2.02 us  [project(): pl.pallas_call(functools.partial(project_body, len(parts), blocks, heads,...]
    ppermute x21, waiting for transfers between devices: 9.65 us -> 7.72 us  [hop(): return lax.ppermute(x, 'tensor', [(i, i ^ k) for i in range(tensor)])]
    unnamed x10 -> x12, local copies, waits for them, and re-layouts: 0.93 us -> 1.61 us
  transfers between devices with their start and end apart: 23 -> 23, of which waited for: 6 -> 5; matrix products, arithmetic and copies ran while one was open for 1% -> 0% of each run, Pallas kernels for 40% -> 41%
where the time goes in v5:
time: 70.1 us; the launch traced here: 69.9 us
  starting transfers between devices  30.4 us (43%)
  Pallas kernels  29.8 us (43%)
  waiting for transfers between devices  7.73 us (11%)
  local copies, waits for them, and re-layouts  1.69 us (2%)
    ppermute x21, starting transfers between devices, hop(): return lax.ppermute(x, 'tensor', [(i, i ^ k) for i in range(tensor)])  30 us
    pallas_call x4, Pallas kernels, attend(): pl.pallas_call(functools.partial(attend_body, which, group, blocks, heads...  16.6 us
    ppermute x21, waiting for transfers between devices, hop(): return lax.ppermute(x, 'tensor', [(i, i ^ k) for i in range(tensor)])  7.72 us
    pallas_call x1, Pallas kernels, load(): pl.pallas_call(functools.partial(load_body, blocks), in_specs=[pl.BlockSp...  5.96 us
    pallas_call x1, Pallas kernels, project_more(): pl.pallas_call(functools.partial(project_more_body, blocks, kinds), in_sp...  2.29 us
    pallas_call x1, Pallas kernels, project(): pl.pallas_call(functools.partial(project_body, len(parts), blocks, heads,...  2.02 us
    unnamed x12, local copies, waits for them, and re-layouts  1.61 us
  transfers between devices with their start and end apart: 23, of which 5 were waited for; matrix products, arithmetic and copies ran while one was open for 0% of the time, Pallas kernels for 41%

profile of v5, /device:TPU:0, one launch (start us, length us, event | category | flops | bytes accessed | tf_op | source)
XLA Modules:
  0.0 69.9 jit_solution(17799653771304328612)
XLA Ops:
  0.5 3.6 %collective-permute-start.3 = (bf16[512,128]{1,0:T(8,128)(2,1)}, bf16[512,128]{1,0:T(8,128)(2,1)S(1)}, u32[]{:S(2)}, u32[]{:S(2)}) collective-permute-start(bf16[512,128]{1,0:T(8,128)(2,1)} %bitcast.9), channel_id=1, source_target_pairs={{0,4},{1,5},{2,6},{3,7},{4,0},{5,1},{6,2},{7,3},{8,12},{9,13},{10,... | collective-permute-start | bytes 393224 | tf_op jit(solution)/shard_map/ppermute | solution.py:391
  4.0 1.6 %collective-permute-start.2 = (bf16[512,128]{1,0:T(8,128)(2,1)}, bf16[512,128]{1,0:T(8,128)(2,1)S(1)}, u32[]{:S(2)}, u32[]{:S(2)}) collective-permute-start(bf16[512,128]{1,0:T(8,128)(2,1)} %bitcast.10), channel_id=1, source_target_pairs={{0,2},{1,3},{2,0},{3,1},{4,6},{5,7},{6,4},{7,5},{8,10},{9,11},{10,... | collective-permute-start | bytes 393224 | tf_op jit(solution)/shard_map/ppermute | solution.py:391
  5.6 1.5 %collective-permute-start.1 = (bf16[512,128]{1,0:T(8,128)(2,1)}, bf16[512,128]{1,0:T(8,128)(2,1)S(1)}, u32[]{:S(2)}, u32[]{:S(2)}) collective-permute-start(bf16[512,128]{1,0:T(8,128)(2,1)} %bitcast.11), channel_id=1, source_target_pairs={{0,1},{1,0},{2,3},{3,2},{4,5},{5,4},{6,7},{7,6},{8,9},{9,8},{10,11... | collective-permute-start | bytes 393224 | tf_op jit(solution)/shard_map/ppermute | solution.py:391
  8.7 3.0 %shard_map.91.refs_3_.a_ref = bf16[528,128]{1,0:T(8,128)(2,1)S(1)} custom-call(s32[64]{0:T(128)S(1)} %copy-done.3, bf16[64,8,96,128]{3,2,1,0:T(8,128)(2,1)} %k_hbm.7, bf16[64,8,96,128]{3,2,1,0:T(8,128)(2,1)} %v_hbm.7, bf16[512,128]{1,0:T(8,128)(2,1)S(1)} %bitcast.12), custom_call_target="tpu_custom_call" | custom-call | flops 201326592 | bytes 3145728 | tf_op jit(solution)/shard_map/pallas_call | solution.py:126
  14.5 5.3 %shard_map.92 = (bf16[528,128]{1,0:T(8,128)(2,1)S(1)}, bf16[528,128]{1,0:T(8,128)(2,1)S(1)}, bf16[528,128]{1,0:T(8,128)(2,1)S(1)}) custom-call(s32[64]{0:T(128)S(1)} %copy-done.3, bf16[64,8,96,128]{3,2,1,0:T(8,128)(2,1)} %k_hbm.7, bf16[64,8,96,128]{3,2,1,0:T(8,128)(2,1)} %v_hbm.7, bf16[512,128]{1,0:T(8,128)(2,1)S(1)} %collective-permute-done.1.refs_0_, ...), custom_call_target="tpu_custom_call" | custom-call | flops 603979776 | bytes 9437184 | tf_op jit(solution)/shard_map/pallas_call | solution.py:126
  19.9 1.3 %collective-permute-start.9 = (bf16[512,128]{1,0:T(8,128)(2,1)S(1)}, bf16[512,128]{1,0:T(8,128)(2,1)S(1)}, u32[]{:S(2)}, u32[]{:S(2)}) collective-permute-start(bf16[512,128]{1,0:T(8,128)(2,1)S(1)} %collective-permute-done.6.refs_1_), channel_id=1, source_target_pairs={{0,2},{1,3},{2,0},{3,1},{4,6},{5,7},{6,4},{7,5},{8,10},{9,11},{10,... | collective-permute-start | bytes 393224 | tf_op jit(solution)/shard_map/ppermute | solution.py:391
  21.2 4.1 %shard_map.94 = (bf16[528,128]{1,0:T(8,128)(2,1)S(1)}, bf16[528,128]{1,0:T(8,128)(2,1)S(1)}) custom-call(s32[64]{0:T(128)S(1)} %copy-done.3, bf16[64,8,96,128]{3,2,1,0:T(8,128)(2,1)} %k_hbm.7, bf16[64,8,96,128]{3,2,1,0:T(8,128)(2,1)} %v_hbm.7, bf16[512,128]{1,0:T(8,128)(2,1)S(1)} %collective-permute-done.5.refs_0_, ...), custom_call_target="tpu_custom_call" | custom-call | flops 402653184 | bytes 6291456 | tf_op jit(solution)/shard_map/pallas_call | solution.py:126
  25.4 1.2 %collective-permute-start.13 = (bf16[528,128]{1,0:T(8,128)(2,1)S(1)}, bf16[528,128]{1,0:T(8,128)(2,1)S(1)}, u32[]{:S(2)}, u32[]{:S(2)}) collective-permute-start(bf16[528,128]{1,0:T(8,128)(2,1)S(1)} %get-tuple-element.42.refs_2_), channel_id=1, source_target_pairs={{0,1},{1,0},{2,3},{3,2},{4,5},{5,4},{6,7},{7,6},{8,9},{9,8},{10,11... | collective-permute-start | bytes 405512 | tf_op jit(solution)/shard_map/ppermute | solution.py:391
  27.5 4.1 %shard_map.96 = (bf16[528,128]{1,0:T(8,128)(2,1)S(1)}, bf16[528,128]{1,0:T(8,128)(2,1)S(1)}) custom-call(s32[64]{0:T(128)S(1)} %copy-done.3, bf16[64,8,96,128]{3,2,1,0:T(8,128)(2,1)} %k_hbm.7, bf16[64,8,96,128]{3,2,1,0:T(8,128)(2,1)} %v_hbm.7, bf16[512,128]{1,0:T(8,128)(2,1)S(1)} %collective-permute-done.9.refs_0_, ...), custom_call_target="tpu_custom_call" | custom-call | flops 402653184 | bytes 6291456 | tf_op jit(solution)/shard_map/pallas_call | solution.py:126
  35.4 1.9 %collective-permute-done.11.b_ref = bf16[528,128]{1,0:T(8,128)(2,1)S(1)} collective-permute-done((bf16[528,128]{1,0:T(8,128)(2,1)S(1)}, bf16[528,128]{1,0:T(8,128)(2,1)S(1)}, u32[]{:S(2)}, u32[]{:S(2)}) %collective-permute-start.11) | collective-permute-done | bytes 135200 | tf_op jit(solution)/shard_map/ppermute | solution.py:391
  37.3 1.6 %collective-permute-start.8 = (bf16[528,128]{1,0:T(8,128)(2,1)S(1)}, bf16[528,128]{1,0:T(8,128)(2,1)S(1)}, u32[]{:S(2)}, u32[]{:S(2)}) collective-permute-start(bf16[528,128]{1,0:T(8,128)(2,1)S(1)} %shard_map.95.refs_0_), channel_id=1, source_target_pairs={{0,4},{1,5},{2,6},{3,7},{4,0},{5,1},{6,2},{7,3},{8,12},{9,13},{10,... | collective-permute-start | bytes 405512 | tf_op jit(solution)/shard_map/ppermute | solution.py:391
  39.3 2.3 %collective-permute-start.12 = (bf16[528,128]{1,0:T(8,128)(2,1)S(1)}, bf16[528,128]{1,0:T(8,128)(2,1)S(1)}, u32[]{:S(2)}, u32[]{:S(2)}) collective-permute-start(bf16[528,128]{1,0:T(8,128)(2,1)S(1)} %shard_map.97.refs_1_), channel_id=1, source_target_pairs={{0,6},{1,7},{2,4},{3,5},{4,2},{5,3},{6,0},{7,1},{8,14},{9,15},{10,... | collective-permute-start | bytes 405512 | tf_op jit(solution)/shard_map/ppermute | solution.py:391
  42.0 6.0 %shard_map.99.refs_4_ = bf16[1024,8192]{1,0:T(8,128)(2,1)S(1)} custom-call(bf16[1024,8192]{1,0:T(8,128)(2,1)} %source.1, bf16[528,128]{1,0:T(8,128)(2,1)S(1)} %shard_map.95.refs_0_, bf16[528,128]{1,0:T(8,128)(2,1)S(1)} %shard_map.97.refs_1_, bf16[528,128]{1,0:T(8,128)(2,1)S(1)} %shard_map.98.refs_2_), custom_call_target="tpu_custom_call" | custom-call | bytes 16777216 | tf_op jit(solution)/shard_map/pallas_call | solution.py:156
  48.1 2.0 %shard_map.100 = (bf16[64,1152]{1,0:T(8,128)(2,1)S(1)}, bf16[64,1024]{1,0:T(8,128)(2,1)S(1)}, bf16[64,1024]{1,0:T(8,128)(2,1)S(1)}, bf16[64,128]{1,0:T(8,128)(2,1)S(1)}, bf16[1024,8192]{1,0:T(8,128)(2,1)S(1)}) custom-call(bf16[528,128]{1,0:T(8,128)(2,1)S(1)} %shard_map.93.refs_0_, ...), custom_call_target="tpu_custom_call", output_to_operand_aliasing={{4}: (4, {})} | custom-call | flops 268435456 | bytes 4194304 | tf_op jit(solution)/shard_map/pallas_call | solution.py:262
  50.1 1.6 %collective-permute-start.17 = (bf16[64,1152]{1,0:T(8,128)(2,1)S(1)}, bf16[64,1152]{1,0:T(8,128)(2,1)S(1)}, u32[]{:S(2)}, u32[]{:S(2)}) collective-permute-start(bf16[64,1152]{1,0:T(8,128)(2,1)S(1)} %get-tuple-element.51), channel_id=1, source_target_pairs={{0,1},{1,0},{2,3},{3,2},{4,5},{5,4},{6,7},{7,6},{8,9},{9,8},{10,11... | collective-permute-start | bytes 442376 | tf_op jit(solution)/shard_map/ppermute | solution.py:391
  52.2 2.3 %shard_map.101 = (bf16[64,1024]{1,0:T(8,128)(2,1)S(1)}, bf16[64,1024]{1,0:T(8,128)(2,1)S(1)}, f32[64,1024]{1,0:T(8,128)S(1)}, f32[64,1024]{1,0:T(8,128)S(1)}, f3...) custom-call(bf16[1024,8192]{1,0:T(8,128)(2,1)S(1)} %get-tuple-element.46.w_ref, bf16[64,1024]{1,0:T(8,128)(2,1)S(1)} %get-tuple-element.47.att_ref), custom_call_target="tpu_custom_call" | custom-call | flops 805306368 | bytes 12582912 | tf_op jit(solution)/shard_map/pallas_call | solution.py:297
  54.5 1.6 %collective-permute-start.16 = (bf16[64,1024]{1,0:T(8,128)(2,1)S(1)}, bf16[64,1024]{1,0:T(8,128)(2,1)S(1)}, u32[]{:S(2)}, u32[]{:S(2)}) collective-permute-start(bf16[64,1024]{1,0:T(8,128)(2,1)S(1)} %get-tuple-element.49), channel_id=1, source_target_pairs={{0,1},{1,0},{2,3},{3,2},{4,5},{5,4},{6,7},{7,6},{8,9},{9,8},{10,11... | collective-permute-start | bytes 393224 | tf_op jit(solution)/shard_map/ppermute | solution.py:391
  56.8 2.4 %collective-permute-start.21 = (bf16[64,1152]{1,0:T(8,128)(2,1)S(1)}, bf16[64,1152]{1,0:T(8,128)(2,1)S(1)}, u32[]{:S(2)}, u32[]{:S(2)}) collective-permute-start(bf16[64,1152]{1,0:T(8,128)(2,1)S(1)} %shard_map.104), channel_id=1, source_target_pairs={{0,4},{1,5},{2,6},{3,7},{4,0},{5,1},{6,2},{7,3},{8,12},{9,13},{10,... | collective-permute-start | bytes 442376 | tf_op jit(solution)/shard_map/ppermute | solution.py:391
  59.3 1.3 %collective-permute-start.20 = (bf16[64,1152]{1,0:T(8,128)(2,1)S(1)}, bf16[64,1152]{1,0:T(8,128)(2,1)S(1)}, u32[]{:S(2)}, u32[]{:S(2)}) collective-permute-start(bf16[64,1152]{1,0:T(8,128)(2,1)S(1)} %shard_map.103), channel_id=1, source_target_pairs={{0,6},{1,7},{2,4},{3,5},{4,2},{5,3},{6,0},{7,1},{8,14},{9,15},{10,... | collective-permute-start | bytes 442376 | tf_op jit(solution)/shard_map/ppermute | solution.py:391
  60.7 1.2 %collective-permute-start.18 = (bf16[64,1152]{1,0:T(8,128)(2,1)S(1)}, bf16[64,1152]{1,0:T(8,128)(2,1)S(1)}, u32[]{:S(2)}, u32[]{:S(2)}) collective-permute-start(bf16[64,1152]{1,0:T(8,128)(2,1)S(1)} %shard_map.102), channel_id=1, source_target_pairs={{0,2},{1,3},{2,0},{3,1},{4,6},{5,7},{6,4},{7,5},{8,10},{9,11},{10,... | collective-permute-start | bytes 442376 | tf_op jit(solution)/shard_map/ppermute | solution.py:391
  62.0 1.5 %collective-permute-start.22 = (bf16[64,1024]{1,0:T(8,128)(2,1)S(1)}, bf16[64,1024]{1,0:T(8,128)(2,1)S(1)}, u32[]{:S(2)}, u32[]{:S(2)}) collective-permute-start(bf16[64,1024]{1,0:T(8,128)(2,1)S(1)} %get-tuple-element.56), channel_id=1, source_target_pairs={{0,1},{1,0},{2,3},{3,2},{4,5},{5,4},{6,7},{7,6},{8,9},{9,8},{10,11... | collective-permute-start | bytes 393224 | tf_op jit(solution)/shard_map/ppermute | solution.py:391
  63.5 3.4 %collective-permute-done.22.b_ref = bf16[64,1024]{1,0:T(8,128)(2,1)S(1)} collective-permute-done((bf16[64,1024]{1,0:T(8,128)(2,1)S(1)}, bf16[64,1024]{1,0:T(8,128)(2,1)S(1)}, u32[]{:S(2)}, u32[]{:S(2)}) %collective-permute-start.22) | collective-permute-done | bytes 131104 | tf_op jit(solution)/shard_map/ppermute | solution.py:391
  67.0 1.3 %collective-permute-done.21.refs_2_ = bf16[64,1152]{1,0:T(8,128)(2,1)S(1)} collective-permute-done((bf16[64,1152]{1,0:T(8,128)(2,1)S(1)}, bf16[64,1152]{1,0:T(8,128)(2,1)S(1)}, u32[]{:S(2)}, u32[]{:S(2)}) %collective-permute-start.21) | collective-permute-done | bytes 147488 | tf_op jit(solution)/shard_map/ppermute | solution.py:391
  68.7 1.2 %shard_map.106 = bf16[64,1024]{1,0:T(8,128)(2,1)} custom-call(s32[64,128]{1,0:T(8,128)S(1)} %broadcast_in_dim.23.refs_5_.slot_ref, bf16[512,1024]{1,0:T(8,128)(2,1)S(1)} %bitcast.8, bf16[512,1024]{1,0:T(8,128)(2,1)S(1)} %collective-permute-done.up_b, bf16[64,1152]{1,0:T(8,128)(2,1)S(1)} %collective-permute-done.18.refs_0_, ...), custom_call_target="tpu_custom_call" | custom-call | flops 2097152 | bytes 2097152 | tf_op jit(solution)/shard_map/pallas_call | solution.py:363
  (52 shorter events, 12.3 us)
Async XLA Ops:
  0.0 48.0 %collective-permute-start.15 = (bf16[512,1024]{1,0:T(8,128)(2,1)}, bf16[512,1024]{1,0:T(8,128)(2,1)S(1)}, u32[]{:S(2)}, u32[]{:S(2)}) collective-permute-start(bf16[512,1024]{1,0:T(8,128)(2,1)} %bitcast.5), channel_id=1, source_target_pairs={{0,8},{8,0},{1,9},{9,1},{2,10},{10,2},{3,11},{11,3},{4,12},{12,4},... | collective-permute-start | bytes 3145736 | tf_op jit(solution)/shard_map/ppermute | solution.py:394
  0.5 11.3 %collective-permute-start.3 = (bf16[512,128]{1,0:T(8,128)(2,1)}, bf16[512,128]{1,0:T(8,128)(2,1)S(1)}, u32[]{:S(2)}, u32[]{:S(2)}) collective-permute-start(bf16[512,128]{1,0:T(8,128)(2,1)} %bitcast.9), channel_id=1, source_target_pairs={{0,4},{1,5},{2,6},{3,7},{4,0},{5,1},{6,2},{7,3},{8,12},{9,13},{10,... | collective-permute-start | bytes 393224 | tf_op jit(solution)/shard_map/ppermute | solution.py:391
  4.0 8.9 %collective-permute-start.2 = (bf16[512,128]{1,0:T(8,128)(2,1)}, bf16[512,128]{1,0:T(8,128)(2,1)S(1)}, u32[]{:S(2)}, u32[]{:S(2)}) collective-permute-start(bf16[512,128]{1,0:T(8,128)(2,1)} %bitcast.10), channel_id=1, source_target_pairs={{0,2},{1,3},{2,0},{3,1},{4,6},{5,7},{6,4},{7,5},{8,10},{9,11},{10,... | collective-permute-start | bytes 393224 | tf_op jit(solution)/shard_map/ppermute | solution.py:391
  5.6 61.4 %collective-permute-start = (bf16[512,1024]{1,0:T(8,128)(2,1)}, bf16[512,1024]{1,0:T(8,128)(2,1)S(1)}, u32[]{:S(2)}, u32[]{:S(2)}) collective-permute-start(bf16[512,1024]{1,0:T(8,128)(2,1)} %bitcast.7), channel_id=1, source_target_pairs={{0,8},{8,0},{1,9},{9,1},{2,10},{10,2},{3,11},{11,3},{4,12},{12,4},... | collective-permute-start | bytes 3145736 | tf_op jit(solution)/shard_map/ppermute | solution.py:394
  5.6 8.3 %collective-permute-start.1 = (bf16[512,128]{1,0:T(8,128)(2,1)}, bf16[512,128]{1,0:T(8,128)(2,1)S(1)}, u32[]{:S(2)}, u32[]{:S(2)}) collective-permute-start(bf16[512,128]{1,0:T(8,128)(2,1)} %bitcast.11), channel_id=1, source_target_pairs={{0,1},{1,0},{2,3},{3,2},{4,5},{5,4},{6,7},{7,6},{8,9},{9,8},{10,11... | collective-permute-start | bytes 393224 | tf_op jit(solution)/shard_map/ppermute | solution.py:391
  11.8 8.1 %collective-permute-start.6 = (bf16[512,128]{1,0:T(8,128)(2,1)S(1)}, bf16[512,128]{1,0:T(8,128)(2,1)S(1)}, u32[]{:S(2)}, u32[]{:S(2)}) collective-permute-start(bf16[512,128]{1,0:T(8,128)(2,1)S(1)} %collective-permute-done.3.refs_2_), channel_id=1, source_target_pairs={{0,1},{1,0},{2,3},{3,2},{4,5},{5,4},{6,7},{7,6},{8,9},{9,8},{10,11... | collective-permute-start | bytes 393224 | tf_op jit(solution)/shard_map/ppermute | solution.py:391
  12.9 8.3 %collective-permute-start.5 = (bf16[512,128]{1,0:T(8,128)(2,1)S(1)}, bf16[512,128]{1,0:T(8,128)(2,1)S(1)}, u32[]{:S(2)}, u32[]{:S(2)}) collective-permute-start(bf16[512,128]{1,0:T(8,128)(2,1)S(1)} %collective-permute-done.2.refs_1_), channel_id=1, source_target_pairs={{0,1},{1,0},{2,3},{3,2},{4,5},{5,4},{6,7},{7,6},{8,9},{9,8},{10,11... | collective-permute-start | bytes 393224 | tf_op jit(solution)/shard_map/ppermute | solution.py:391
  13.9 12.7 %collective-permute-start.10 = (bf16[512,128]{1,0:T(8,128)(2,1)S(1)}, bf16[512,128]{1,0:T(8,128)(2,1)S(1)}, u32[]{:S(2)}, u32[]{:S(2)}) collective-permute-start(bf16[512,128]{1,0:T(8,128)(2,1)S(1)} %collective-permute-done.3.refs_2_), channel_id=1, source_target_pairs={{0,2},{1,3},{2,0},{3,1},{4,6},{5,7},{6,4},{7,5},{8,10},{9,11},{10,... | collective-permute-start | bytes 393224 | tf_op jit(solution)/shard_map/ppermute | solution.py:391
  19.9 7.6 %collective-permute-start.9 = (bf16[512,128]{1,0:T(8,128)(2,1)S(1)}, bf16[512,128]{1,0:T(8,128)(2,1)S(1)}, u32[]{:S(2)}, u32[]{:S(2)}) collective-permute-start(bf16[512,128]{1,0:T(8,128)(2,1)S(1)} %collective-permute-done.6.refs_1_), channel_id=1, source_target_pairs={{0,2},{1,3},{2,0},{3,1},{4,6},{5,7},{6,4},{7,5},{8,10},{9,11},{10,... | collective-permute-start | bytes 393224 | tf_op jit(solution)/shard_map/ppermute | solution.py:391
  25.4 7.4 %collective-permute-start.13 = (bf16[528,128]{1,0:T(8,128)(2,1)S(1)}, bf16[528,128]{1,0:T(8,128)(2,1)S(1)}, u32[]{:S(2)}, u32[]{:S(2)}) collective-permute-start(bf16[528,128]{1,0:T(8,128)(2,1)S(1)} %get-tuple-element.42.refs_2_), channel_id=1, source_target_pairs={{0,1},{1,0},{2,3},{3,2},{4,5},{5,4},{6,7},{7,6},{8,9},{9,8},{10,11... | collective-permute-start | bytes 405512 | tf_op jit(solution)/shard_map/ppermute | solution.py:391
  26.6 7.5 %collective-permute-start.7 = (bf16[528,128]{1,0:T(8,128)(2,1)S(1)}, bf16[528,128]{1,0:T(8,128)(2,1)S(1)}, u32[]{:S(2)}, u32[]{:S(2)}) collective-permute-start(bf16[528,128]{1,0:T(8,128)(2,1)S(1)} %get-tuple-element.39), channel_id=1, source_target_pairs={{0,1},{1,0},{2,3},{3,2},{4,5},{5,4},{6,7},{7,6},{8,9},{9,8},{10,11... | collective-permute-start | bytes 405512 | tf_op jit(solution)/shard_map/ppermute | solution.py:391
  31.6 5.7 %collective-permute-start.11 = (bf16[528,128]{1,0:T(8,128)(2,1)S(1)}, bf16[528,128]{1,0:T(8,128)(2,1)S(1)}, u32[]{:S(2)}, u32[]{:S(2)}) collective-permute-start(bf16[528,128]{1,0:T(8,128)(2,1)S(1)} %get-tuple-element.44), channel_id=1, source_target_pairs={{0,1},{1,0},{2,3},{3,2},{4,5},{5,4},{6,7},{7,6},{8,9},{9,8},{10,11... | collective-permute-start | bytes 405512 | tf_op jit(solution)/shard_map/ppermute | solution.py:391
  32.8 6.5 %collective-permute-start.4 = (bf16[528,128]{1,0:T(8,128)(2,1)S(1)}, bf16[528,128]{1,0:T(8,128)(2,1)S(1)}, u32[]{:S(2)}, u32[]{:S(2)}) collective-permute-start(bf16[528,128]{1,0:T(8,128)(2,1)S(1)} %get-tuple-element.38.refs_2_), channel_id=1, source_target_pairs={{0,1},{1,0},{2,3},{3,2},{4,5},{5,4},{6,7},{7,6},{8,9},{9,8},{10,11... | collective-permute-start | bytes 405512 | tf_op jit(solution)/shard_map/ppermute | solution.py:391
  34.1 13.9 %collective-permute-start.14 = (bf16[528,128]{1,0:T(8,128)(2,1)S(1)}, bf16[528,128]{1,0:T(8,128)(2,1)S(1)}, u32[]{:S(2)}, u32[]{:S(2)}) collective-permute-start(bf16[528,128]{1,0:T(8,128)(2,1)S(1)} %shard_map.98.refs_2_), channel_id=1, source_target_pairs={{0,2},{1,3},{2,0},{3,1},{4,6},{5,7},{6,4},{7,5},{8,10},{9,11},{10,... | collective-permute-start | bytes 405512 | tf_op jit(solution)/shard_map/ppermute | solution.py:391
  37.3 10.7 %collective-permute-start.8 = (bf16[528,128]{1,0:T(8,128)(2,1)S(1)}, bf16[528,128]{1,0:T(8,128)(2,1)S(1)}, u32[]{:S(2)}, u32[]{:S(2)}) collective-permute-start(bf16[528,128]{1,0:T(8,128)(2,1)S(1)} %shard_map.95.refs_0_), channel_id=1, source_target_pairs={{0,4},{1,5},{2,6},{3,7},{4,0},{5,1},{6,2},{7,3},{8,12},{9,13},{10,... | collective-permute-start | bytes 405512 | tf_op jit(solution)/shard_map/ppermute | solution.py:391
  39.3 8.7 %collective-permute-start.12 = (bf16[528,128]{1,0:T(8,128)(2,1)S(1)}, bf16[528,128]{1,0:T(8,128)(2,1)S(1)}, u32[]{:S(2)}, u32[]{:S(2)}) collective-permute-start(bf16[528,128]{1,0:T(8,128)(2,1)S(1)} %shard_map.97.refs_1_), channel_id=1, source_target_pairs={{0,6},{1,7},{2,4},{3,5},{4,2},{5,3},{6,0},{7,1},{8,14},{9,15},{10,... | collective-permute-start | bytes 405512 | tf_op jit(solution)/shard_map/ppermute | solution.py:391
  48.1 20.6 %copy-start.1 = (bf16[8,64,1024]{2,1,0:T(8,128)(2,1)S(1)}, bf16[8,64,1024]{2,1,0:T(8,128)(2,1)}, u32[]{:S(2)}) copy-start(bf16[8,64,1024]{2,1,0:T(8,128)(2,1)} %param.17) | copy-start | bytes 3145732
  50.1 6.6 %collective-permute-start.17 = (bf16[64,1152]{1,0:T(8,128)(2,1)S(1)}, bf16[64,1152]{1,0:T(8,128)(2,1)S(1)}, u32[]{:S(2)}, u32[]{:S(2)}) collective-permute-start(bf16[64,1152]{1,0:T(8,128)(2,1)S(1)} %get-tuple-element.51), channel_id=1, source_target_pairs={{0,1},{1,0},{2,3},{3,2},{4,5},{5,4},{6,7},{7,6},{8,9},{9,8},{10,11... | collective-permute-start | bytes 442376 | tf_op jit(solution)/shard_map/ppermute | solution.py:391
  51.7 7.6 %collective-permute-start.19 = (bf16[64,1024]{1,0:T(8,128)(2,1)S(1)}, bf16[64,1024]{1,0:T(8,128)(2,1)S(1)}, u32[]{:S(2)}, u32[]{:S(2)}) collective-permute-start(bf16[64,1024]{1,0:T(8,128)(2,1)S(1)} %get-tuple-element.53), channel_id=1, source_target_pairs={{0,1},{1,0},{2,3},{3,2},{4,5},{5,4},{6,7},{7,6},{8,9},{9,8},{10,11... | collective-permute-start | bytes 393224 | tf_op jit(solution)/shard_map/ppermute | solution.py:391
  54.5 6.2 %collective-permute-start.16 = (bf16[64,1024]{1,0:T(8,128)(2,1)S(1)}, bf16[64,1024]{1,0:T(8,128)(2,1)S(1)}, u32[]{:S(2)}, u32[]{:S(2)}) collective-permute-start(bf16[64,1024]{1,0:T(8,128)(2,1)S(1)} %get-tuple-element.49), channel_id=1, source_target_pairs={{0,1},{1,0},{2,3},{3,2},{4,5},{5,4},{6,7},{7,6},{8,9},{9,8},{10,11... | collective-permute-start | bytes 393224 | tf_op jit(solution)/shard_map/ppermute | solution.py:391
  56.8 11.5 %collective-permute-start.21 = (bf16[64,1152]{1,0:T(8,128)(2,1)S(1)}, bf16[64,1152]{1,0:T(8,128)(2,1)S(1)}, u32[]{:S(2)}, u32[]{:S(2)}) collective-permute-start(bf16[64,1152]{1,0:T(8,128)(2,1)S(1)} %shard_map.104), channel_id=1, source_target_pairs={{0,4},{1,5},{2,6},{3,7},{4,0},{5,1},{6,2},{7,3},{8,12},{9,13},{10,... | collective-permute-start | bytes 442376 | tf_op jit(solution)/shard_map/ppermute | solution.py:391
  59.3 9.0 %collective-permute-start.20 = (bf16[64,1152]{1,0:T(8,128)(2,1)S(1)}, bf16[64,1152]{1,0:T(8,128)(2,1)S(1)}, u32[]{:S(2)}, u32[]{:S(2)}) collective-permute-start(bf16[64,1152]{1,0:T(8,128)(2,1)S(1)} %shard_map.103), channel_id=1, source_target_pairs={{0,6},{1,7},{2,4},{3,5},{4,2},{5,3},{6,0},{7,1},{8,14},{9,15},{10,... | collective-permute-start | bytes 442376 | tf_op jit(solution)/shard_map/ppermute | solution.py:391
  60.7 8.0 %collective-permute-start.18 = (bf16[64,1152]{1,0:T(8,128)(2,1)S(1)}, bf16[64,1152]{1,0:T(8,128)(2,1)S(1)}, u32[]{:S(2)}, u32[]{:S(2)}) collective-permute-start(bf16[64,1152]{1,0:T(8,128)(2,1)S(1)} %shard_map.102), channel_id=1, source_target_pairs={{0,2},{1,3},{2,0},{3,1},{4,6},{5,7},{6,4},{7,5},{8,10},{9,11},{10,... | collective-permute-start | bytes 442376 | tf_op jit(solution)/shard_map/ppermute | solution.py:391
  62.0 5.0 %collective-permute-start.22 = (bf16[64,1024]{1,0:T(8,128)(2,1)S(1)}, bf16[64,1024]{1,0:T(8,128)(2,1)S(1)}, u32[]{:S(2)}, u32[]{:S(2)}) collective-permute-start(bf16[64,1024]{1,0:T(8,128)(2,1)S(1)} %get-tuple-element.56), channel_id=1, source_target_pairs={{0,1},{1,0},{2,3},{3,2},{4,5},{5,4},{6,7},{7,6},{8,9},{9,8},{10,11... | collective-permute-start | bytes 393224 | tf_op jit(solution)/shard_map/ppermute | solution.py:391
  (5 other events, 40.0 us)

commit v6 on v5

--- a/solution.py
+++ b/solution.py
@@ -173,7 +173,8 @@
     return best, weights, total
 
 
-def pair_body(a_ref, b_ref, o_ref):
+def pair_body(a_ref, b_ref, *refs):
+    o_ref = refs[-1]
     n = a_ref.shape[0] - TILE
     sa = a_ref[pl.ds(n, TILE), :].astype(F32)
     sb = b_ref[pl.ds(n, TILE), :].astype(F32)
@@ -196,13 +197,16 @@
         ).astype(BF16)
 
 
-def pair(a, b):
+def pair(a, b, *after):
+    vmem = pl.BlockSpec(memory_space=pltpu.VMEM)
     return pl.pallas_call(
         pair_body,
+        in_specs=[vmem, vmem] + [pl.BlockSpec(memory_space=pl.ANY)] * len(after),
+        out_specs=vmem,
         out_shape=jax.ShapeDtypeStruct(a.shape, BF16),
         compiler_params=pltpu.CompilerParams(vmem_limit_bytes=SMALL),
         cost_estimate=pl.CostEstimate(flops=3 * a.size, bytes_accessed=6 * a.size, transcendentals=0),
-    )(a, b)
+    )(a, b, *after)
 
 
 def finish_attention(parts, att32, att_ref, heads):
@@ -421,8 +425,10 @@
             if kind == "forward" and token:
                 source, token[0] = lax.optimization_barrier((source, token[0]))
             held[k] = hop(source, bit)
-    sent = {k: hop(partial[k ^ 1], 1) for k in [0] + far}
-    merged = {k: pair(partial[k], sent[k]) for k in [0] + far}
+    sent = {k: hop(partial[k ^ 1], 1) for k in [0, *far[1:], far[0]]}
+    merged = {}
+    for k in far + [0]:
+        merged[k] = pair(partial[k], sent[k], *([merged[far[0]]] if k == 2 and k != far[0] else []))
     parts = [merged[0]] + [hop(merged[k], k) for k in far]
 
     total_slots = adapter_slot_index.shape[0]

time: 70.1 us -> 69 us (0.984)
  starting transfers between devices: 30.4 us -> 29.5 us
    ppermute x21, starting transfers between devices: 30 us -> 29 us  [hop(): return lax.ppermute(x, 'tensor', [(i, i ^ k) for i in range(tensor)])]
    unnamed x12 -> x14, local copies, waits for them, and re-layouts: 1.61 us -> 1.62 us
  transfers between devices with their start and end apart: 23 -> 23, of which waited for: 5 -> 7; matrix products, arithmetic and copies ran while one was open for 0% -> 0% of each run, Pallas kernels for 41% -> 42%
where the time goes in v6:
time: 69 us; the launch traced here: 68.8 us
  Pallas kernels  29.8 us (43%)
  starting transfers between devices  29.5 us (43%)
  waiting for transfers between devices  7.6 us (11%)
  local copies, waits for them, and re-layouts  1.69 us (2%)
    ppermute x21, starting transfers between devices, hop(): return lax.ppermute(x, 'tensor', [(i, i ^ k) for i in range(tensor)])  29 us
    pallas_call x4, Pallas kernels, attend(): pl.pallas_call(functools.partial(attend_body, which, group, blocks, heads...  16.6 us
    ppermute x21, waiting for transfers between devices, hop(): return lax.ppermute(x, 'tensor', [(i, i ^ k) for i in range(tensor)])  7.59 us
    pallas_call x1, Pallas kernels, load(): pl.pallas_call(functools.partial(load_body, blocks), in_specs=[pl.BlockSp...  5.96 us
    pallas_call x1, Pallas kernels, project_more(): pl.pallas_call(functools.partial(project_more_body, blocks, kinds), in_sp...  2.29 us
    pallas_call x1, Pallas kernels, project(): pl.pallas_call(functools.partial(project_body, len(parts), blocks, heads,...  2.02 us
    unnamed x14, local copies, waits for them, and re-layouts  1.62 us
  transfers between devices with their start and end apart: 23, of which 7 were waited for; matrix products, arithmetic and copies ran while one was open for 0% of the time, Pallas kernels for 42%

profile of v6, /device:TPU:0, one launch (start us, length us, event | category | flops | bytes accessed | tf_op | source)
XLA Modules:
  0.0 68.8 jit_solution(7404461882626446218)
XLA Ops:
  0.5 3.6 %collective-permute-start.3 = (bf16[512,128]{1,0:T(8,128)(2,1)}, bf16[512,128]{1,0:T(8,128)(2,1)S(1)}, u32[]{:S(2)}, u32[]{:S(2)}) collective-permute-start(bf16[512,128]{1,0:T(8,128)(2,1)} %bitcast.9), channel_id=1, source_target_pairs={{0,4},{1,5},{2,6},{3,7},{4,0},{5,1},{6,2},{7,3},{8,12},{9,13},{10,... | collective-permute-start | bytes 393224 | tf_op jit(solution)/shard_map/ppermute | solution.py:395
  4.0 1.6 %collective-permute-start.2 = (bf16[512,128]{1,0:T(8,128)(2,1)}, bf16[512,128]{1,0:T(8,128)(2,1)S(1)}, u32[]{:S(2)}, u32[]{:S(2)}) collective-permute-start(bf16[512,128]{1,0:T(8,128)(2,1)} %bitcast.10), channel_id=1, source_target_pairs={{0,2},{1,3},{2,0},{3,1},{4,6},{5,7},{6,4},{7,5},{8,10},{9,11},{10,... | collective-permute-start | bytes 393224 | tf_op jit(solution)/shard_map/ppermute | solution.py:395
  5.6 1.5 %collective-permute-start.1 = (bf16[512,128]{1,0:T(8,128)(2,1)}, bf16[512,128]{1,0:T(8,128)(2,1)S(1)}, u32[]{:S(2)}, u32[]{:S(2)}) collective-permute-start(bf16[512,128]{1,0:T(8,128)(2,1)} %bitcast.11), channel_id=1, source_target_pairs={{0,1},{1,0},{2,3},{3,2},{4,5},{5,4},{6,7},{7,6},{8,9},{9,8},{10,11... | collective-permute-start | bytes 393224 | tf_op jit(solution)/shard_map/ppermute | solution.py:395
  8.7 3.0 %shard_map.91.refs_3_.a_ref = bf16[528,128]{1,0:T(8,128)(2,1)S(1)} custom-call(s32[64]{0:T(128)S(1)} %copy-done.3, bf16[64,8,96,128]{3,2,1,0:T(8,128)(2,1)} %k_hbm.7, bf16[64,8,96,128]{3,2,1,0:T(8,128)(2,1)} %v_hbm.7, bf16[512,128]{1,0:T(8,128)(2,1)S(1)} %bitcast.12), custom_call_target="tpu_custom_call" | custom-call | flops 201326592 | bytes 3145728 | tf_op jit(solution)/shard_map/pallas_call | solution.py:126
  14.5 5.3 %shard_map.92 = (bf16[528,128]{1,0:T(8,128)(2,1)S(1)}, bf16[528,128]{1,0:T(8,128)(2,1)S(1)}, bf16[528,128]{1,0:T(8,128)(2,1)S(1)}) custom-call(s32[64]{0:T(128)S(1)} %copy-done.3, bf16[64,8,96,128]{3,2,1,0:T(8,128)(2,1)} %k_hbm.7, bf16[64,8,96,128]{3,2,1,0:T(8,128)(2,1)} %v_hbm.7, bf16[512,128]{1,0:T(8,128)(2,1)S(1)} %collective-permute-done.1.refs_0_, ...), custom_call_target="tpu_custom_call" | custom-call | flops 603979776 | bytes 9437184 | tf_op jit(solution)/shard_map/pallas_call | solution.py:126
  19.9 1.3 %collective-permute-start.9 = (bf16[512,128]{1,0:T(8,128)(2,1)S(1)}, bf16[512,128]{1,0:T(8,128)(2,1)S(1)}, u32[]{:S(2)}, u32[]{:S(2)}) collective-permute-start(bf16[512,128]{1,0:T(8,128)(2,1)S(1)} %collective-permute-done.6.refs_1_), channel_id=1, source_target_pairs={{0,2},{1,3},{2,0},{3,1},{4,6},{5,7},{6,4},{7,5},{8,10},{9,11},{10,... | collective-permute-start | bytes 393224 | tf_op jit(solution)/shard_map/ppermute | solution.py:395
  21.2 4.1 %shard_map.94 = (bf16[528,128]{1,0:T(8,128)(2,1)S(1)}, bf16[528,128]{1,0:T(8,128)(2,1)S(1)}) custom-call(s32[64]{0:T(128)S(1)} %copy-done.3, bf16[64,8,96,128]{3,2,1,0:T(8,128)(2,1)} %k_hbm.7, bf16[64,8,96,128]{3,2,1,0:T(8,128)(2,1)} %v_hbm.7, bf16[512,128]{1,0:T(8,128)(2,1)S(1)} %collective-permute-done.5.refs_0_, ...), custom_call_target="tpu_custom_call" | custom-call | flops 402653184 | bytes 6291456 | tf_op jit(solution)/shard_map/pallas_call | solution.py:126
  25.4 1.2 %collective-permute-start.7 = (bf16[528,128]{1,0:T(8,128)(2,1)S(1)}, bf16[528,128]{1,0:T(8,128)(2,1)S(1)}, u32[]{:S(2)}, u32[]{:S(2)}) collective-permute-start(bf16[528,128]{1,0:T(8,128)(2,1)S(1)} %get-tuple-element.39), channel_id=1, source_target_pairs={{0,1},{1,0},{2,3},{3,2},{4,5},{5,4},{6,7},{7,6},{8,9},{9,8},{10,11... | collective-permute-start | bytes 405512 | tf_op jit(solution)/shard_map/ppermute | solution.py:395
  27.5 4.1 %shard_map.96 = (bf16[528,128]{1,0:T(8,128)(2,1)S(1)}, bf16[528,128]{1,0:T(8,128)(2,1)S(1)}) custom-call(s32[64]{0:T(128)S(1)} %copy-done.4, bf16[64,8,96,128]{3,2,1,0:T(8,128)(2,1)} %k_hbm.7, bf16[64,8,96,128]{3,2,1,0:T(8,128)(2,1)} %v_hbm.7, bf16[512,128]{1,0:T(8,128)(2,1)S(1)} %collective-permute-done.9.refs_0_, ...), custom_call_target="tpu_custom_call" | custom-call | flops 402653184 | bytes 6291456 | tf_op jit(solution)/shard_map/pallas_call | solution.py:126
  31.7 1.2 %collective-permute-start.11 = (bf16[528,128]{1,0:T(8,128)(2,1)S(1)}, bf16[528,128]{1,0:T(8,128)(2,1)S(1)}, u32[]{:S(2)}, u32[]{:S(2)}) collective-permute-start(bf16[528,128]{1,0:T(8,128)(2,1)S(1)} %get-tuple-element.44), channel_id=1, source_target_pairs={{0,1},{1,0},{2,3},{3,2},{4,5},{5,4},{6,7},{7,6},{8,9},{9,8},{10,11... | collective-permute-start | bytes 405512 | tf_op jit(solution)/shard_map/ppermute | solution.py:395
  34.1 1.6 %collective-permute-start.8 = (bf16[528,128]{1,0:T(8,128)(2,1)S(1)}, bf16[528,128]{1,0:T(8,128)(2,1)S(1)}, u32[]{:S(2)}, u32[]{:S(2)}) collective-permute-start(bf16[528,128]{1,0:T(8,128)(2,1)S(1)} %shard_map.95.refs_0_), channel_id=1, source_target_pairs={{0,4},{1,5},{2,6},{3,7},{4,0},{5,1},{6,2},{7,3},{8,12},{9,13},{10,... | collective-permute-start | bytes 405512 | tf_op jit(solution)/shard_map/ppermute | solution.py:395
  36.0 1.3 %collective-permute-done.11.b_ref = bf16[528,128]{1,0:T(8,128)(2,1)S(1)} collective-permute-done((bf16[528,128]{1,0:T(8,128)(2,1)S(1)}, bf16[528,128]{1,0:T(8,128)(2,1)S(1)}, u32[]{:S(2)}, u32[]{:S(2)}) %collective-permute-start.11) | collective-permute-done | bytes 135200 | tf_op jit(solution)/shard_map/ppermute | solution.py:395
  38.8 2.8 %collective-permute-start.12 = (bf16[528,128]{1,0:T(8,128)(2,1)S(1)}, bf16[528,128]{1,0:T(8,128)(2,1)S(1)}, u32[]{:S(2)}, u32[]{:S(2)}) collective-permute-start(bf16[528,128]{1,0:T(8,128)(2,1)S(1)} %shard_map.97.refs_1_), channel_id=1, source_target_pairs={{0,6},{1,7},{2,4},{3,5},{4,2},{5,3},{6,0},{7,1},{8,14},{9,15},{10,... | collective-permute-start | bytes 405512 | tf_op jit(solution)/shard_map/ppermute | solution.py:395
  42.0 6.0 %shard_map.99.refs_4_ = bf16[1024,8192]{1,0:T(8,128)(2,1)S(1)} custom-call(bf16[1024,8192]{1,0:T(8,128)(2,1)} %source.1, bf16[528,128]{1,0:T(8,128)(2,1)S(1)} %shard_map.95.refs_0_, bf16[528,128]{1,0:T(8,128)(2,1)S(1)} %shard_map.97.refs_1_, bf16[528,128]{1,0:T(8,128)(2,1)S(1)} %shard_map.98.refs_2_), custom_call_target="tpu_custom_call" | custom-call | bytes 16777216 | tf_op jit(solution)/shard_map/pallas_call | solution.py:156
  48.1 2.0 %shard_map.100 = (bf16[64,1152]{1,0:T(8,128)(2,1)S(1)}, bf16[64,1024]{1,0:T(8,128)(2,1)S(1)}, bf16[64,1024]{1,0:T(8,128)(2,1)S(1)}, bf16[64,128]{1,0:T(8,128)(2,1)S(1)}, bf16[1024,8192]{1,0:T(8,128)(2,1)S(1)}) custom-call(bf16[528,128]{1,0:T(8,128)(2,1)S(1)} %shard_map.93.refs_0_, ...), custom_call_target="tpu_custom_call", output_to_operand_aliasing={{4}: (4, {})} | custom-call | flops 268435456 | bytes 4194304 | tf_op jit(solution)/shard_map/pallas_call | solution.py:266
  50.1 1.6 %collective-permute-start.17 = (bf16[64,1152]{1,0:T(8,128)(2,1)S(1)}, bf16[64,1152]{1,0:T(8,128)(2,1)S(1)}, u32[]{:S(2)}, u32[]{:S(2)}) collective-permute-start(bf16[64,1152]{1,0:T(8,128)(2,1)S(1)} %get-tuple-element.51), channel_id=1, source_target_pairs={{0,1},{1,0},{2,3},{3,2},{4,5},{5,4},{6,7},{7,6},{8,9},{9,8},{10,11... | collective-permute-start | bytes 442376 | tf_op jit(solution)/shard_map/ppermute | solution.py:395
  52.2 2.3 %shard_map.101 = (bf16[64,1024]{1,0:T(8,128)(2,1)S(1)}, bf16[64,1024]{1,0:T(8,128)(2,1)S(1)}, f32[64,1024]{1,0:T(8,128)S(1)}, f32[64,1024]{1,0:T(8,128)S(1)}, f3...) custom-call(bf16[1024,8192]{1,0:T(8,128)(2,1)S(1)} %get-tuple-element.46.w_ref, bf16[64,1024]{1,0:T(8,128)(2,1)S(1)} %get-tuple-element.47.att_ref), custom_call_target="tpu_custom_call" | custom-call | flops 805306368 | bytes 12582912 | tf_op jit(solution)/shard_map/pallas_call | solution.py:301
  54.5 1.6 %collective-permute-start.16 = (bf16[64,1024]{1,0:T(8,128)(2,1)S(1)}, bf16[64,1024]{1,0:T(8,128)(2,1)S(1)}, u32[]{:S(2)}, u32[]{:S(2)}) collective-permute-start(bf16[64,1024]{1,0:T(8,128)(2,1)S(1)} %get-tuple-element.49), channel_id=1, source_target_pairs={{0,1},{1,0},{2,3},{3,2},{4,5},{5,4},{6,7},{7,6},{8,9},{9,8},{10,11... | collective-permute-start | bytes 393224 | tf_op jit(solution)/shard_map/ppermute | solution.py:395
  58.2 1.3 %collective-permute-start.20 = (bf16[64,1152]{1,0:T(8,128)(2,1)S(1)}, bf16[64,1152]{1,0:T(8,128)(2,1)S(1)}, u32[]{:S(2)}, u32[]{:S(2)}) collective-permute-start(bf16[64,1152]{1,0:T(8,128)(2,1)S(1)} %shard_map.103), channel_id=1, source_target_pairs={{0,6},{1,7},{2,4},{3,5},{4,2},{5,3},{6,0},{7,1},{8,14},{9,15},{10,... | collective-permute-start | bytes 442376 | tf_op jit(solution)/shard_map/ppermute | solution.py:395
  59.7 1.2 %collective-permute-start.18 = (bf16[64,1152]{1,0:T(8,128)(2,1)S(1)}, bf16[64,1152]{1,0:T(8,128)(2,1)S(1)}, u32[]{:S(2)}, u32[]{:S(2)}) collective-permute-start(bf16[64,1152]{1,0:T(8,128)(2,1)S(1)} %shard_map.102), channel_id=1, source_target_pairs={{0,2},{1,3},{2,0},{3,1},{4,6},{5,7},{6,4},{7,5},{8,10},{9,11},{10,... | collective-permute-start | bytes 442376 | tf_op jit(solution)/shard_map/ppermute | solution.py:395
  60.8 1.5 %collective-permute-start.22 = (bf16[64,1024]{1,0:T(8,128)(2,1)S(1)}, bf16[64,1024]{1,0:T(8,128)(2,1)S(1)}, u32[]{:S(2)}, u32[]{:S(2)}) collective-permute-start(bf16[64,1024]{1,0:T(8,128)(2,1)S(1)} %get-tuple-element.56), channel_id=1, source_target_pairs={{0,1},{1,0},{2,3},{3,2},{4,5},{5,4},{6,7},{7,6},{8,9},{9,8},{10,11... | collective-permute-start | bytes 393224 | tf_op jit(solution)/shard_map/ppermute | solution.py:395
  62.3 3.5 %collective-permute-done.22.b_ref = bf16[64,1024]{1,0:T(8,128)(2,1)S(1)} collective-permute-done((bf16[64,1024]{1,0:T(8,128)(2,1)S(1)}, bf16[64,1024]{1,0:T(8,128)(2,1)S(1)}, u32[]{:S(2)}, u32[]{:S(2)}) %collective-permute-start.22) | collective-permute-done | bytes 131104 | tf_op jit(solution)/shard_map/ppermute | solution.py:395
  65.9 1.4 %collective-permute-done.21.refs_2_ = bf16[64,1152]{1,0:T(8,128)(2,1)S(1)} collective-permute-done((bf16[64,1152]{1,0:T(8,128)(2,1)S(1)}, bf16[64,1152]{1,0:T(8,128)(2,1)S(1)}, u32[]{:S(2)}, u32[]{:S(2)}) %collective-permute-start.21) | collective-permute-done | bytes 147488 | tf_op jit(solution)/shard_map/ppermute | solution.py:395
  67.7 1.2 %shard_map.106 = bf16[64,1024]{1,0:T(8,128)(2,1)} custom-call(s32[64,128]{1,0:T(8,128)S(1)} %broadcast_in_dim.23.refs_5_.slot_ref, bf16[512,1024]{1,0:T(8,128)(2,1)S(1)} %bitcast.8, bf16[512,1024]{1,0:T(8,128)(2,1)S(1)} %collective-permute-done.up_b, bf16[64,1152]{1,0:T(8,128)(2,1)S(1)} %collective-permute-done.18.refs_0_, ...), custom_call_target="tpu_custom_call" | custom-call | flops 2097152 | bytes 2097152 | tf_op jit(solution)/shard_map/pallas_call | solution.py:367
  (54 shorter events, 12.6 us)
Async XLA Ops:
  0.0 48.0 %collective-permute-start.15 = (bf16[512,1024]{1,0:T(8,128)(2,1)}, bf16[512,1024]{1,0:T(8,128)(2,1)S(1)}, u32[]{:S(2)}, u32[]{:S(2)}) collective-permute-start(bf16[512,1024]{1,0:T(8,128)(2,1)} %bitcast.5), channel_id=1, source_target_pairs={{0,8},{8,0},{1,9},{9,1},{2,10},{10,2},{3,11},{11,3},{4,12},{12,4},... | collective-permute-start | bytes 3145736 | tf_op jit(solution)/shard_map/ppermute | solution.py:398
  0.5 11.3 %collective-permute-start.3 = (bf16[512,128]{1,0:T(8,128)(2,1)}, bf16[512,128]{1,0:T(8,128)(2,1)S(1)}, u32[]{:S(2)}, u32[]{:S(2)}) collective-permute-start(bf16[512,128]{1,0:T(8,128)(2,1)} %bitcast.9), channel_id=1, source_target_pairs={{0,4},{1,5},{2,6},{3,7},{4,0},{5,1},{6,2},{7,3},{8,12},{9,13},{10,... | collective-permute-start | bytes 393224 | tf_op jit(solution)/shard_map/ppermute | solution.py:395
  4.0 8.9 %collective-permute-start.2 = (bf16[512,128]{1,0:T(8,128)(2,1)}, bf16[512,128]{1,0:T(8,128)(2,1)S(1)}, u32[]{:S(2)}, u32[]{:S(2)}) collective-permute-start(bf16[512,128]{1,0:T(8,128)(2,1)} %bitcast.10), channel_id=1, source_target_pairs={{0,2},{1,3},{2,0},{3,1},{4,6},{5,7},{6,4},{7,5},{8,10},{9,11},{10,... | collective-permute-start | bytes 393224 | tf_op jit(solution)/shard_map/ppermute | solution.py:395
  5.6 60.3 %collective-permute-start = (bf16[512,1024]{1,0:T(8,128)(2,1)}, bf16[512,1024]{1,0:T(8,128)(2,1)S(1)}, u32[]{:S(2)}, u32[]{:S(2)}) collective-permute-start(bf16[512,1024]{1,0:T(8,128)(2,1)} %bitcast.7), channel_id=1, source_target_pairs={{0,8},{8,0},{1,9},{9,1},{2,10},{10,2},{3,11},{11,3},{4,12},{12,4},... | collective-permute-start | bytes 3145736 | tf_op jit(solution)/shard_map/ppermute | solution.py:398
  5.6 8.3 %collective-permute-start.1 = (bf16[512,128]{1,0:T(8,128)(2,1)}, bf16[512,128]{1,0:T(8,128)(2,1)S(1)}, u32[]{:S(2)}, u32[]{:S(2)}) collective-permute-start(bf16[512,128]{1,0:T(8,128)(2,1)} %bitcast.11), channel_id=1, source_target_pairs={{0,1},{1,0},{2,3},{3,2},{4,5},{5,4},{6,7},{7,6},{8,9},{9,8},{10,11... | collective-permute-start | bytes 393224 | tf_op jit(solution)/shard_map/ppermute | solution.py:395
  11.8 8.1 %collective-permute-start.6 = (bf16[512,128]{1,0:T(8,128)(2,1)S(1)}, bf16[512,128]{1,0:T(8,128)(2,1)S(1)}, u32[]{:S(2)}, u32[]{:S(2)}) collective-permute-start(bf16[512,128]{1,0:T(8,128)(2,1)S(1)} %collective-permute-done.3.refs_2_), channel_id=1, source_target_pairs={{0,1},{1,0},{2,3},{3,2},{4,5},{5,4},{6,7},{7,6},{8,9},{9,8},{10,11... | collective-permute-start | bytes 393224 | tf_op jit(solution)/shard_map/ppermute | solution.py:395
  12.9 8.3 %collective-permute-start.5 = (bf16[512,128]{1,0:T(8,128)(2,1)S(1)}, bf16[512,128]{1,0:T(8,128)(2,1)S(1)}, u32[]{:S(2)}, u32[]{:S(2)}) collective-permute-start(bf16[512,128]{1,0:T(8,128)(2,1)S(1)} %collective-permute-done.2.refs_1_), channel_id=1, source_target_pairs={{0,1},{1,0},{2,3},{3,2},{4,5},{5,4},{6,7},{7,6},{8,9},{9,8},{10,11... | collective-permute-start | bytes 393224 | tf_op jit(solution)/shard_map/ppermute | solution.py:395
  13.9 12.7 %collective-permute-start.10 = (bf16[512,128]{1,0:T(8,128)(2,1)S(1)}, bf16[512,128]{1,0:T(8,128)(2,1)S(1)}, u32[]{:S(2)}, u32[]{:S(2)}) collective-permute-start(bf16[512,128]{1,0:T(8,128)(2,1)S(1)} %collective-permute-done.3.refs_2_), channel_id=1, source_target_pairs={{0,2},{1,3},{2,0},{3,1},{4,6},{5,7},{6,4},{7,5},{8,10},{9,11},{10,... | collective-permute-start | bytes 393224 | tf_op jit(solution)/shard_map/ppermute | solution.py:395
  19.9 7.6 %collective-permute-start.9 = (bf16[512,128]{1,0:T(8,128)(2,1)S(1)}, bf16[512,128]{1,0:T(8,128)(2,1)S(1)}, u32[]{:S(2)}, u32[]{:S(2)}) collective-permute-start(bf16[512,128]{1,0:T(8,128)(2,1)S(1)} %collective-permute-done.6.refs_1_), channel_id=1, source_target_pairs={{0,2},{1,3},{2,0},{3,1},{4,6},{5,7},{6,4},{7,5},{8,10},{9,11},{10,... | collective-permute-start | bytes 393224 | tf_op jit(solution)/shard_map/ppermute | solution.py:395
  25.4 7.4 %collective-permute-start.7 = (bf16[528,128]{1,0:T(8,128)(2,1)S(1)}, bf16[528,128]{1,0:T(8,128)(2,1)S(1)}, u32[]{:S(2)}, u32[]{:S(2)}) collective-permute-start(bf16[528,128]{1,0:T(8,128)(2,1)S(1)} %get-tuple-element.39), channel_id=1, source_target_pairs={{0,1},{1,0},{2,3},{3,2},{4,5},{5,4},{6,7},{7,6},{8,9},{9,8},{10,11... | collective-permute-start | bytes 405512 | tf_op jit(solution)/shard_map/ppermute | solution.py:395
  26.6 7.5 %collective-permute-start.13 = (bf16[528,128]{1,0:T(8,128)(2,1)S(1)}, bf16[528,128]{1,0:T(8,128)(2,1)S(1)}, u32[]{:S(2)}, u32[]{:S(2)}) collective-permute-start(bf16[528,128]{1,0:T(8,128)(2,1)S(1)} %get-tuple-element.42.refs_2_), channel_id=1, source_target_pairs={{0,1},{1,0},{2,3},{3,2},{4,5},{5,4},{6,7},{7,6},{8,9},{9,8},{10,11... | collective-permute-start | bytes 405512 | tf_op jit(solution)/shard_map/ppermute | solution.py:395
  31.7 5.7 %collective-permute-start.11 = (bf16[528,128]{1,0:T(8,128)(2,1)S(1)}, bf16[528,128]{1,0:T(8,128)(2,1)S(1)}, u32[]{:S(2)}, u32[]{:S(2)}) collective-permute-start(bf16[528,128]{1,0:T(8,128)(2,1)S(1)} %get-tuple-element.44), channel_id=1, source_target_pairs={{0,1},{1,0},{2,3},{3,2},{4,5},{5,4},{6,7},{7,6},{8,9},{9,8},{10,11... | collective-permute-start | bytes 405512 | tf_op jit(solution)/shard_map/ppermute | solution.py:395
  32.8 6.0 %collective-permute-start.4 = (bf16[528,128]{1,0:T(8,128)(2,1)S(1)}, bf16[528,128]{1,0:T(8,128)(2,1)S(1)}, u32[]{:S(2)}, u32[]{:S(2)}) collective-permute-start(bf16[528,128]{1,0:T(8,128)(2,1)S(1)} %get-tuple-element.38.refs_2_), channel_id=1, source_target_pairs={{0,1},{1,0},{2,3},{3,2},{4,5},{5,4},{6,7},{7,6},{8,9},{9,8},{10,11... | collective-permute-start | bytes 405512 | tf_op jit(solution)/shard_map/ppermute | solution.py:395
  34.1 13.9 %collective-permute-start.8 = (bf16[528,128]{1,0:T(8,128)(2,1)S(1)}, bf16[528,128]{1,0:T(8,128)(2,1)S(1)}, u32[]{:S(2)}, u32[]{:S(2)}) collective-permute-start(bf16[528,128]{1,0:T(8,128)(2,1)S(1)} %shard_map.95.refs_0_), channel_id=1, source_target_pairs={{0,4},{1,5},{2,6},{3,7},{4,0},{5,1},{6,2},{7,3},{8,12},{9,13},{10,... | collective-permute-start | bytes 405512 | tf_op jit(solution)/shard_map/ppermute | solution.py:395
  37.3 10.7 %collective-permute-start.14 = (bf16[528,128]{1,0:T(8,128)(2,1)S(1)}, bf16[528,128]{1,0:T(8,128)(2,1)S(1)}, u32[]{:S(2)}, u32[]{:S(2)}) collective-permute-start(bf16[528,128]{1,0:T(8,128)(2,1)S(1)} %shard_map.98.refs_2_), channel_id=1, source_target_pairs={{0,2},{1,3},{2,0},{3,1},{4,6},{5,7},{6,4},{7,5},{8,10},{9,11},{10,... | collective-permute-start | bytes 405512 | tf_op jit(solution)/shard_map/ppermute | solution.py:395
  38.8 9.2 %collective-permute-start.12 = (bf16[528,128]{1,0:T(8,128)(2,1)S(1)}, bf16[528,128]{1,0:T(8,128)(2,1)S(1)}, u32[]{:S(2)}, u32[]{:S(2)}) collective-permute-start(bf16[528,128]{1,0:T(8,128)(2,1)S(1)} %shard_map.97.refs_1_), channel_id=1, source_target_pairs={{0,6},{1,7},{2,4},{3,5},{4,2},{5,3},{6,0},{7,1},{8,14},{9,15},{10,... | collective-permute-start | bytes 405512 | tf_op jit(solution)/shard_map/ppermute | solution.py:395
  48.1 19.6 %copy-start.1 = (bf16[8,64,1024]{2,1,0:T(8,128)(2,1)S(1)}, bf16[8,64,1024]{2,1,0:T(8,128)(2,1)}, u32[]{:S(2)}) copy-start(bf16[8,64,1024]{2,1,0:T(8,128)(2,1)} %param.17) | copy-start | bytes 3145732
  50.1 6.6 %collective-permute-start.17 = (bf16[64,1152]{1,0:T(8,128)(2,1)S(1)}, bf16[64,1152]{1,0:T(8,128)(2,1)S(1)}, u32[]{:S(2)}, u32[]{:S(2)}) collective-permute-start(bf16[64,1152]{1,0:T(8,128)(2,1)S(1)} %get-tuple-element.51), channel_id=1, source_target_pairs={{0,1},{1,0},{2,3},{3,2},{4,5},{5,4},{6,7},{7,6},{8,9},{9,8},{10,11... | collective-permute-start | bytes 442376 | tf_op jit(solution)/shard_map/ppermute | solution.py:395
  51.7 6.5 %collective-permute-start.19 = (bf16[64,1024]{1,0:T(8,128)(2,1)S(1)}, bf16[64,1024]{1,0:T(8,128)(2,1)S(1)}, u32[]{:S(2)}, u32[]{:S(2)}) collective-permute-start(bf16[64,1024]{1,0:T(8,128)(2,1)S(1)} %get-tuple-element.53), channel_id=1, source_target_pairs={{0,1},{1,0},{2,3},{3,2},{4,5},{5,4},{6,7},{7,6},{8,9},{9,8},{10,11... | collective-permute-start | bytes 393224 | tf_op jit(solution)/shard_map/ppermute | solution.py:395
  54.5 5.1 %collective-permute-start.16 = (bf16[64,1024]{1,0:T(8,128)(2,1)S(1)}, bf16[64,1024]{1,0:T(8,128)(2,1)S(1)}, u32[]{:S(2)}, u32[]{:S(2)}) collective-permute-start(bf16[64,1024]{1,0:T(8,128)(2,1)S(1)} %get-tuple-element.49), channel_id=1, source_target_pairs={{0,1},{1,0},{2,3},{3,2},{4,5},{5,4},{6,7},{7,6},{8,9},{9,8},{10,11... | collective-permute-start | bytes 393224 | tf_op jit(solution)/shard_map/ppermute | solution.py:395
  56.8 10.5 %collective-permute-start.21 = (bf16[64,1152]{1,0:T(8,128)(2,1)S(1)}, bf16[64,1152]{1,0:T(8,128)(2,1)S(1)}, u32[]{:S(2)}, u32[]{:S(2)}) collective-permute-start(bf16[64,1152]{1,0:T(8,128)(2,1)S(1)} %shard_map.104), channel_id=1, source_target_pairs={{0,4},{1,5},{2,6},{3,7},{4,0},{5,1},{6,2},{7,3},{8,12},{9,13},{10,... | collective-permute-start | bytes 442376 | tf_op jit(solution)/shard_map/ppermute | solution.py:395
  58.2 9.1 %collective-permute-start.20 = (bf16[64,1152]{1,0:T(8,128)(2,1)S(1)}, bf16[64,1152]{1,0:T(8,128)(2,1)S(1)}, u32[]{:S(2)}, u32[]{:S(2)}) collective-permute-start(bf16[64,1152]{1,0:T(8,128)(2,1)S(1)} %shard_map.103), channel_id=1, source_target_pairs={{0,6},{1,7},{2,4},{3,5},{4,2},{5,3},{6,0},{7,1},{8,14},{9,15},{10,... | collective-permute-start | bytes 442376 | tf_op jit(solution)/shard_map/ppermute | solution.py:395
  59.7 8.0 %collective-permute-start.18 = (bf16[64,1152]{1,0:T(8,128)(2,1)S(1)}, bf16[64,1152]{1,0:T(8,128)(2,1)S(1)}, u32[]{:S(2)}, u32[]{:S(2)}) collective-permute-start(bf16[64,1152]{1,0:T(8,128)(2,1)S(1)} %shard_map.102), channel_id=1, source_target_pairs={{0,2},{1,3},{2,0},{3,1},{4,6},{5,7},{6,4},{7,5},{8,10},{9,11},{10,... | collective-permute-start | bytes 442376 | tf_op jit(solution)/shard_map/ppermute | solution.py:395
  60.8 5.0 %collective-permute-start.22 = (bf16[64,1024]{1,0:T(8,128)(2,1)S(1)}, bf16[64,1024]{1,0:T(8,128)(2,1)S(1)}, u32[]{:S(2)}, u32[]{:S(2)}) collective-permute-start(bf16[64,1024]{1,0:T(8,128)(2,1)S(1)} %get-tuple-element.56), channel_id=1, source_target_pairs={{0,1},{1,0},{2,3},{3,2},{4,5},{5,4},{6,7},{7,6},{8,9},{9,8},{10,11... | collective-permute-start | bytes 393224 | tf_op jit(solution)/shard_map/ppermute | solution.py:395
  (6 other events, 47.6 us)

commit v7 on v6

--- a/solution.py
+++ b/solution.py
@@ -25,6 +25,8 @@
     ("attend", 3, 5),
     ("attend", 7, 6),
 ]
+
+AHEAD = {(1, 2, 4): (3, 5)}
 
 
 def split2(x):
@@ -78,64 +80,94 @@
     return stat
 
 
-def attend_body(which, group, blocks, heads, scale, len_ref, k_hbm, v_hbm, *refs):
+def fetch(which, group, heads, hbm_refs, buffers, sems, blocks):
+    me = lax.axis_index("tensor")
+    size = hbm_refs[0].shape[0] // blocks
+    copies = []
+    for j, k in enumerate(which):
+        kv = lax.div((me ^ k) * heads, group)
+        for b in range(blocks):
+            i = j * blocks + b
+            copies.append(
+                [
+                    pltpu.make_async_copy(src.at[pl.ds(b * size, size), kv], dst.at[i], sem.at[i])
+                    for src, dst, sem in zip(hbm_refs, buffers, sems)
+                ]
+            )
+    for pair_of in copies:
+        for c in pair_of:
+            c.start()
+    return copies
+
+
+def attend_body(which, following, given, group, blocks, heads, scale, len_ref, k_hbm, v_hbm, *refs):
     n = len(which)
-    me = lax.axis_index("tensor")
+    refs = list(refs)
+    take = lambda count: [refs.pop() for _ in range(count)][::-1]
+    next_sems = take(2) if following else []
+    own = take(4) if not given else []
+    next_bufs = take(2) if following else []
+    o_refs = take(n)
     q_refs = refs[:n]
-    o_refs = refs[-4 - n : -4]
-    k_buf, v_buf, k_sem, v_sem = refs[-4:]
-    size = k_hbm.shape[0] // blocks
-    many = size * heads
-    begin = me * k_hbm.shape[2]
-    copies = []
-    for j in range(n):
-        kv = lax.div((me ^ which[j]) * heads, group)
-        for b in range(blocks):
-            at, i = pl.ds(b * size, size), j * blocks + b
-            copies.append(
-                (
-                    pltpu.make_async_copy(k_hbm.at[at, kv], k_buf.at[i], k_sem.at[i]),
-                    pltpu.make_async_copy(v_hbm.at[at, kv], v_buf.at[i], v_sem.at[i]),
-                )
-            )
-    for ck, cv in copies:
-        ck.start()
-        cv.start()
+    begin = lax.axis_index("tensor") * k_hbm.shape[2]
+    many = k_hbm.shape[0] // blocks * heads
+    if given:
+        k_buf, v_buf = refs[n : n + 2]
+    else:
+        k_buf, v_buf = own[:2]
+        copies = fetch(which, group, heads, (k_hbm, v_hbm), own[:2], own[2:], blocks)
+    if following:
+        ahead = fetch(following, group, heads, (k_hbm, v_hbm), next_bufs, next_sems, blocks)
     for j in range(n):
         stat = jnp.zeros((TILE, LANES), F32)
         for b in range(blocks):
             i = j * blocks + b
-            copies[i][0].wait()
-            copies[i][1].wait()
+            if not given:
+                for c in copies[i]:
+                    c.wait()
             stat = stat + attend_part(
-                heads, scale, q_refs[j][b * many : (b + 1) * many, :], len_ref, begin, k_buf.at[i], v_buf.at[i],
-                b * many // TILE, o_refs[j],
+                heads, scale, q_refs[j][b * many : (b + 1) * many, :], len_ref, begin,
+                k_buf.at[i], v_buf.at[i], b * many // TILE, o_refs[j],
             )
         o_refs[j][many * blocks :, :] = stat.astype(BF16)
-
-
-def attend(which, group, queries, live, keys, values, heads, scale, after):
+    if following:
+        for pair_of in ahead:
+            for c in pair_of:
+                c.wait()
+
+
+def attend(which, following, given, group, queries, live, keys, values, heads, scale, after):
     n, blocks = len(queries), 2
     rows, _, positions, width = keys.shape
     vmem = pl.BlockSpec(memory_space=pltpu.VMEM)
     smem = pl.BlockSpec(memory_space=pltpu.SMEM)
     hbm = pl.BlockSpec(memory_space=pltpu.HBM)
     anywhere = pl.BlockSpec(memory_space=pl.ANY)
-    buf = pltpu.VMEM((n * blocks, rows // blocks, positions, width), BF16)
-    sem = pltpu.SemaphoreType.DMA((n * blocks,))
-    return pl.pallas_call(
-        functools.partial(attend_body, which, group, blocks, heads, scale),
-        in_specs=[smem, hbm, hbm] + [vmem] * n + [anywhere] * len(after),
-        out_specs=[vmem] * n,
-        out_shape=[jax.ShapeDtypeStruct((rows * heads + TILE, width), BF16)] * n,
-        scratch_shapes=[buf, buf, sem, sem],
+
+    def buf(count):
+        return pltpu.VMEM((count * blocks, rows // blocks, positions, width), BF16)
+
+    def sem(count):
+        return pltpu.SemaphoreType.DMA((count * blocks,))
+
+    scratch = [] if given else [buf(n), buf(n), sem(n), sem(n)]
+    more = [buf(len(following))] * 2 if following else []
+    if following:
+        scratch += [sem(len(following))] * 2
+    outs = pl.pallas_call(
+        functools.partial(attend_body, which, following, bool(given), group, blocks, heads, scale),
+        in_specs=[smem, hbm, hbm] + [vmem] * (n + len(given)) + [anywhere] * len(after),
+        out_specs=[vmem] * (n + len(more)),
+        out_shape=[jax.ShapeDtypeStruct((rows * heads + TILE, width), BF16)] * n + more,
+        scratch_shapes=scratch,
         compiler_params=pltpu.CompilerParams(vmem_limit_bytes=LARGE),
         cost_estimate=pl.CostEstimate(
             flops=32 * n * rows * heads * positions * width,
             bytes_accessed=4 * n * rows * positions * width,
             transcendentals=n * rows * heads * positions,
         ),
-    )(live, keys, values, *queries, *after)
+    )(live, keys, values, *queries, *given, *after)
+    return outs[:n], list(outs[n:])
 
 
 def load_body(blocks, source, *refs):
@@ -413,9 +445,13 @@
 
     q = queries.reshape(rows * heads, width)
     held, partial, token = {0: q}, {}, ()
+    given = []
     for kind, *ks in PLAN + [(kind, k) for k in range(8, tensor) for kind in ("forward", "attend")]:
         if kind == "attend":
-            outs = attend(ks, group, [held[k] for k in ks], live, keys, values, heads, scale, token)
+            outs, given = attend(
+                ks, AHEAD.get(tuple(ks), ()), given, group, [held[k] for k in ks],
+                live, keys, values, heads, scale, token,
+            )
             partial.update(zip(ks, outs))
             token = [outs[0]]
             continue

time: 69 us -> 68.4 us (level)
  Pallas kernels: 29.8 us -> 29 us
    pallas_call x4, Pallas kernels: 16.6 us -> 15.9 us  [attend(): pl.pallas_call(functools.partial(attend_body, which, following, bool(give...]
    unnamed x14 -> x12, local copies, waits for them, and re-layouts: 1.62 us -> 1.61 us
  transfers between devices with their start and end apart: 23 -> 23, of which waited for: 7 -> 8; matrix products, arithmetic and copies ran while one was open for 0% -> 0% of each run, Pallas kernels for 42% -> 41%
where the time goes in v7:
time: 68.4 us; the launch traced here: 68.3 us
  starting transfers between devices  29.2 us (43%)
  Pallas kernels  29 us (42%)
  waiting for transfers between devices  8.09 us (12%)
  local copies, waits for them, and re-layouts  1.68 us (2%)
    ppermute x21, starting transfers between devices, hop(): return lax.ppermute(x, 'tensor', [(i, i ^ k) for i in range(tensor)])  28.8 us
    pallas_call x4, Pallas kernels, attend(): pl.pallas_call(functools.partial(attend_body, which, following, bool(give...  15.9 us
    ppermute x21, waiting for transfers between devices, hop(): return lax.ppermute(x, 'tensor', [(i, i ^ k) for i in range(tensor)])  8.08 us
    pallas_call x1, Pallas kernels, load(): pl.pallas_call(functools.partial(load_body, blocks), in_specs=[pl.BlockSp...  5.96 us
    pallas_call x1, Pallas kernels, project_more(): pl.pallas_call(functools.partial(project_more_body, blocks, kinds), in_sp...  2.29 us
    pallas_call x1, Pallas kernels, project(): pl.pallas_call(functools.partial(project_body, len(parts), blocks, heads,...  2.02 us
    unnamed x12, local copies, waits for them, and re-layouts  1.61 us
  transfers between devices with their start and end apart: 23, of which 8 were waited for; matrix products, arithmetic and copies ran while one was open for 0% of the time, Pallas kernels for 41%

profile of v7, /device:TPU:0, one launch (start us, length us, event | category | flops | bytes accessed | tf_op | source)
XLA Modules:
  0.0 68.3 jit_solution(8236168595485859390)
XLA Ops:
  0.5 3.6 %collective-permute-start.3 = (bf16[512,128]{1,0:T(8,128)(2,1)}, bf16[512,128]{1,0:T(8,128)(2,1)S(1)}, u32[]{:S(2)}, u32[]{:S(2)}) collective-permute-start(bf16[512,128]{1,0:T(8,128)(2,1)} %bitcast.9), channel_id=1, source_target_pairs={{0,4},{1,5},{2,6},{3,7},{4,0},{5,1},{6,2},{7,3},{8,12},{9,13},{10,... | collective-permute-start | bytes 393224 | tf_op jit(solution)/shard_map/ppermute | solution.py:427
  4.0 1.6 %collective-permute-start.2 = (bf16[512,128]{1,0:T(8,128)(2,1)}, bf16[512,128]{1,0:T(8,128)(2,1)S(1)}, u32[]{:S(2)}, u32[]{:S(2)}) collective-permute-start(bf16[512,128]{1,0:T(8,128)(2,1)} %bitcast.10), channel_id=1, source_target_pairs={{0,2},{1,3},{2,0},{3,1},{4,6},{5,7},{6,4},{7,5},{8,10},{9,11},{10,... | collective-permute-start | bytes 393224 | tf_op jit(solution)/shard_map/ppermute | solution.py:427
  5.6 1.5 %collective-permute-start.1 = (bf16[512,128]{1,0:T(8,128)(2,1)}, bf16[512,128]{1,0:T(8,128)(2,1)S(1)}, u32[]{:S(2)}, u32[]{:S(2)}) collective-permute-start(bf16[512,128]{1,0:T(8,128)(2,1)} %bitcast.11), channel_id=1, source_target_pairs={{0,1},{1,0},{2,3},{3,2},{4,5},{5,4},{6,7},{7,6},{8,9},{9,8},{10,11... | collective-permute-start | bytes 393224 | tf_op jit(solution)/shard_map/ppermute | solution.py:427
  8.7 3.0 %shard_map.91.refs_3_.a_ref = bf16[528,128]{1,0:T(8,128)(2,1)S(1)} custom-call(s32[64]{0:T(128)S(1)} %copy-done.3, bf16[64,8,96,128]{3,2,1,0:T(8,128)(2,1)} %k_hbm.7, bf16[64,8,96,128]{3,2,1,0:T(8,128)(2,1)} %v_hbm.7, bf16[512,128]{1,0:T(8,128)(2,1)S(1)} %bitcast.12), custom_call_target="tpu_custom_call" | custom-call | flops 201326592 | bytes 3145728 | tf_op jit(solution)/shard_map/pallas_call | solution.py:157
  11.8 1.1 %collective-permute-start.6 = (bf16[512,128]{1,0:T(8,128)(2,1)S(1)}, bf16[512,128]{1,0:T(8,128)(2,1)S(1)}, u32[]{:S(2)}, u32[]{:S(2)}) collective-permute-start(bf16[512,128]{1,0:T(8,128)(2,1)S(1)} %collective-permute-done.3.refs_2_), channel_id=1, source_target_pairs={{0,1},{1,0},{2,3},{3,2},{4,5},{5,4},{6,7},{7,6},{8,9},{9,8},{10,11... | collective-permute-start | bytes 393224 | tf_op jit(solution)/shard_map/ppermute | solution.py:427
  14.5 6.3 %shard_map.92 = (bf16[528,128]{1,0:T(8,128)(2,1)S(1)}, bf16[528,128]{1,0:T(8,128)(2,1)S(1)}, bf16[528,128]{1,0:T(8,128)(2,1)S(1)}, bf16[4,32,96,128]{3,2,1,0:T(8,128)(2,1)S(1)}, bf16[4,32,96,128]{3,2,1,0:T(8,128)(2,1)S(1)}) custom-call(s32[64]{0:T(128)S(1)} %copy-done.3, bf16[64,8,96,128]{3,2,1,0:T(8,128)(2,1)} %k_hbm.7, bf16[64,8,96,128]{3,2,1,0:T(8,128)(2,1)} %v_hbm.7, ...), custom_call_target="tpu_custom_call" | custom-call | flops 603979776 | bytes 9437184 | tf_op jit(solution)/shard_map/pallas_call | solution.py:157
  20.9 1.4 %collective-permute-start.9 = (bf16[512,128]{1,0:T(8,128)(2,1)S(1)}, bf16[512,128]{1,0:T(8,128)(2,1)S(1)}, u32[]{:S(2)}, u32[]{:S(2)}) collective-permute-start(bf16[512,128]{1,0:T(8,128)(2,1)S(1)} %collective-permute-done.6.refs_1_), channel_id=1, source_target_pairs={{0,2},{1,3},{2,0},{3,1},{4,6},{5,7},{6,4},{7,5},{8,10},{9,11},{10,... | collective-permute-start | bytes 393224 | tf_op jit(solution)/shard_map/ppermute | solution.py:427
  22.3 2.4 %shard_map.94 = (bf16[528,128]{1,0:T(8,128)(2,1)S(1)}, bf16[528,128]{1,0:T(8,128)(2,1)S(1)}) custom-call(s32[64]{0:T(128)S(1)} %copy-done.3, bf16[64,8,96,128]{3,2,1,0:T(8,128)(2,1)} %k_hbm.7, bf16[64,8,96,128]{3,2,1,0:T(8,128)(2,1)} %v_hbm.7, bf16[512,128]{1,0:T(8,128)(2,1)S(1)} %collective-permute-done.5.refs_0_, ...), custom_call_target="tpu_custom_call" | custom-call | flops 402653184 | bytes 6291456 | tf_op jit(solution)/shard_map/pallas_call | solution.py:157
  24.7 1.1 %collective-permute-start.7 = (bf16[528,128]{1,0:T(8,128)(2,1)S(1)}, bf16[528,128]{1,0:T(8,128)(2,1)S(1)}, u32[]{:S(2)}, u32[]{:S(2)}) collective-permute-start(bf16[528,128]{1,0:T(8,128)(2,1)S(1)} %get-tuple-element.43), channel_id=1, source_target_pairs={{0,1},{1,0},{2,3},{3,2},{4,5},{5,4},{6,7},{7,6},{8,9},{9,8},{10,11... | collective-permute-start | bytes 405512 | tf_op jit(solution)/shard_map/ppermute | solution.py:427
  26.8 4.1 %shard_map.96 = (bf16[528,128]{1,0:T(8,128)(2,1)S(1)}, bf16[528,128]{1,0:T(8,128)(2,1)S(1)}) custom-call(s32[64]{0:T(128)S(1)} %copy-done.3, bf16[64,8,96,128]{3,2,1,0:T(8,128)(2,1)} %k_hbm.7, bf16[64,8,96,128]{3,2,1,0:T(8,128)(2,1)} %v_hbm.7, bf16[512,128]{1,0:T(8,128)(2,1)S(1)} %collective-permute-done.9.refs_0_, ...), custom_call_target="tpu_custom_call" | custom-call | flops 402653184 | bytes 6291456 | tf_op jit(solution)/shard_map/pallas_call | solution.py:157
  30.9 1.1 %collective-permute-start.11 = (bf16[528,128]{1,0:T(8,128)(2,1)S(1)}, bf16[528,128]{1,0:T(8,128)(2,1)S(1)}, u32[]{:S(2)}, u32[]{:S(2)}) collective-permute-start(bf16[528,128]{1,0:T(8,128)(2,1)S(1)} %get-tuple-element.48), channel_id=1, source_target_pairs={{0,1},{1,0},{2,3},{3,2},{4,5},{5,4},{6,7},{7,6},{8,9},{9,8},{10,11... | collective-permute-start | bytes 405512 | tf_op jit(solution)/shard_map/ppermute | solution.py:427
  33.4 2.1 %collective-permute-start.8 = (bf16[528,128]{1,0:T(8,128)(2,1)S(1)}, bf16[528,128]{1,0:T(8,128)(2,1)S(1)}, u32[]{:S(2)}, u32[]{:S(2)}) collective-permute-start(bf16[528,128]{1,0:T(8,128)(2,1)S(1)} %shard_map.95.refs_0_), channel_id=1, source_target_pairs={{0,4},{1,5},{2,6},{3,7},{4,0},{5,1},{6,2},{7,3},{8,12},{9,13},{10,... | collective-permute-start | bytes 405512 | tf_op jit(solution)/shard_map/ppermute | solution.py:427
  38.1 2.9 %collective-permute-start.12 = (bf16[528,128]{1,0:T(8,128)(2,1)S(1)}, bf16[528,128]{1,0:T(8,128)(2,1)S(1)}, u32[]{:S(2)}, u32[]{:S(2)}) collective-permute-start(bf16[528,128]{1,0:T(8,128)(2,1)S(1)} %shard_map.97.refs_1_), channel_id=1, source_target_pairs={{0,6},{1,7},{2,4},{3,5},{4,2},{5,3},{6,0},{7,1},{8,14},{9,15},{10,... | collective-permute-start | bytes 405512 | tf_op jit(solution)/shard_map/ppermute | solution.py:427
  41.4 6.0 %shard_map.99.refs_4_ = bf16[1024,8192]{1,0:T(8,128)(2,1)S(1)} custom-call(bf16[1024,8192]{1,0:T(8,128)(2,1)} %source.1, bf16[528,128]{1,0:T(8,128)(2,1)S(1)} %shard_map.95.refs_0_, bf16[528,128]{1,0:T(8,128)(2,1)S(1)} %shard_map.97.refs_1_, bf16[528,128]{1,0:T(8,128)(2,1)S(1)} %shard_map.98.refs_2_), custom_call_target="tpu_custom_call" | custom-call | bytes 16777216 | tf_op jit(solution)/shard_map/pallas_call | solution.py:188
  47.4 2.0 %shard_map.100 = (bf16[64,1152]{1,0:T(8,128)(2,1)S(1)}, bf16[64,1024]{1,0:T(8,128)(2,1)S(1)}, bf16[64,1024]{1,0:T(8,128)(2,1)S(1)}, bf16[64,128]{1,0:T(8,128)(2,1)S(1)}, bf16[1024,8192]{1,0:T(8,128)(2,1)S(1)}) custom-call(bf16[528,128]{1,0:T(8,128)(2,1)S(1)} %shard_map.93.refs_0_, ...), custom_call_target="tpu_custom_call", output_to_operand_aliasing={{4}: (4, {})} | custom-call | flops 268435456 | bytes 4194304 | tf_op jit(solution)/shard_map/pallas_call | solution.py:298
  49.5 1.5 %collective-permute-start.17 = (bf16[64,1152]{1,0:T(8,128)(2,1)S(1)}, bf16[64,1152]{1,0:T(8,128)(2,1)S(1)}, u32[]{:S(2)}, u32[]{:S(2)}) collective-permute-start(bf16[64,1152]{1,0:T(8,128)(2,1)S(1)} %get-tuple-element.55), channel_id=1, source_target_pairs={{0,1},{1,0},{2,3},{3,2},{4,5},{5,4},{6,7},{7,6},{8,9},{9,8},{10,11... | collective-permute-start | bytes 442376 | tf_op jit(solution)/shard_map/ppermute | solution.py:427
  51.6 2.3 %shard_map.101 = (bf16[64,1024]{1,0:T(8,128)(2,1)S(1)}, bf16[64,1024]{1,0:T(8,128)(2,1)S(1)}, f32[64,1024]{1,0:T(8,128)S(1)}, f32[64,1024]{1,0:T(8,128)S(1)}, f3...) custom-call(bf16[1024,8192]{1,0:T(8,128)(2,1)S(1)} %get-tuple-element.50.w_ref, bf16[64,1024]{1,0:T(8,128)(2,1)S(1)} %get-tuple-element.51.att_ref), custom_call_target="tpu_custom_call" | custom-call | flops 805306368 | bytes 12582912 | tf_op jit(solution)/shard_map/pallas_call | solution.py:333
  53.9 1.5 %collective-permute-start.16 = (bf16[64,1024]{1,0:T(8,128)(2,1)S(1)}, bf16[64,1024]{1,0:T(8,128)(2,1)S(1)}, u32[]{:S(2)}, u32[]{:S(2)}) collective-permute-start(bf16[64,1024]{1,0:T(8,128)(2,1)S(1)} %get-tuple-element.53), channel_id=1, source_target_pairs={{0,1},{1,0},{2,3},{3,2},{4,5},{5,4},{6,7},{7,6},{8,9},{9,8},{10,11... | collective-permute-start | bytes 393224 | tf_op jit(solution)/shard_map/ppermute | solution.py:427
  57.6 1.1 %collective-permute-start.20 = (bf16[64,1152]{1,0:T(8,128)(2,1)S(1)}, bf16[64,1152]{1,0:T(8,128)(2,1)S(1)}, u32[]{:S(2)}, u32[]{:S(2)}) collective-permute-start(bf16[64,1152]{1,0:T(8,128)(2,1)S(1)} %shard_map.103), channel_id=1, source_target_pairs={{0,6},{1,7},{2,4},{3,5},{4,2},{5,3},{6,0},{7,1},{8,14},{9,15},{10,... | collective-permute-start | bytes 442376 | tf_op jit(solution)/shard_map/ppermute | solution.py:427
  59.0 1.1 %collective-permute-start.18 = (bf16[64,1152]{1,0:T(8,128)(2,1)S(1)}, bf16[64,1152]{1,0:T(8,128)(2,1)S(1)}, u32[]{:S(2)}, u32[]{:S(2)}) collective-permute-start(bf16[64,1152]{1,0:T(8,128)(2,1)S(1)} %shard_map.102), channel_id=1, source_target_pairs={{0,2},{1,3},{2,0},{3,1},{4,6},{5,7},{6,4},{7,5},{8,10},{9,11},{10,... | collective-permute-start | bytes 442376 | tf_op jit(solution)/shard_map/ppermute | solution.py:427
  60.0 1.4 %collective-permute-start.22 = (bf16[64,1024]{1,0:T(8,128)(2,1)S(1)}, bf16[64,1024]{1,0:T(8,128)(2,1)S(1)}, u32[]{:S(2)}, u32[]{:S(2)}) collective-permute-start(bf16[64,1024]{1,0:T(8,128)(2,1)S(1)} %get-tuple-element.60), channel_id=1, source_target_pairs={{0,1},{1,0},{2,3},{3,2},{4,5},{5,4},{6,7},{7,6},{8,9},{9,8},{10,11... | collective-permute-start | bytes 393224 | tf_op jit(solution)/shard_map/ppermute | solution.py:427
  61.5 3.5 %collective-permute-done.22.b_ref = bf16[64,1024]{1,0:T(8,128)(2,1)S(1)} collective-permute-done((bf16[64,1024]{1,0:T(8,128)(2,1)S(1)}, bf16[64,1024]{1,0:T(8,128)(2,1)S(1)}, u32[]{:S(2)}, u32[]{:S(2)}) %collective-permute-start.22) | collective-permute-done | bytes 131104 | tf_op jit(solution)/shard_map/ppermute | solution.py:427
  65.1 1.4 %collective-permute-done.21.refs_2_ = bf16[64,1152]{1,0:T(8,128)(2,1)S(1)} collective-permute-done((bf16[64,1152]{1,0:T(8,128)(2,1)S(1)}, bf16[64,1152]{1,0:T(8,128)(2,1)S(1)}, u32[]{:S(2)}, u32[]{:S(2)}) %collective-permute-start.21) | collective-permute-done | bytes 147488 | tf_op jit(solution)/shard_map/ppermute | solution.py:427
  67.1 1.2 %shard_map.106 = bf16[64,1024]{1,0:T(8,128)(2,1)} custom-call(s32[64,128]{1,0:T(8,128)S(1)} %broadcast_in_dim.23.refs_5_.slot_ref, bf16[512,1024]{1,0:T(8,128)(2,1)S(1)} %bitcast.8, bf16[512,1024]{1,0:T(8,128)(2,1)S(1)} %collective-permute-done.up_b, bf16[64,1152]{1,0:T(8,128)(2,1)S(1)} %collective-permute-done.18.refs_0_, ...), custom_call_target="tpu_custom_call" | custom-call | flops 2097152 | bytes 2097152 | tf_op jit(solution)/shard_map/pallas_call | solution.py:399
  (52 shorter events, 12.7 us)
Async XLA Ops:
  0.0 47.4 %collective-permute-start.15 = (bf16[512,1024]{1,0:T(8,128)(2,1)}, bf16[512,1024]{1,0:T(8,128)(2,1)S(1)}, u32[]{:S(2)}, u32[]{:S(2)}) collective-permute-start(bf16[512,1024]{1,0:T(8,128)(2,1)} %bitcast.5), channel_id=1, source_target_pairs={{0,8},{8,0},{1,9},{9,1},{2,10},{10,2},{3,11},{11,3},{4,12},{12,4},... | collective-permute-start | bytes 3145736 | tf_op jit(solution)/shard_map/ppermute | solution.py:430
  0.5 11.3 %collective-permute-start.3 = (bf16[512,128]{1,0:T(8,128)(2,1)}, bf16[512,128]{1,0:T(8,128)(2,1)S(1)}, u32[]{:S(2)}, u32[]{:S(2)}) collective-permute-start(bf16[512,128]{1,0:T(8,128)(2,1)} %bitcast.9), channel_id=1, source_target_pairs={{0,4},{1,5},{2,6},{3,7},{4,0},{5,1},{6,2},{7,3},{8,12},{9,13},{10,... | collective-permute-start | bytes 393224 | tf_op jit(solution)/shard_map/ppermute | solution.py:427
  4.0 8.9 %collective-permute-start.2 = (bf16[512,128]{1,0:T(8,128)(2,1)}, bf16[512,128]{1,0:T(8,128)(2,1)S(1)}, u32[]{:S(2)}, u32[]{:S(2)}) collective-permute-start(bf16[512,128]{1,0:T(8,128)(2,1)} %bitcast.10), channel_id=1, source_target_pairs={{0,2},{1,3},{2,0},{3,1},{4,6},{5,7},{6,4},{7,5},{8,10},{9,11},{10,... | collective-permute-start | bytes 393224 | tf_op jit(solution)/shard_map/ppermute | solution.py:427
  5.6 59.5 %collective-permute-start = (bf16[512,1024]{1,0:T(8,128)(2,1)}, bf16[512,1024]{1,0:T(8,128)(2,1)S(1)}, u32[]{:S(2)}, u32[]{:S(2)}) collective-permute-start(bf16[512,1024]{1,0:T(8,128)(2,1)} %bitcast.7), channel_id=1, source_target_pairs={{0,8},{8,0},{1,9},{9,1},{2,10},{10,2},{3,11},{11,3},{4,12},{12,4},... | collective-permute-start | bytes 3145736 | tf_op jit(solution)/shard_map/ppermute | solution.py:430
  5.6 8.3 %collective-permute-start.1 = (bf16[512,128]{1,0:T(8,128)(2,1)}, bf16[512,128]{1,0:T(8,128)(2,1)S(1)}, u32[]{:S(2)}, u32[]{:S(2)}) collective-permute-start(bf16[512,128]{1,0:T(8,128)(2,1)} %bitcast.11), channel_id=1, source_target_pairs={{0,1},{1,0},{2,3},{3,2},{4,5},{5,4},{6,7},{7,6},{8,9},{9,8},{10,11... | collective-permute-start | bytes 393224 | tf_op jit(solution)/shard_map/ppermute | solution.py:427
  11.8 9.1 %collective-permute-start.6 = (bf16[512,128]{1,0:T(8,128)(2,1)S(1)}, bf16[512,128]{1,0:T(8,128)(2,1)S(1)}, u32[]{:S(2)}, u32[]{:S(2)}) collective-permute-start(bf16[512,128]{1,0:T(8,128)(2,1)S(1)} %collective-permute-done.3.refs_2_), channel_id=1, source_target_pairs={{0,1},{1,0},{2,3},{3,2},{4,5},{5,4},{6,7},{7,6},{8,9},{9,8},{10,11... | collective-permute-start | bytes 393224 | tf_op jit(solution)/shard_map/ppermute | solution.py:427
  12.9 9.4 %collective-permute-start.5 = (bf16[512,128]{1,0:T(8,128)(2,1)S(1)}, bf16[512,128]{1,0:T(8,128)(2,1)S(1)}, u32[]{:S(2)}, u32[]{:S(2)}) collective-permute-start(bf16[512,128]{1,0:T(8,128)(2,1)S(1)} %collective-permute-done.2.refs_1_), channel_id=1, source_target_pairs={{0,1},{1,0},{2,3},{3,2},{4,5},{5,4},{6,7},{7,6},{8,9},{9,8},{10,11... | collective-permute-start | bytes 393224 | tf_op jit(solution)/shard_map/ppermute | solution.py:427
  13.9 11.9 %collective-permute-start.10 = (bf16[512,128]{1,0:T(8,128)(2,1)S(1)}, bf16[512,128]{1,0:T(8,128)(2,1)S(1)}, u32[]{:S(2)}, u32[]{:S(2)}) collective-permute-start(bf16[512,128]{1,0:T(8,128)(2,1)S(1)} %collective-permute-done.3.refs_2_), channel_id=1, source_target_pairs={{0,2},{1,3},{2,0},{3,1},{4,6},{5,7},{6,4},{7,5},{8,10},{9,11},{10,... | collective-permute-start | bytes 393224 | tf_op jit(solution)/shard_map/ppermute | solution.py:427
  20.9 5.9 %collective-permute-start.9 = (bf16[512,128]{1,0:T(8,128)(2,1)S(1)}, bf16[512,128]{1,0:T(8,128)(2,1)S(1)}, u32[]{:S(2)}, u32[]{:S(2)}) collective-permute-start(bf16[512,128]{1,0:T(8,128)(2,1)S(1)} %collective-permute-done.6.refs_1_), channel_id=1, source_target_pairs={{0,2},{1,3},{2,0},{3,1},{4,6},{5,7},{6,4},{7,5},{8,10},{9,11},{10,... | collective-permute-start | bytes 393224 | tf_op jit(solution)/shard_map/ppermute | solution.py:427
  24.7 7.4 %collective-permute-start.7 = (bf16[528,128]{1,0:T(8,128)(2,1)S(1)}, bf16[528,128]{1,0:T(8,128)(2,1)S(1)}, u32[]{:S(2)}, u32[]{:S(2)}) collective-permute-start(bf16[528,128]{1,0:T(8,128)(2,1)S(1)} %get-tuple-element.43), channel_id=1, source_target_pairs={{0,1},{1,0},{2,3},{3,2},{4,5},{5,4},{6,7},{7,6},{8,9},{9,8},{10,11... | collective-permute-start | bytes 405512 | tf_op jit(solution)/shard_map/ppermute | solution.py:427
  25.8 7.6 %collective-permute-start.13 = (bf16[528,128]{1,0:T(8,128)(2,1)S(1)}, bf16[528,128]{1,0:T(8,128)(2,1)S(1)}, u32[]{:S(2)}, u32[]{:S(2)}) collective-permute-start(bf16[528,128]{1,0:T(8,128)(2,1)S(1)} %get-tuple-element.46.refs_2_), channel_id=1, source_target_pairs={{0,1},{1,0},{2,3},{3,2},{4,5},{5,4},{6,7},{7,6},{8,9},{9,8},{10,11... | collective-permute-start | bytes 405512 | tf_op jit(solution)/shard_map/ppermute | solution.py:427
  30.9 5.7 %collective-permute-start.11 = (bf16[528,128]{1,0:T(8,128)(2,1)S(1)}, bf16[528,128]{1,0:T(8,128)(2,1)S(1)}, u32[]{:S(2)}, u32[]{:S(2)}) collective-permute-start(bf16[528,128]{1,0:T(8,128)(2,1)S(1)} %get-tuple-element.48), channel_id=1, source_target_pairs={{0,1},{1,0},{2,3},{3,2},{4,5},{5,4},{6,7},{7,6},{8,9},{9,8},{10,11... | collective-permute-start | bytes 405512 | tf_op jit(solution)/shard_map/ppermute | solution.py:427
  32.1 6.0 %collective-permute-start.4 = (bf16[528,128]{1,0:T(8,128)(2,1)S(1)}, bf16[528,128]{1,0:T(8,128)(2,1)S(1)}, u32[]{:S(2)}, u32[]{:S(2)}) collective-permute-start(bf16[528,128]{1,0:T(8,128)(2,1)S(1)} %get-tuple-element.42.refs_4_), channel_id=1, source_target_pairs={{0,1},{1,0},{2,3},{3,2},{4,5},{5,4},{6,7},{7,6},{8,9},{9,8},{10,11... | collective-permute-start | bytes 405512 | tf_op jit(solution)/shard_map/ppermute | solution.py:427
  33.4 13.9 %collective-permute-start.8 = (bf16[528,128]{1,0:T(8,128)(2,1)S(1)}, bf16[528,128]{1,0:T(8,128)(2,1)S(1)}, u32[]{:S(2)}, u32[]{:S(2)}) collective-permute-start(bf16[528,128]{1,0:T(8,128)(2,1)S(1)} %shard_map.95.refs_0_), channel_id=1, source_target_pairs={{0,4},{1,5},{2,6},{3,7},{4,0},{5,1},{6,2},{7,3},{8,12},{9,13},{10,... | collective-permute-start | bytes 405512 | tf_op jit(solution)/shard_map/ppermute | solution.py:427
  36.6 10.7 %collective-permute-start.14 = (bf16[528,128]{1,0:T(8,128)(2,1)S(1)}, bf16[528,128]{1,0:T(8,128)(2,1)S(1)}, u32[]{:S(2)}, u32[]{:S(2)}) collective-permute-start(bf16[528,128]{1,0:T(8,128)(2,1)S(1)} %shard_map.98.refs_2_), channel_id=1, source_target_pairs={{0,2},{1,3},{2,0},{3,1},{4,6},{5,7},{6,4},{7,5},{8,10},{9,11},{10,... | collective-permute-start | bytes 405512 | tf_op jit(solution)/shard_map/ppermute | solution.py:427
  38.1 9.3 %collective-permute-start.12 = (bf16[528,128]{1,0:T(8,128)(2,1)S(1)}, bf16[528,128]{1,0:T(8,128)(2,1)S(1)}, u32[]{:S(2)}, u32[]{:S(2)}) collective-permute-start(bf16[528,128]{1,0:T(8,128)(2,1)S(1)} %shard_map.97.refs_1_), channel_id=1, source_target_pairs={{0,6},{1,7},{2,4},{3,5},{4,2},{5,3},{6,0},{7,1},{8,14},{9,15},{10,... | collective-permute-start | bytes 405512 | tf_op jit(solution)/shard_map/ppermute | solution.py:427
  49.5 17.6 %copy-start.1 = (bf16[8,64,1024]{2,1,0:T(8,128)(2,1)S(1)}, bf16[8,64,1024]{2,1,0:T(8,128)(2,1)}, u32[]{:S(2)}) copy-start(bf16[8,64,1024]{2,1,0:T(8,128)(2,1)} %param.17) | copy-start | bytes 3145732
  49.5 6.6 %collective-permute-start.17 = (bf16[64,1152]{1,0:T(8,128)(2,1)S(1)}, bf16[64,1152]{1,0:T(8,128)(2,1)S(1)}, u32[]{:S(2)}, u32[]{:S(2)}) collective-permute-start(bf16[64,1152]{1,0:T(8,128)(2,1)S(1)} %get-tuple-element.55), channel_id=1, source_target_pairs={{0,1},{1,0},{2,3},{3,2},{4,5},{5,4},{6,7},{7,6},{8,9},{9,8},{10,11... | collective-permute-start | bytes 442376 | tf_op jit(solution)/shard_map/ppermute | solution.py:427
  51.0 6.5 %collective-permute-start.19 = (bf16[64,1024]{1,0:T(8,128)(2,1)S(1)}, bf16[64,1024]{1,0:T(8,128)(2,1)S(1)}, u32[]{:S(2)}, u32[]{:S(2)}) collective-permute-start(bf16[64,1024]{1,0:T(8,128)(2,1)S(1)} %get-tuple-element.57), channel_id=1, source_target_pairs={{0,1},{1,0},{2,3},{3,2},{4,5},{5,4},{6,7},{7,6},{8,9},{9,8},{10,11... | collective-permute-start | bytes 393224 | tf_op jit(solution)/shard_map/ppermute | solution.py:427
  53.9 5.0 %collective-permute-start.16 = (bf16[64,1024]{1,0:T(8,128)(2,1)S(1)}, bf16[64,1024]{1,0:T(8,128)(2,1)S(1)}, u32[]{:S(2)}, u32[]{:S(2)}) collective-permute-start(bf16[64,1024]{1,0:T(8,128)(2,1)S(1)} %get-tuple-element.53), channel_id=1, source_target_pairs={{0,1},{1,0},{2,3},{3,2},{4,5},{5,4},{6,7},{7,6},{8,9},{9,8},{10,11... | collective-permute-start | bytes 393224 | tf_op jit(solution)/shard_map/ppermute | solution.py:427
  56.2 10.4 %collective-permute-start.21 = (bf16[64,1152]{1,0:T(8,128)(2,1)S(1)}, bf16[64,1152]{1,0:T(8,128)(2,1)S(1)}, u32[]{:S(2)}, u32[]{:S(2)}) collective-permute-start(bf16[64,1152]{1,0:T(8,128)(2,1)S(1)} %shard_map.104), channel_id=1, source_target_pairs={{0,4},{1,5},{2,6},{3,7},{4,0},{5,1},{6,2},{7,3},{8,12},{9,13},{10,... | collective-permute-start | bytes 442376 | tf_op jit(solution)/shard_map/ppermute | solution.py:427
  57.6 9.0 %collective-permute-start.20 = (bf16[64,1152]{1,0:T(8,128)(2,1)S(1)}, bf16[64,1152]{1,0:T(8,128)(2,1)S(1)}, u32[]{:S(2)}, u32[]{:S(2)}) collective-permute-start(bf16[64,1152]{1,0:T(8,128)(2,1)S(1)} %shard_map.103), channel_id=1, source_target_pairs={{0,6},{1,7},{2,4},{3,5},{4,2},{5,3},{6,0},{7,1},{8,14},{9,15},{10,... | collective-permute-start | bytes 442376 | tf_op jit(solution)/shard_map/ppermute | solution.py:427
  59.0 8.1 %collective-permute-start.18 = (bf16[64,1152]{1,0:T(8,128)(2,1)S(1)}, bf16[64,1152]{1,0:T(8,128)(2,1)S(1)}, u32[]{:S(2)}, u32[]{:S(2)}) collective-permute-start(bf16[64,1152]{1,0:T(8,128)(2,1)S(1)} %shard_map.102), channel_id=1, source_target_pairs={{0,2},{1,3},{2,0},{3,1},{4,6},{5,7},{6,4},{7,5},{8,10},{9,11},{10,... | collective-permute-start | bytes 442376 | tf_op jit(solution)/shard_map/ppermute | solution.py:427
  60.0 5.0 %collective-permute-start.22 = (bf16[64,1024]{1,0:T(8,128)(2,1)S(1)}, bf16[64,1024]{1,0:T(8,128)(2,1)S(1)}, u32[]{:S(2)}, u32[]{:S(2)}) collective-permute-start(bf16[64,1024]{1,0:T(8,128)(2,1)S(1)} %get-tuple-element.60), channel_id=1, source_target_pairs={{0,1},{1,0},{2,3},{3,2},{4,5},{5,4},{6,7},{7,6},{8,9},{9,8},{10,11... | collective-permute-start | bytes 393224 | tf_op jit(solution)/shard_map/ppermute | solution.py:427
  (5 other events, 37.9 us)

commit v8 on v7

--- a/solution.py
+++ b/solution.py
@@ -463,9 +463,9 @@
             held[k] = hop(source, bit)
     sent = {k: hop(partial[k ^ 1], 1) for k in [0, *far[1:], far[0]]}
     merged = {}
-    for k in far + [0]:
+    for k in far:
         merged[k] = pair(partial[k], sent[k], *([merged[far[0]]] if k == 2 and k != far[0] else []))
-    parts = [merged[0]] + [hop(merged[k], k) for k in far]
+    parts = [partial[0], sent[0]] + [hop(merged[k], k) for k in far]
 
     total_slots = adapter_slot_index.shape[0]
     match = adapter_index[:, None] == jnp.arange(total_slots, dtype=jnp.int32)[None, :]

time: 68.4 us -> 68.3 us (level)
  transfers between devices with their start and end apart: 23 -> 23, of which waited for: 8 -> 7; matrix products, arithmetic and copies ran while one was open for 0% -> 0% of each run, Pallas kernels for 41% -> 41%
where the time goes in v8:
time: 68.3 us; the launch traced here: 68.1 us
  starting transfers between devices  29.8 us (44%)
  Pallas kernels  28.8 us (42%)
  waiting for transfers between devices  7.67 us (11%)
  local copies, waits for them, and re-layouts  1.68 us (2%)
    ppermute x21, starting transfers between devices, hop(): return lax.ppermute(x, 'tensor', [(i, i ^ k) for i in range(tensor)])  29.3 us
    pallas_call x4, Pallas kernels, attend(): pl.pallas_call(functools.partial(attend_body, which, following, bool(give...  15.9 us
    ppermute x21, waiting for transfers between devices, hop(): return lax.ppermute(x, 'tensor', [(i, i ^ k) for i in range(tensor)])  7.67 us
    pallas_call x1, Pallas kernels, load(): pl.pallas_call(functools.partial(load_body, blocks), in_specs=[pl.BlockSp...  5.96 us
    pallas_call x1, Pallas kernels, project_more(): pl.pallas_call(functools.partial(project_more_body, blocks, kinds), in_sp...  2.29 us
    pallas_call x1, Pallas kernels, project(): pl.pallas_call(functools.partial(project_body, len(parts), blocks, heads,...  2.12 us
    unnamed x12, local copies, waits for them, and re-layouts  1.61 us
  transfers between devices with their start and end apart: 23, of which 7 were waited for; matrix products, arithmetic and copies ran while one was open for 0% of the time, Pallas kernels for 41%

profile of v8, /device:TPU:0, one launch (start us, length us, event | category | flops | bytes accessed | tf_op | source)
XLA Modules:
  0.0 68.1 jit_solution(1519019070401308918)
XLA Ops:
  0.5 3.6 %collective-permute-start.3 = (bf16[512,128]{1,0:T(8,128)(2,1)}, bf16[512,128]{1,0:T(8,128)(2,1)S(1)}, u32[]{:S(2)}, u32[]{:S(2)}) collective-permute-start(bf16[512,128]{1,0:T(8,128)(2,1)} %bitcast.9), channel_id=1, source_target_pairs={{0,4},{1,5},{2,6},{3,7},{4,0},{5,1},{6,2},{7,3},{8,12},{9,13},{10,... | collective-permute-start | bytes 393224 | tf_op jit(solution)/shard_map/ppermute | solution.py:427
  4.0 1.6 %collective-permute-start.2 = (bf16[512,128]{1,0:T(8,128)(2,1)}, bf16[512,128]{1,0:T(8,128)(2,1)S(1)}, u32[]{:S(2)}, u32[]{:S(2)}) collective-permute-start(bf16[512,128]{1,0:T(8,128)(2,1)} %bitcast.10), channel_id=1, source_target_pairs={{0,2},{1,3},{2,0},{3,1},{4,6},{5,7},{6,4},{7,5},{8,10},{9,11},{10,... | collective-permute-start | bytes 393224 | tf_op jit(solution)/shard_map/ppermute | solution.py:427
  5.6 1.5 %collective-permute-start.1 = (bf16[512,128]{1,0:T(8,128)(2,1)}, bf16[512,128]{1,0:T(8,128)(2,1)S(1)}, u32[]{:S(2)}, u32[]{:S(2)}) collective-permute-start(bf16[512,128]{1,0:T(8,128)(2,1)} %bitcast.11), channel_id=1, source_target_pairs={{0,1},{1,0},{2,3},{3,2},{4,5},{5,4},{6,7},{7,6},{8,9},{9,8},{10,11... | collective-permute-start | bytes 393224 | tf_op jit(solution)/shard_map/ppermute | solution.py:427
  8.7 3.0 %shard_map.91.refs_3_.refs_0_ = bf16[528,128]{1,0:T(8,128)(2,1)S(1)} custom-call(s32[64]{0:T(128)S(1)} %copy-done.3, bf16[64,8,96,128]{3,2,1,0:T(8,128)(2,1)} %k_hbm.7, bf16[64,8,96,128]{3,2,1,0:T(8,128)(2,1)} %v_hbm.7, bf16[512,128]{1,0:T(8,128)(2,1)S(1)} %bitcast.12), custom_call_target="tpu_custom_call" | custom-call | flops 201326592 | bytes 3145728 | tf_op jit(solution)/shard_map/pallas_call | solution.py:157
  11.8 1.1 %collective-permute-start.6 = (bf16[512,128]{1,0:T(8,128)(2,1)S(1)}, bf16[512,128]{1,0:T(8,128)(2,1)S(1)}, u32[]{:S(2)}, u32[]{:S(2)}) collective-permute-start(bf16[512,128]{1,0:T(8,128)(2,1)S(1)} %collective-permute-done.3.refs_2_), channel_id=1, source_target_pairs={{0,1},{1,0},{2,3},{3,2},{4,5},{5,4},{6,7},{7,6},{8,9},{9,8},{10,11... | collective-permute-start | bytes 393224 | tf_op jit(solution)/shard_map/ppermute | solution.py:427
  12.9 1.0 %collective-permute-start.5 = (bf16[512,128]{1,0:T(8,128)(2,1)S(1)}, bf16[512,128]{1,0:T(8,128)(2,1)S(1)}, u32[]{:S(2)}, u32[]{:S(2)}) collective-permute-start(bf16[512,128]{1,0:T(8,128)(2,1)S(1)} %collective-permute-done.2.refs_1_), channel_id=1, source_target_pairs={{0,1},{1,0},{2,3},{3,2},{4,5},{5,4},{6,7},{7,6},{8,9},{9,8},{10,11... | collective-permute-start | bytes 393224 | tf_op jit(solution)/shard_map/ppermute | solution.py:427
  14.5 6.3 %shard_map.92 = (bf16[528,128]{1,0:T(8,128)(2,1)S(1)}, bf16[528,128]{1,0:T(8,128)(2,1)S(1)}, bf16[528,128]{1,0:T(8,128)(2,1)S(1)}, bf16[4,32,96,128]{3,2,1,0:T(8,128)(2,1)S(1)}, bf16[4,32,96,128]{3,2,1,0:T(8,128)(2,1)S(1)}) custom-call(s32[64]{0:T(128)S(1)} %copy-done.3, bf16[64,8,96,128]{3,2,1,0:T(8,128)(2,1)} %k_hbm.7, bf16[64,8,96,128]{3,2,1,0:T(8,128)(2,1)} %v_hbm.7, ...), custom_call_target="tpu_custom_call" | custom-call | flops 603979776 | bytes 9437184 | tf_op jit(solution)/shard_map/pallas_call | solution.py:157
  20.9 1.4 %collective-permute-start.9 = (bf16[512,128]{1,0:T(8,128)(2,1)S(1)}, bf16[512,128]{1,0:T(8,128)(2,1)S(1)}, u32[]{:S(2)}, u32[]{:S(2)}) collective-permute-start(bf16[512,128]{1,0:T(8,128)(2,1)S(1)} %collective-permute-done.6.refs_1_), channel_id=1, source_target_pairs={{0,2},{1,3},{2,0},{3,1},{4,6},{5,7},{6,4},{7,5},{8,10},{9,11},{10,... | collective-permute-start | bytes 393224 | tf_op jit(solution)/shard_map/ppermute | solution.py:427
  22.3 2.4 %shard_map.93 = (bf16[528,128]{1,0:T(8,128)(2,1)S(1)}, bf16[528,128]{1,0:T(8,128)(2,1)S(1)}) custom-call(s32[64]{0:T(128)S(1)} %copy-done.3, bf16[64,8,96,128]{3,2,1,0:T(8,128)(2,1)} %k_hbm.7, bf16[64,8,96,128]{3,2,1,0:T(8,128)(2,1)} %v_hbm.7, bf16[512,128]{1,0:T(8,128)(2,1)S(1)} %collective-permute-done.5.refs_0_, ...), custom_call_target="tpu_custom_call" | custom-call | flops 402653184 | bytes 6291456 | tf_op jit(solution)/shard_map/pallas_call | solution.py:157
  24.7 1.1 %collective-permute-start.7 = (bf16[528,128]{1,0:T(8,128)(2,1)S(1)}, bf16[528,128]{1,0:T(8,128)(2,1)S(1)}, u32[]{:S(2)}, u32[]{:S(2)}) collective-permute-start(bf16[528,128]{1,0:T(8,128)(2,1)S(1)} %get-tuple-element.43), channel_id=1, source_target_pairs={{0,1},{1,0},{2,3},{3,2},{4,5},{5,4},{6,7},{7,6},{8,9},{9,8},{10,11... | collective-permute-start | bytes 405512 | tf_op jit(solution)/shard_map/ppermute | solution.py:427
  26.8 4.1 %shard_map.95 = (bf16[528,128]{1,0:T(8,128)(2,1)S(1)}, bf16[528,128]{1,0:T(8,128)(2,1)S(1)}) custom-call(s32[64]{0:T(128)S(1)} %copy-done.3, bf16[64,8,96,128]{3,2,1,0:T(8,128)(2,1)} %k_hbm.7, bf16[64,8,96,128]{3,2,1,0:T(8,128)(2,1)} %v_hbm.7, bf16[512,128]{1,0:T(8,128)(2,1)S(1)} %collective-permute-done.9.refs_0_, ...), custom_call_target="tpu_custom_call" | custom-call | flops 402653184 | bytes 6291456 | tf_op jit(solution)/shard_map/pallas_call | solution.py:157
  30.9 1.1 %collective-permute-start.11 = (bf16[528,128]{1,0:T(8,128)(2,1)S(1)}, bf16[528,128]{1,0:T(8,128)(2,1)S(1)}, u32[]{:S(2)}, u32[]{:S(2)}) collective-permute-start(bf16[528,128]{1,0:T(8,128)(2,1)S(1)} %get-tuple-element.48), channel_id=1, source_target_pairs={{0,1},{1,0},{2,3},{3,2},{4,5},{5,4},{6,7},{7,6},{8,9},{9,8},{10,11... | collective-permute-start | bytes 405512 | tf_op jit(solution)/shard_map/ppermute | solution.py:427
  33.4 2.1 %collective-permute-start.8 = (bf16[528,128]{1,0:T(8,128)(2,1)S(1)}, bf16[528,128]{1,0:T(8,128)(2,1)S(1)}, u32[]{:S(2)}, u32[]{:S(2)}) collective-permute-start(bf16[528,128]{1,0:T(8,128)(2,1)S(1)} %shard_map.94.refs_0_), channel_id=1, source_target_pairs={{0,4},{1,5},{2,6},{3,7},{4,0},{5,1},{6,2},{7,3},{8,12},{9,13},{10,... | collective-permute-start | bytes 405512 | tf_op jit(solution)/shard_map/ppermute | solution.py:427
  38.1 2.9 %collective-permute-start.12 = (bf16[528,128]{1,0:T(8,128)(2,1)S(1)}, bf16[528,128]{1,0:T(8,128)(2,1)S(1)}, u32[]{:S(2)}, u32[]{:S(2)}) collective-permute-start(bf16[528,128]{1,0:T(8,128)(2,1)S(1)} %shard_map.96.refs_1_), channel_id=1, source_target_pairs={{0,6},{1,7},{2,4},{3,5},{4,2},{5,3},{6,0},{7,1},{8,14},{9,15},{10,... | collective-permute-start | bytes 405512 | tf_op jit(solution)/shard_map/ppermute | solution.py:427
  41.0 6.0 %shard_map.98.refs_5_ = bf16[1024,8192]{1,0:T(8,128)(2,1)S(1)} custom-call(bf16[1024,8192]{1,0:T(8,128)(2,1)} %source.1, bf16[528,128]{1,0:T(8,128)(2,1)S(1)} %shard_map.94.refs_0_, bf16[528,128]{1,0:T(8,128)(2,1)S(1)} %shard_map.96.refs_1_, bf16[528,128]{1,0:T(8,128)(2,1)S(1)} %shard_map.97.refs_2_), custom_call_target="tpu_custom_call" | custom-call | bytes 16777216 | tf_op jit(solution)/shard_map/pallas_call | solution.py:188
  47.1 2.1 %shard_map.99 = (bf16[64,1152]{1,0:T(8,128)(2,1)S(1)}, bf16[64,1024]{1,0:T(8,128)(2,1)S(1)}, bf16[64,1024]{1,0:T(8,128)(2,1)S(1)}, bf16[64,128]{1,0:T(8,128)(2,1)S(1)}, bf16[1024,8192]{1,0:T(8,128)(2,1)S(1)}) custom-call(bf16[528,128]{1,0:T(8,128)(2,1)S(1)} %shard_map.91.refs_3_.refs_0_, ...), custom_call_target="tpu_custom_call", output_to_operand_aliasing={{4}: (5, {})} | custom-call | flops 268435456 | bytes 4194304 | tf_op jit(solution)/shard_map/pallas_call | solution.py:298
  49.2 1.5 %collective-permute-start.17 = (bf16[64,1152]{1,0:T(8,128)(2,1)S(1)}, bf16[64,1152]{1,0:T(8,128)(2,1)S(1)}, u32[]{:S(2)}, u32[]{:S(2)}) collective-permute-start(bf16[64,1152]{1,0:T(8,128)(2,1)S(1)} %get-tuple-element.55), channel_id=1, source_target_pairs={{0,1},{1,0},{2,3},{3,2},{4,5},{5,4},{6,7},{7,6},{8,9},{9,8},{10,11... | collective-permute-start | bytes 442376 | tf_op jit(solution)/shard_map/ppermute | solution.py:427
  51.3 2.3 %shard_map.100 = (bf16[64,1024]{1,0:T(8,128)(2,1)S(1)}, bf16[64,1024]{1,0:T(8,128)(2,1)S(1)}, f32[64,1024]{1,0:T(8,128)S(1)}, f32[64,1024]{1,0:T(8,128)S(1)}, f3...) custom-call(bf16[1024,8192]{1,0:T(8,128)(2,1)S(1)} %get-tuple-element.50.w_ref, bf16[64,1024]{1,0:T(8,128)(2,1)S(1)} %get-tuple-element.51.att_ref), custom_call_target="tpu_custom_call" | custom-call | flops 805306368 | bytes 12582912 | tf_op jit(solution)/shard_map/pallas_call | solution.py:333
  53.6 1.5 %collective-permute-start.16 = (bf16[64,1024]{1,0:T(8,128)(2,1)S(1)}, bf16[64,1024]{1,0:T(8,128)(2,1)S(1)}, u32[]{:S(2)}, u32[]{:S(2)}) collective-permute-start(bf16[64,1024]{1,0:T(8,128)(2,1)S(1)} %get-tuple-element.53), channel_id=1, source_target_pairs={{0,1},{1,0},{2,3},{3,2},{4,5},{5,4},{6,7},{7,6},{8,9},{9,8},{10,11... | collective-permute-start | bytes 393224 | tf_op jit(solution)/shard_map/ppermute | solution.py:427
  57.3 1.5 %collective-permute-start.20 = (bf16[64,1152]{1,0:T(8,128)(2,1)S(1)}, bf16[64,1152]{1,0:T(8,128)(2,1)S(1)}, u32[]{:S(2)}, u32[]{:S(2)}) collective-permute-start(bf16[64,1152]{1,0:T(8,128)(2,1)S(1)} %shard_map.102), channel_id=1, source_target_pairs={{0,6},{1,7},{2,4},{3,5},{4,2},{5,3},{6,0},{7,1},{8,14},{9,15},{10,... | collective-permute-start | bytes 442376 | tf_op jit(solution)/shard_map/ppermute | solution.py:427
  59.8 1.4 %collective-permute-start.22 = (bf16[64,1024]{1,0:T(8,128)(2,1)S(1)}, bf16[64,1024]{1,0:T(8,128)(2,1)S(1)}, u32[]{:S(2)}, u32[]{:S(2)}) collective-permute-start(bf16[64,1024]{1,0:T(8,128)(2,1)S(1)} %get-tuple-element.60), channel_id=1, source_target_pairs={{0,1},{1,0},{2,3},{3,2},{4,5},{5,4},{6,7},{7,6},{8,9},{9,8},{10,11... | collective-permute-start | bytes 393224 | tf_op jit(solution)/shard_map/ppermute | solution.py:427
  61.2 3.6 %collective-permute-done.22.b_ref = bf16[64,1024]{1,0:T(8,128)(2,1)S(1)} collective-permute-done((bf16[64,1024]{1,0:T(8,128)(2,1)S(1)}, bf16[64,1024]{1,0:T(8,128)(2,1)S(1)}, u32[]{:S(2)}, u32[]{:S(2)}) %collective-permute-start.22) | collective-permute-done | bytes 131104 | tf_op jit(solution)/shard_map/ppermute | solution.py:427
  64.9 1.5 %collective-permute-done.21.refs_2_ = bf16[64,1152]{1,0:T(8,128)(2,1)S(1)} collective-permute-done((bf16[64,1152]{1,0:T(8,128)(2,1)S(1)}, bf16[64,1152]{1,0:T(8,128)(2,1)S(1)}, u32[]{:S(2)}, u32[]{:S(2)}) %collective-permute-start.21) | collective-permute-done | bytes 147488 | tf_op jit(solution)/shard_map/ppermute | solution.py:427
  67.0 1.2 %shard_map.105 = bf16[64,1024]{1,0:T(8,128)(2,1)} custom-call(s32[64,128]{1,0:T(8,128)S(1)} %broadcast_in_dim.23.refs_6_.slot_ref, bf16[512,1024]{1,0:T(8,128)(2,1)S(1)} %bitcast.8, bf16[512,1024]{1,0:T(8,128)(2,1)S(1)} %collective-permute-done.up_b, bf16[64,1152]{1,0:T(8,128)(2,1)S(1)} %collective-permute-done.18.refs_0_, ...), custom_call_target="tpu_custom_call" | custom-call | flops 2097152 | bytes 2097152 | tf_op jit(solution)/shard_map/pallas_call | solution.py:399
  (51 shorter events, 12.2 us)
Async XLA Ops:
  0.0 47.0 %collective-permute-start.15 = (bf16[512,1024]{1,0:T(8,128)(2,1)}, bf16[512,1024]{1,0:T(8,128)(2,1)S(1)}, u32[]{:S(2)}, u32[]{:S(2)}) collective-permute-start(bf16[512,1024]{1,0:T(8,128)(2,1)} %bitcast.5), channel_id=1, source_target_pairs={{0,8},{8,0},{1,9},{9,1},{2,10},{10,2},{3,11},{11,3},{4,12},{12,4},... | collective-permute-start | bytes 3145736 | tf_op jit(solution)/shard_map/ppermute | solution.py:430
  0.5 11.3 %collective-permute-start.3 = (bf16[512,128]{1,0:T(8,128)(2,1)}, bf16[512,128]{1,0:T(8,128)(2,1)S(1)}, u32[]{:S(2)}, u32[]{:S(2)}) collective-permute-start(bf16[512,128]{1,0:T(8,128)(2,1)} %bitcast.9), channel_id=1, source_target_pairs={{0,4},{1,5},{2,6},{3,7},{4,0},{5,1},{6,2},{7,3},{8,12},{9,13},{10,... | collective-permute-start | bytes 393224 | tf_op jit(solution)/shard_map/ppermute | solution.py:427
  4.0 8.9 %collective-permute-start.2 = (bf16[512,128]{1,0:T(8,128)(2,1)}, bf16[512,128]{1,0:T(8,128)(2,1)S(1)}, u32[]{:S(2)}, u32[]{:S(2)}) collective-permute-start(bf16[512,128]{1,0:T(8,128)(2,1)} %bitcast.10), channel_id=1, source_target_pairs={{0,2},{1,3},{2,0},{3,1},{4,6},{5,7},{6,4},{7,5},{8,10},{9,11},{10,... | collective-permute-start | bytes 393224 | tf_op jit(solution)/shard_map/ppermute | solution.py:427
  5.6 59.3 %collective-permute-start = (bf16[512,1024]{1,0:T(8,128)(2,1)}, bf16[512,1024]{1,0:T(8,128)(2,1)S(1)}, u32[]{:S(2)}, u32[]{:S(2)}) collective-permute-start(bf16[512,1024]{1,0:T(8,128)(2,1)} %bitcast.7), channel_id=1, source_target_pairs={{0,8},{8,0},{1,9},{9,1},{2,10},{10,2},{3,11},{11,3},{4,12},{12,4},... | collective-permute-start | bytes 3145736 | tf_op jit(solution)/shard_map/ppermute | solution.py:430
  5.6 8.3 %collective-permute-start.1 = (bf16[512,128]{1,0:T(8,128)(2,1)}, bf16[512,128]{1,0:T(8,128)(2,1)S(1)}, u32[]{:S(2)}, u32[]{:S(2)}) collective-permute-start(bf16[512,128]{1,0:T(8,128)(2,1)} %bitcast.11), channel_id=1, source_target_pairs={{0,1},{1,0},{2,3},{3,2},{4,5},{5,4},{6,7},{7,6},{8,9},{9,8},{10,11... | collective-permute-start | bytes 393224 | tf_op jit(solution)/shard_map/ppermute | solution.py:427
  11.8 9.1 %collective-permute-start.6 = (bf16[512,128]{1,0:T(8,128)(2,1)S(1)}, bf16[512,128]{1,0:T(8,128)(2,1)S(1)}, u32[]{:S(2)}, u32[]{:S(2)}) collective-permute-start(bf16[512,128]{1,0:T(8,128)(2,1)S(1)} %collective-permute-done.3.refs_2_), channel_id=1, source_target_pairs={{0,1},{1,0},{2,3},{3,2},{4,5},{5,4},{6,7},{7,6},{8,9},{9,8},{10,11... | collective-permute-start | bytes 393224 | tf_op jit(solution)/shard_map/ppermute | solution.py:427
  12.9 9.4 %collective-permute-start.5 = (bf16[512,128]{1,0:T(8,128)(2,1)S(1)}, bf16[512,128]{1,0:T(8,128)(2,1)S(1)}, u32[]{:S(2)}, u32[]{:S(2)}) collective-permute-start(bf16[512,128]{1,0:T(8,128)(2,1)S(1)} %collective-permute-done.2.refs_1_), channel_id=1, source_target_pairs={{0,1},{1,0},{2,3},{3,2},{4,5},{5,4},{6,7},{7,6},{8,9},{9,8},{10,11... | collective-permute-start | bytes 393224 | tf_op jit(solution)/shard_map/ppermute | solution.py:427
  13.9 11.9 %collective-permute-start.10 = (bf16[512,128]{1,0:T(8,128)(2,1)S(1)}, bf16[512,128]{1,0:T(8,128)(2,1)S(1)}, u32[]{:S(2)}, u32[]{:S(2)}) collective-permute-start(bf16[512,128]{1,0:T(8,128)(2,1)S(1)} %collective-permute-done.3.refs_2_), channel_id=1, source_target_pairs={{0,2},{1,3},{2,0},{3,1},{4,6},{5,7},{6,4},{7,5},{8,10},{9,11},{10,... | collective-permute-start | bytes 393224 | tf_op jit(solution)/shard_map/ppermute | solution.py:427
  20.9 5.9 %collective-permute-start.9 = (bf16[512,128]{1,0:T(8,128)(2,1)S(1)}, bf16[512,128]{1,0:T(8,128)(2,1)S(1)}, u32[]{:S(2)}, u32[]{:S(2)}) collective-permute-start(bf16[512,128]{1,0:T(8,128)(2,1)S(1)} %collective-permute-done.6.refs_1_), channel_id=1, source_target_pairs={{0,2},{1,3},{2,0},{3,1},{4,6},{5,7},{6,4},{7,5},{8,10},{9,11},{10,... | collective-permute-start | bytes 393224 | tf_op jit(solution)/shard_map/ppermute | solution.py:427
  24.7 7.4 %collective-permute-start.7 = (bf16[528,128]{1,0:T(8,128)(2,1)S(1)}, bf16[528,128]{1,0:T(8,128)(2,1)S(1)}, u32[]{:S(2)}, u32[]{:S(2)}) collective-permute-start(bf16[528,128]{1,0:T(8,128)(2,1)S(1)} %get-tuple-element.43), channel_id=1, source_target_pairs={{0,1},{1,0},{2,3},{3,2},{4,5},{5,4},{6,7},{7,6},{8,9},{9,8},{10,11... | collective-permute-start | bytes 405512 | tf_op jit(solution)/shard_map/ppermute | solution.py:427
  25.8 7.6 %collective-permute-start.13 = (bf16[528,128]{1,0:T(8,128)(2,1)S(1)}, bf16[528,128]{1,0:T(8,128)(2,1)S(1)}, u32[]{:S(2)}, u32[]{:S(2)}) collective-permute-start(bf16[528,128]{1,0:T(8,128)(2,1)S(1)} %get-tuple-element.46.refs_2_), channel_id=1, source_target_pairs={{0,1},{1,0},{2,3},{3,2},{4,5},{5,4},{6,7},{7,6},{8,9},{9,8},{10,11... | collective-permute-start | bytes 405512 | tf_op jit(solution)/shard_map/ppermute | solution.py:427
  30.9 5.7 %collective-permute-start.11 = (bf16[528,128]{1,0:T(8,128)(2,1)S(1)}, bf16[528,128]{1,0:T(8,128)(2,1)S(1)}, u32[]{:S(2)}, u32[]{:S(2)}) collective-permute-start(bf16[528,128]{1,0:T(8,128)(2,1)S(1)} %get-tuple-element.48), channel_id=1, source_target_pairs={{0,1},{1,0},{2,3},{3,2},{4,5},{5,4},{6,7},{7,6},{8,9},{9,8},{10,11... | collective-permute-start | bytes 405512 | tf_op jit(solution)/shard_map/ppermute | solution.py:427
  32.1 6.0 %collective-permute-start.4 = (bf16[528,128]{1,0:T(8,128)(2,1)S(1)}, bf16[528,128]{1,0:T(8,128)(2,1)S(1)}, u32[]{:S(2)}, u32[]{:S(2)}) collective-permute-start(bf16[528,128]{1,0:T(8,128)(2,1)S(1)} %get-tuple-element.42.refs_4_), channel_id=1, source_target_pairs={{0,1},{1,0},{2,3},{3,2},{4,5},{5,4},{6,7},{7,6},{8,9},{9,8},{10,11... | collective-permute-start | bytes 405512 | tf_op jit(solution)/shard_map/ppermute | solution.py:427
  33.4 13.6 %collective-permute-start.8 = (bf16[528,128]{1,0:T(8,128)(2,1)S(1)}, bf16[528,128]{1,0:T(8,128)(2,1)S(1)}, u32[]{:S(2)}, u32[]{:S(2)}) collective-permute-start(bf16[528,128]{1,0:T(8,128)(2,1)S(1)} %shard_map.94.refs_0_), channel_id=1, source_target_pairs={{0,4},{1,5},{2,6},{3,7},{4,0},{5,1},{6,2},{7,3},{8,12},{9,13},{10,... | collective-permute-start | bytes 405512 | tf_op jit(solution)/shard_map/ppermute | solution.py:427
  36.6 10.4 %collective-permute-start.14 = (bf16[528,128]{1,0:T(8,128)(2,1)S(1)}, bf16[528,128]{1,0:T(8,128)(2,1)S(1)}, u32[]{:S(2)}, u32[]{:S(2)}) collective-permute-start(bf16[528,128]{1,0:T(8,128)(2,1)S(1)} %shard_map.97.refs_2_), channel_id=1, source_target_pairs={{0,2},{1,3},{2,0},{3,1},{4,6},{5,7},{6,4},{7,5},{8,10},{9,11},{10,... | collective-permute-start | bytes 405512 | tf_op jit(solution)/shard_map/ppermute | solution.py:427
  38.1 8.9 %collective-permute-start.12 = (bf16[528,128]{1,0:T(8,128)(2,1)S(1)}, bf16[528,128]{1,0:T(8,128)(2,1)S(1)}, u32[]{:S(2)}, u32[]{:S(2)}) collective-permute-start(bf16[528,128]{1,0:T(8,128)(2,1)S(1)} %shard_map.96.refs_1_), channel_id=1, source_target_pairs={{0,6},{1,7},{2,4},{3,5},{4,2},{5,3},{6,0},{7,1},{8,14},{9,15},{10,... | collective-permute-start | bytes 405512 | tf_op jit(solution)/shard_map/ppermute | solution.py:427
  49.2 17.7 %copy-start.1 = (bf16[8,64,1024]{2,1,0:T(8,128)(2,1)S(1)}, bf16[8,64,1024]{2,1,0:T(8,128)(2,1)}, u32[]{:S(2)}) copy-start(bf16[8,64,1024]{2,1,0:T(8,128)(2,1)} %param.17) | copy-start | bytes 3145732
  49.2 6.6 %collective-permute-start.17 = (bf16[64,1152]{1,0:T(8,128)(2,1)S(1)}, bf16[64,1152]{1,0:T(8,128)(2,1)S(1)}, u32[]{:S(2)}, u32[]{:S(2)}) collective-permute-start(bf16[64,1152]{1,0:T(8,128)(2,1)S(1)} %get-tuple-element.55), channel_id=1, source_target_pairs={{0,1},{1,0},{2,3},{3,2},{4,5},{5,4},{6,7},{7,6},{8,9},{9,8},{10,11... | collective-permute-start | bytes 442376 | tf_op jit(solution)/shard_map/ppermute | solution.py:427
  50.7 6.5 %collective-permute-start.19 = (bf16[64,1024]{1,0:T(8,128)(2,1)S(1)}, bf16[64,1024]{1,0:T(8,128)(2,1)S(1)}, u32[]{:S(2)}, u32[]{:S(2)}) collective-permute-start(bf16[64,1024]{1,0:T(8,128)(2,1)S(1)} %get-tuple-element.57), channel_id=1, source_target_pairs={{0,1},{1,0},{2,3},{3,2},{4,5},{5,4},{6,7},{7,6},{8,9},{9,8},{10,11... | collective-permute-start | bytes 393224 | tf_op jit(solution)/shard_map/ppermute | solution.py:427
  53.6 5.2 %collective-permute-start.16 = (bf16[64,1024]{1,0:T(8,128)(2,1)S(1)}, bf16[64,1024]{1,0:T(8,128)(2,1)S(1)}, u32[]{:S(2)}, u32[]{:S(2)}) collective-permute-start(bf16[64,1024]{1,0:T(8,128)(2,1)S(1)} %get-tuple-element.53), channel_id=1, source_target_pairs={{0,1},{1,0},{2,3},{3,2},{4,5},{5,4},{6,7},{7,6},{8,9},{9,8},{10,11... | collective-permute-start | bytes 393224 | tf_op jit(solution)/shard_map/ppermute | solution.py:427
  55.9 10.5 %collective-permute-start.21 = (bf16[64,1152]{1,0:T(8,128)(2,1)S(1)}, bf16[64,1152]{1,0:T(8,128)(2,1)S(1)}, u32[]{:S(2)}, u32[]{:S(2)}) collective-permute-start(bf16[64,1152]{1,0:T(8,128)(2,1)S(1)} %shard_map.103), channel_id=1, source_target_pairs={{0,4},{1,5},{2,6},{3,7},{4,0},{5,1},{6,2},{7,3},{8,12},{9,13},{10,... | collective-permute-start | bytes 442376 | tf_op jit(solution)/shard_map/ppermute | solution.py:427
  57.3 9.1 %collective-permute-start.20 = (bf16[64,1152]{1,0:T(8,128)(2,1)S(1)}, bf16[64,1152]{1,0:T(8,128)(2,1)S(1)}, u32[]{:S(2)}, u32[]{:S(2)}) collective-permute-start(bf16[64,1152]{1,0:T(8,128)(2,1)S(1)} %shard_map.102), channel_id=1, source_target_pairs={{0,6},{1,7},{2,4},{3,5},{4,2},{5,3},{6,0},{7,1},{8,14},{9,15},{10,... | collective-permute-start | bytes 442376 | tf_op jit(solution)/shard_map/ppermute | solution.py:427
  58.9 8.1 %collective-permute-start.18 = (bf16[64,1152]{1,0:T(8,128)(2,1)S(1)}, bf16[64,1152]{1,0:T(8,128)(2,1)S(1)}, u32[]{:S(2)}, u32[]{:S(2)}) collective-permute-start(bf16[64,1152]{1,0:T(8,128)(2,1)S(1)} %shard_map.101), channel_id=1, source_target_pairs={{0,2},{1,3},{2,0},{3,1},{4,6},{5,7},{6,4},{7,5},{8,10},{9,11},{10,... | collective-permute-start | bytes 442376 | tf_op jit(solution)/shard_map/ppermute | solution.py:427
  59.8 5.0 %collective-permute-start.22 = (bf16[64,1024]{1,0:T(8,128)(2,1)S(1)}, bf16[64,1024]{1,0:T(8,128)(2,1)S(1)}, u32[]{:S(2)}, u32[]{:S(2)}) collective-permute-start(bf16[64,1024]{1,0:T(8,128)(2,1)S(1)} %get-tuple-element.60), channel_id=1, source_target_pairs={{0,1},{1,0},{2,3},{3,2},{4,5},{5,4},{6,7},{7,6},{8,9},{9,8},{10,11... | collective-permute-start | bytes 393224 | tf_op jit(solution)/shard_map/ppermute | solution.py:427
  (5 other events, 37.8 us)
